TPU v7x, 128 devices: a whole 4x4x4 slice. The times are simulated.
128 devices in a mesh: row: 4 (over x_hi, core), col: 32 (over x_lo, z, y).
Axes of the slice: x: 4 (x_hi: 2, x_lo: 2; x = x_hi * 2 + x_lo), y: 4, z: 4, core: 2. Of those that a mesh axis runs over, the one named last changes fastest.
Arguments:
- current: bfloat16 [128, 1024, 256], P('row', 'col'), may hold values from -6 to 6
- history: bfloat16 [4, 128, 1024, 256], P(None, 'row', 'col'), may hold values from -6 to 6
- validity: int32 [4, 128, 1024], P(None, 'row', 'col'), may hold values 0 or 1
- offsets: int32 [4, 2], replicated, may hold values from 2 to 30, as said below
- merge_weight: bfloat16 [3, 3, 1280, 256], replicated, may hold values from -0.0546875 to 0.0546875
- out_weight: bfloat16 [3, 3, 256, 256], replicated, may hold values from -0.125 to 0.125
- cotangent: bfloat16 [128, 1024, 256], P('row', 'col'), may hold values from -0.016479492 to 0.016479492
Outputs:
- merged: bfloat16 [128, 1024, 256], P('row', 'col')
- merge_grad: float32 [3, 3, 1280, 256], replicated
- out_grad: float32 [3, 3, 256, 256], replicated
Inputs may be any that keep to these rules, and one draw needn't show every extreme that they name: offsets[k, 0] lies in 2 to 30 and offsets[k, 1] in 2 to 30; both never fall as k rises; offsets[0] = (2, 2) and offsets[3] = (30, 30).
All inputs are finite; a program needn't handle non-finite values. No bound on the sum of `validity` on one device may be relied on, other than what follows from the above.
Results may differ from a plain program's by a relative error of at most 0.0037.
Values may be sent and summed in bfloat16 or wider, within the bound.
No kernel may reach another device: no remote copies, remote signals or barrier semaphores. Data moves between devices by JAX's collectives and lax.ppermute only.
A program may use at most 128 MiB of HBM per device.

v0:
```python
import jax
import jax.numpy as jnp
from jax import lax
from jax.sharding import PartitionSpec as P


def shifted(x, axis, by):
    peers = lax.axis_size(axis)
    pairs = [(i, i + by) for i in range(peers) if 0 <= i + by < peers]
    return lax.ppermute(x, axis, pairs)


def extended(x, sides, width):
    for axis, dim in sides:
        peers, length = (lax.axis_size(axis), x.shape[dim])
        up = [(i, (i + 1) % peers) for i in range(peers - 1)]
        down = [(j, i) for i, j in up]
        last = lax.slice_in_dim(x, length - width, length, axis=dim)
        initial = lax.slice_in_dim(x, 0, width, axis=dim)
        before = lax.ppermute(last, axis, up)
        after = lax.ppermute(initial, axis, down)
        x = jnp.concatenate([before, x, after], axis=dim)
    return x


def conv_apply(padded, weight, out_rows, out_cols):
    in_width = padded.shape[-1]
    summed = None
    for row_step in range(3):
        for col_step in range(3):
            window = padded[row_step : row_step + out_rows, col_step : col_step + out_cols].reshape(
                out_rows * out_cols, in_width
            )
            partial_sum = jnp.dot(
                window, weight[row_step, col_step], preferred_element_type=jnp.float32
            )
            summed = partial_sum if summed is None else summed + partial_sum
    return summed.reshape(out_rows, out_cols, -1)


def weight_grad(padded, back, out_rows, out_cols):
    in_width = padded.shape[-1]
    flat_back = back.reshape(out_rows * out_cols, -1)
    rows_list = []
    for row_step in range(3):
        cols_list = []
        for col_step in range(3):
            window = padded[row_step : row_step + out_rows, col_step : col_step + out_cols].reshape(
                out_rows * out_cols, in_width
            )
            cols_list.append(
                lax.dot_general(
                    window, flat_back, (((0,), (0,)), ((), ())), preferred_element_type=jnp.float32
                )
            )
        rows_list.append(jnp.stack(cols_list))
    return jnp.stack(rows_list)


def shards(current, history, validity, offsets, merge_weight, out_weight, cotangent):
    tile_rows, tile_cols, width = current.shape
    frames = history.shape[0]
    masked = history * validity.astype(jnp.bfloat16)[..., None]
    above = shifted(masked, "row", 1)
    beside = shifted(masked, "col", 1)
    corner = shifted(beside, "row", 1)
    joined = jnp.concatenate(
        [jnp.concatenate([corner, above], axis=2), jnp.concatenate([beside, masked], axis=2)],
        axis=1,
    )
    margin = 1
    ext_rows = tile_rows + 2 * margin
    ext_cols = tile_cols + 2 * margin
    row_place = lax.axis_index("row") * tile_rows - margin + jnp.arange(ext_rows, dtype=jnp.int32)
    col_place = lax.axis_index("col") * tile_cols - margin + jnp.arange(ext_cols, dtype=jnp.int32)
    row_inside = (row_place >= 0) & (row_place < tile_rows * lax.axis_size("row"))
    col_inside = (col_place >= 0) & (col_place < tile_cols * lax.axis_size("col"))
    inside = (row_inside[:, None] & col_inside[None, :]).astype(jnp.bfloat16)[..., None]
    current_pad = extended(current, (("row", 0), ("col", 1)), margin)
    pieces = [current_pad]
    for frame in range(frames):
        start_row = tile_rows - margin - offsets[frame, 0]
        start_col = tile_cols - margin - offsets[frame, 1]
        window = lax.dynamic_slice(
            joined[frame], (start_row, start_col, jnp.int32(0)), (ext_rows, ext_cols, width)
        )
        pieces.append(window * inside)
    stacked = jnp.concatenate(pieces, axis=-1)
    pre = conv_apply(stacked, merge_weight, tile_rows, tile_cols)
    hidden = jax.nn.silu(pre).astype(jnp.bfloat16)
    hidden_pad = extended(hidden, (("row", 0), ("col", 1)), 1)
    merged = (
        current.astype(jnp.float32) + conv_apply(hidden_pad, out_weight, tile_rows, tile_cols)
    ).astype(jnp.bfloat16)
    grad_pad = extended(cotangent, (("row", 0), ("col", 1)), 1)
    local_out = weight_grad(hidden_pad, cotangent, tile_rows, tile_cols)
    back_hidden = None
    for row_step in range(3):
        for col_step in range(3):
            window = grad_pad[
                2 - row_step : 2 - row_step + tile_rows, 2 - col_step : 2 - col_step + tile_cols
            ].reshape(tile_rows * tile_cols, width)
            partial_sum = lax.dot_general(
                window,
                out_weight[row_step, col_step],
                (((1,), (1,)), ((), ())),
                preferred_element_type=jnp.float32,
            )
            back_hidden = partial_sum if back_hidden is None else back_hidden + partial_sum
    back_hidden = back_hidden.reshape(tile_rows, tile_cols, width)
    sigma = jax.nn.sigmoid(pre)
    back_pre = (back_hidden * (sigma * (1.0 + pre * (1.0 - sigma)))).astype(jnp.bfloat16)
    local_merge = weight_grad(stacked, back_pre, tile_rows, tile_cols)
    merge_grad, out_grad = lax.psum((local_merge, local_out), ("row", "col"))
    return (merged, merge_grad, out_grad)


def solution(mesh):
    return jax.shard_map(
        shards,
        mesh=mesh,
        in_specs=(
            P("row", "col", None),
            P(None, "row", "col", None),
            P(None, "row", "col"),
            P(),
            P(),
            P(),
            P("row", "col", None),
        ),
        out_specs=(P("row", "col", None), P(), P()),
        check_vma=False,
    )
```

profile of v0, /device:TPU:1, one launch (start us, length us, event | category | flops | bytes accessed | tf_op | source)
XLA Modules:
  0.0 408.6 jit_solution(9587713921807527277)
XLA Ops:
  7.2 0.9 convert_element_type.26
  8.2 2.9 broadcast_multiply_fusion
  11.1 6.0 %collective-permute-start.6 = (bf16[4,32,32,256]{3,2,1,0:T(8,128)(2,1)}, bf16[4,32,32,256]{3,2,1,0:T(8,128)(2,1)}, u32[]{:S(2)}, u32[]{:S(2)}) collective-permute-start(bf16[4,32,32,256]{3,2,1,0:T(8,128)(2,1)} %broadcast_multiply_fusion), channel_id=1, source_target_pairs={{0,32},{32,64},{64,96},{1,33},{33,65},{65,97},{2,34},{34,66},{66,9... | collective-permute-start | bytes 6291464 | tf_op jit(solution)/shard_map/ppermute | solution.py:10
  17.1 4.6 %collective-permute-start.4 = (bf16[4,32,32,256]{3,2,1,0:T(8,128)(2,1)}, bf16[4,32,32,256]{3,2,1,0:T(8,128)(2,1)}, u32[]{:S(2)}, u32[]{:S(2)}) collective-permute-start(bf16[4,32,32,256]{3,2,1,0:T(8,128)(2,1)} %broadcast_multiply_fusion), channel_id=1, source_target_pairs={{0,1},{1,2},{2,3},{3,4},{4,5},{5,6},{6,7},{7,8},{8,9},{9,10},{10,1... | collective-permute-start | bytes 6291464 | tf_op jit(solution)/shard_map/ppermute | solution.py:10
  21.7 1.9 collective-permute-start.1
  23.6 5.1 %collective-permute-start = (bf16[1,32,256]{2,1,0:T(8,128)(2,1)S(1)}, bf16[1,32,256]{2,1,0:T(8,128)(2,1)S(1)}, u32[]{:S(2)}, u32[]{:S(2)}) collective-permute-start(bf16[1,32,256]{2,1,0:T(8,128)(2,1)S(1)} %get-tuple-element.53), channel_id=1, source_target_pairs={{0,32},{32,64},{64,96},{1,33},{33,65},{65,97},{2,34},{34,66},{66,9... | collective-permute-start | bytes 49160 | tf_op jit(solution)/shard_map/ppermute | solution.py:20
  28.8 1.9 collective-permute-start.12
  30.8 0.7 fusion.105
  41.6 5.1 %collective-permute-start.11 = (bf16[1,32,256]{2,1,0:T(8,128)(2,1)S(1)}, bf16[1,32,256]{2,1,0:T(8,128)(2,1)S(1)}, u32[]{:S(2)}, u32[]{:S(2)}) collective-permute-start(bf16[1,32,256]{2,1,0:T(8,128)(2,1)S(1)} %get-tuple-element.47), channel_id=1, source_target_pairs={{0,32},{32,64},{64,96},{1,33},{33,65},{65,97},{2,34},{34,66},{66,9... | collective-permute-start | bytes 49160 | tf_op jit(solution)/shard_map/ppermute | solution.py:20
  46.9 2.8 collective-permute-start.2
  50.0 1.3 collective-permute-start.13
  51.3 4.0 collective-permute-start.14
  55.3 1.2 fusion.41
  56.5 1.2 fusion.54
  57.8 1.4 collective-permute-start.3
  59.2 7.2 %collective-permute-done.14 = bf16[34,1,256]{2,1,0:T(2,128)(2,1)S(1)} collective-permute-done((bf16[34,1,256]{2,1,0:T(2,128)(2,1)S(1)}, bf16[34,1,256]{2,1,0:T(2,128)(2,1)S(1)}, u32[]{:S(2)}, u32[]{:S(2)}) %collective-permute-start.14) | collective-permute-done | bytes 17440 | tf_op jit(solution)/shard_map/ppermute | solution.py:20
  66.5 0.9 pad_maximum_fusion.5
  67.4 2.0 collective-permute-start.5
  72.1 1.4 fusion.1
  73.5 19.2 %collective-permute-done.5 = bf16[4,32,32,256]{3,2,1,0:T(8,128)(2,1)S(1)} collective-permute-done((bf16[4,32,32,256]{3,2,1,0:T(8,128)(2,1)}, bf16[4,32,32,256]{3,2,1,0:T(8,128)(2,1)S(1)}, u32[]{:S(2)}, u32[]{:S(2)}) %collective-permute-start.5) | collective-permute-done | bytes 2097184 | tf_op jit(solution)/shard_map/ppermute | solution.py:10
  92.7 3.9 maximum_maximum_fusion
  96.5 1.2 fusion.96
  98.2 0.4 fusion.5
  99.4 10.0 %fusion.97 = (bf16[32,32,1280]{2,1,0:T(8,128)(2,1)}, bf16[32,32,1280]{2,1,0:T(8,128)(2,1)}, bf16[32,32,1280]{2,1,0:T(8,128)(2,1)}, bf16[32,32,1280]{2,1,0:T(8,12...) fusion(bf16[34,34,1280]{2,1,0:T(8,128)(2,1)S(1)} %fusion.3), kind=kLoop, calls=%fused_computation.184 | loop fusion | bytes 47185920 | tf_op jit(solution)/shard_map/slice | solution.py:31
  109.4 2.9 fusion.15
  112.3 2.1 convolution_add_fusion.20
  114.4 2.1 convolution_add_fusion.19
  116.6 0.8 convolution_add_fusion.18
  117.4 0.9 copy-done.4
  118.3 0.8 convolution_add_fusion.17
  119.1 0.9 copy-done.3
  120.0 0.8 convolution_add_fusion.16
  120.9 0.9 copy-done.2
  121.8 0.8 convolution_add_fusion.15
  122.6 0.9 copy-done.1
  123.5 0.8 convolution_add_fusion.14
  124.4 0.9 copy-done
  125.3 0.8 convolution_add_fusion.13
  126.5 0.5 multiply_convert_fusion
  127.0 0.9 convolution_bitcast_fusion
  127.9 0.9 convolution_bitcast_fusion.1
  128.8 0.9 convolution_bitcast_fusion.2
  129.7 0.9 convolution_bitcast_fusion.3
  130.6 0.9 convolution_bitcast_fusion.4
  131.5 1.1 convolution_bitcast_fusion.5
  132.6 0.9 convolution_bitcast_fusion.6
  133.5 0.9 convolution_bitcast_fusion.7
  134.4 0.9 convolution_bitcast_fusion.8
  135.3 5.8 %collective-permute-start.7 = (bf16[1,32,256]{2,1,0:T(8,128)(2,1)S(1)}, bf16[1,32,256]{2,1,0:T(8,128)(2,1)S(1)}, u32[]{:S(2)}, u32[]{:S(2)}) collective-permute-start(bf16[1,32,256]{2,1,0:T(8,128)(2,1)S(1)} %get-tuple-element.50), channel_id=1, source_target_pairs={{0,32},{32,64},{64,96},{1,33},{33,65},{65,97},{2,34},{34,66},{66,9... | collective-permute-start | bytes 49160 | tf_op jit(solution)/shard_map/ppermute | solution.py:20
  141.1 1.9 collective-permute-start.8
  143.9 4.8 %pad_maximum_fusion = f32[3,3,1280,256]{3,2,1,0:T(8,128)} fusion(f32[1,3,1280,256]{3,2,1,0:T(8,128)S(1)} %maximum_bitcast_fusion.2, f32[1,3,1280,256]{3,2,1,0:T(8,128)S(1)} %maximum_bitcast_fusion.1, f32[1,3,1280,256]{3,2,1,0:T(8,128)S(1)} %maximum_bitcast_fusion), kind=kLoop, calls=%fused_computation | loop fusion | flops 5898240 | bytes 23592960 | tf_op jit(solution)/shard_map/stack | solution.py:57
  149.1 4.1 %collective-permute-start.9 = (bf16[34,1,256]{2,1,0:T(2,128)(2,1)S(1)}, bf16[34,1,256]{2,1,0:T(2,128)(2,1)S(1)}, u32[]{:S(2)}, u32[]{:S(2)}) collective-permute-start(bf16[34,1,256]{2,1,0:T(2,128)(2,1)S(1)} %get-tuple-element.39), channel_id=1, source_target_pairs={{0,1},{1,2},{2,3},{3,4},{4,5},{5,6},{6,7},{7,8},{8,9},{9,10},{10,1... | collective-permute-start | bytes 52232 | tf_op jit(solution)/shard_map/ppermute | solution.py:20
  153.2 1.3 collective-permute-start.10
  155.2 2.7 collective-permute-done.10
  157.9 0.4 maximum_maximum_fusion.1
  160.5 1.6 pad_maximum_fusion.1
  162.2 1.0 copy-done.9
  165.5 0.6 copy-done.11
  166.1 0.4 convolution_add_fusion.9
  167.5 0.4 copy-done.17
  167.9 1.0 add_convert_fusion
  168.9 221.7 %all-reduce.3.cloned.1.call-done = (f32[3,3,1280,256]{3,2,1,0:T(8,128)}, f32[3,3,256,256]{3,2,1,0:T(8,128)}) async-done(((f32[3,3,1280,256]{3,2,1,0:T(8,128)}, f32[3,3,256,256]{3,2,1,0:T(8,128)}), (f32[3,3,1280,256]{3,2,1,0:T(8,128)}, f32[3,3,256,256]{3,2,1,0:T(8,128)})) %all-reduce.3.cloned.1.call-update) | async-done | bytes 14155792 | tf_op jit(solution)/shard_map/psum | solution.py:114
  390.6 9.8 %copy.20 = f32[3,3,1280,256]{3,2,1,0:T(8,128)} copy(f32[3,3,1280,256]{3,2,1,0:T(8,128)} %get-tuple-element.65) | data formatting | bytes 23592960
  400.4 1.4 copy.21
  (105 shorter events, 12.1 us)
Async XLA Ops:
  7.2 14.5 %copy-start.16 = (bf16[32,32,256]{2,1,0:T(8,128)(2,1)S(1)}, bf16[32,32,256]{2,1,0:T(8,128)(2,1)}, u32[]{:S(2)}) copy-start(bf16[32,32,256]{2,1,0:T(8,128)(2,1)} %param.7) | copy-start | bytes 1572868
  7.2 21.6 %copy-start.18 = (bf16[32,32,256]{2,1,0:T(8,128)(2,1)S(1)}, bf16[32,32,256]{2,1,0:T(8,128)(2,1)}, u32[]{:S(2)}) copy-start(bf16[32,32,256]{2,1,0:T(8,128)(2,1)} %param.13) | copy-start | bytes 1572868
  7.2 23.6 %copy-start.21 = (s32[4,2]{0,1:T(2,128)S(1)}, s32[4,2]{0,1:T(2,128)}, u32[]{:S(2)}) copy-start(s32[4,2]{0,1:T(2,128)} %param.10) | copy-start | bytes 100
  7.2 383.4 %all-reduce.3.cloned.1.call-start = ((), (), s32[]{:S(2)}) async-start(), calls=%async_computation | async-start | bytes 28311552 | tf_op jit(solution)/shard_map/psum | solution.py:114
  11.1 62.4 %collective-permute-start.6 = (bf16[4,32,32,256]{3,2,1,0:T(8,128)(2,1)}, bf16[4,32,32,256]{3,2,1,0:T(8,128)(2,1)}, u32[]{:S(2)}, u32[]{:S(2)}) collective-permute-start(bf16[4,32,32,256]{3,2,1,0:T(8,128)(2,1)} %broadcast_multiply_fusion), channel_id=1, source_target_pairs={{0,32},{32,64},{64,96},{1,33},{33,65},{65,97},{2,34},{34,66},{66,9... | collective-permute-start | bytes 6291464 | tf_op jit(solution)/shard_map/ppermute | solution.py:10
  17.1 50.3 %collective-permute-start.4 = (bf16[4,32,32,256]{3,2,1,0:T(8,128)(2,1)}, bf16[4,32,32,256]{3,2,1,0:T(8,128)(2,1)}, u32[]{:S(2)}, u32[]{:S(2)}) collective-permute-start(bf16[4,32,32,256]{3,2,1,0:T(8,128)(2,1)} %broadcast_multiply_fusion), channel_id=1, source_target_pairs={{0,1},{1,2},{2,3},{3,4},{4,5},{5,6},{6,7},{7,8},{8,9},{9,10},{10,1... | collective-permute-start | bytes 6291464 | tf_op jit(solution)/shard_map/ppermute | solution.py:10
  21.7 25.1 %collective-permute-start.1 = (bf16[1,32,256]{2,1,0:T(8,128)(2,1)S(1)}, bf16[1,32,256]{2,1,0:T(8,128)(2,1)S(1)}, u32[]{:S(2)}, u32[]{:S(2)}) collective-permute-start(bf16[1,32,256]{2,1,0:T(8,128)(2,1)S(1)} %get-tuple-element.52), channel_id=1, source_target_pairs={{32,0},{64,32},{96,64},{33,1},{65,33},{97,65},{34,2},{66,34},{98,6... | collective-permute-start | bytes 49160 | tf_op jit(solution)/shard_map/ppermute | solution.py:21
  23.6 18.0 %collective-permute-start = (bf16[1,32,256]{2,1,0:T(8,128)(2,1)S(1)}, bf16[1,32,256]{2,1,0:T(8,128)(2,1)S(1)}, u32[]{:S(2)}, u32[]{:S(2)}) collective-permute-start(bf16[1,32,256]{2,1,0:T(8,128)(2,1)S(1)} %get-tuple-element.53), channel_id=1, source_target_pairs={{0,32},{32,64},{64,96},{1,33},{33,65},{65,97},{2,34},{34,66},{66,9... | collective-permute-start | bytes 49160 | tf_op jit(solution)/shard_map/ppermute | solution.py:20
  28.8 21.0 %collective-permute-start.12 = (bf16[1,32,256]{2,1,0:T(8,128)(2,1)S(1)}, bf16[1,32,256]{2,1,0:T(8,128)(2,1)S(1)}, u32[]{:S(2)}, u32[]{:S(2)}) collective-permute-start(bf16[1,32,256]{2,1,0:T(8,128)(2,1)S(1)} %get-tuple-element.46), channel_id=1, source_target_pairs={{32,0},{64,32},{96,64},{33,1},{65,33},{97,65},{34,2},{66,34},{98,6... | collective-permute-start | bytes 49160 | tf_op jit(solution)/shard_map/ppermute | solution.py:21
  41.6 8.1 %collective-permute-start.11 = (bf16[1,32,256]{2,1,0:T(8,128)(2,1)S(1)}, bf16[1,32,256]{2,1,0:T(8,128)(2,1)S(1)}, u32[]{:S(2)}, u32[]{:S(2)}) collective-permute-start(bf16[1,32,256]{2,1,0:T(8,128)(2,1)S(1)} %get-tuple-element.47), channel_id=1, source_target_pairs={{0,32},{32,64},{64,96},{1,33},{33,65},{65,97},{2,34},{34,66},{66,9... | collective-permute-start | bytes 49160 | tf_op jit(solution)/shard_map/ppermute | solution.py:20
  46.9 22.5 %collective-permute-start.2 = (bf16[34,1,256]{2,1,0:T(2,128)(2,1)S(1)}, bf16[34,1,256]{2,1,0:T(2,128)(2,1)S(1)}, u32[]{:S(2)}, u32[]{:S(2)}) collective-permute-start(bf16[34,1,256]{2,1,0:T(2,128)(2,1)S(1)} %get-tuple-element.41), channel_id=1, source_target_pairs={{0,1},{1,2},{2,3},{3,4},{4,5},{5,6},{6,7},{7,8},{8,9},{9,10},{10,1... | collective-permute-start | bytes 52232 | tf_op jit(solution)/shard_map/ppermute | solution.py:20
  50.0 7.8 %collective-permute-start.13 = (bf16[34,1,256]{2,1,0:T(2,128)(2,1)S(1)}, bf16[34,1,256]{2,1,0:T(2,128)(2,1)S(1)}, u32[]{:S(2)}, u32[]{:S(2)}) collective-permute-start(bf16[34,1,256]{2,1,0:T(2,128)(2,1)S(1)} %get-tuple-element.35), channel_id=1, source_target_pairs={{1,0},{2,1},{3,2},{4,3},{5,4},{6,5},{7,6},{8,7},{9,8},{10,9},{11,1... | collective-permute-start | bytes 52232 | tf_op jit(solution)/shard_map/ppermute | solution.py:21
  51.3 15.2 %collective-permute-start.14 = (bf16[34,1,256]{2,1,0:T(2,128)(2,1)S(1)}, bf16[34,1,256]{2,1,0:T(2,128)(2,1)S(1)}, u32[]{:S(2)}, u32[]{:S(2)}) collective-permute-start(bf16[34,1,256]{2,1,0:T(2,128)(2,1)S(1)} %get-tuple-element.36), channel_id=1, source_target_pairs={{0,1},{1,2},{2,3},{3,4},{4,5},{5,6},{6,7},{7,8},{8,9},{9,10},{10,1... | collective-permute-start | bytes 52232 | tf_op jit(solution)/shard_map/ppermute | solution.py:20
  57.8 12.0 %copy-start.12 = (bf16[3,3,256,256]{3,2,1,0:T(8,128)(2,1)S(1)}, bf16[3,3,256,256]{3,2,1,0:T(8,128)(2,1)}, u32[]{:S(2)}) copy-start(bf16[3,3,256,256]{3,2,1,0:T(8,128)(2,1)} %param.12) | copy-start | bytes 3538948
  57.8 11.6 %collective-permute-start.3 = (bf16[34,1,256]{2,1,0:T(2,128)(2,1)S(1)}, bf16[34,1,256]{2,1,0:T(2,128)(2,1)S(1)}, u32[]{:S(2)}, u32[]{:S(2)}) collective-permute-start(bf16[34,1,256]{2,1,0:T(2,128)(2,1)S(1)} %get-tuple-element.42), channel_id=1, source_target_pairs={{1,0},{2,1},{3,2},{4,3},{5,4},{6,5},{7,6},{8,7},{9,8},{10,9},{11,1... | collective-permute-start | bytes 52232 | tf_op jit(solution)/shard_map/ppermute | solution.py:21
  67.4 25.3 %collective-permute-start.5 = (bf16[4,32,32,256]{3,2,1,0:T(8,128)(2,1)}, bf16[4,32,32,256]{3,2,1,0:T(8,128)(2,1)S(1)}, u32[]{:S(2)}, u32[]{:S(2)}) collective-permute-start(bf16[4,32,32,256]{3,2,1,0:T(8,128)(2,1)} %collective-permute-done.4), channel_id=1, source_target_pairs={{0,32},{32,64},{64,96},{1,33},{33,65},{65,97},{2,34},{34,66},{66,9... | collective-permute-start | bytes 6291464 | tf_op jit(solution)/shard_map/ppermute | solution.py:10
  70.4 1.0 copy-start.19
  109.4 2.9 copy-start.7
  109.4 7.1 %slice-start = ((s8[5898240]{0:T(1024)(128)(4,1)}), s8[4194304]{0:T(1024)(128)(4,1)S(1)}, s32[]{:S(2)}) async-start(s8[5898240]{0:T(1024)(128)(4,1)} %bitcast.253), calls=%async_computation.1 | async-start | bytes 8388608
  112.3 2.1 copy-start.6
  112.3 4.2 %slice-start.1 = ((s8[5898240]{0:T(1024)(128)(4,1)}), s8[1703936]{0:T(1024)(128)(4,1)S(1)}, s32[]{:S(2)}) async-start(s8[5898240]{0:T(1024)(128)(4,1)} %bitcast.253), calls=%async_computation.2 | async-start | bytes 3407872
  114.4 2.1 copy-start.5
  116.6 1.7 copy-start.4
  118.3 1.7 copy-start.3
  120.0 1.7 copy-start.2
  121.8 1.7 copy-start.1
  123.5 1.7 copy-start
  125.3 1.2 copy-start.14
  126.1 1.8 copy-start.10
  127.0 30.9 %copy-start.8 = (bf16[32,32,256]{2,1,0:T(8,128)(2,1)}, bf16[32,32,256]{2,1,0:T(8,128)(2,1)S(1)}, u32[]{:S(2)}) copy-start(bf16[32,32,256]{2,1,0:T(8,128)(2,1)S(1)} %get-tuple-element.19) | copy-start | bytes 1572868
  135.3 13.7 %collective-permute-start.7 = (bf16[1,32,256]{2,1,0:T(8,128)(2,1)S(1)}, bf16[1,32,256]{2,1,0:T(8,128)(2,1)S(1)}, u32[]{:S(2)}, u32[]{:S(2)}) collective-permute-start(bf16[1,32,256]{2,1,0:T(8,128)(2,1)S(1)} %get-tuple-element.50), channel_id=1, source_target_pairs={{0,32},{32,64},{64,96},{1,33},{33,65},{65,97},{2,34},{34,66},{66,9... | collective-permute-start | bytes 49160 | tf_op jit(solution)/shard_map/ppermute | solution.py:20
  141.1 7.9 %collective-permute-start.8 = (bf16[1,32,256]{2,1,0:T(8,128)(2,1)S(1)}, bf16[1,32,256]{2,1,0:T(8,128)(2,1)S(1)}, u32[]{:S(2)}, u32[]{:S(2)}) collective-permute-start(bf16[1,32,256]{2,1,0:T(8,128)(2,1)S(1)} %get-tuple-element.51), channel_id=1, source_target_pairs={{32,0},{64,32},{96,64},{33,1},{65,33},{97,65},{34,2},{66,34},{98,6... | collective-permute-start | bytes 49160 | tf_op jit(solution)/shard_map/ppermute | solution.py:21
  143.8 4.8 %copy-start.20 = (bf16[32,32,256]{2,1,0:T(8,128)(2,1)S(1)}, bf16[32,32,256]{2,1,0:T(8,128)(2,1)}, u32[]{:S(2)}) copy-start(bf16[32,32,256]{2,1,0:T(8,128)(2,1)} %param.13) | copy-start | bytes 1572868
  149.1 6.1 %collective-permute-start.9 = (bf16[34,1,256]{2,1,0:T(2,128)(2,1)S(1)}, bf16[34,1,256]{2,1,0:T(2,128)(2,1)S(1)}, u32[]{:S(2)}, u32[]{:S(2)}) collective-permute-start(bf16[34,1,256]{2,1,0:T(2,128)(2,1)S(1)} %get-tuple-element.39), channel_id=1, source_target_pairs={{0,1},{1,2},{2,3},{3,4},{4,5},{5,6},{6,7},{7,8},{8,9},{9,10},{10,1... | collective-permute-start | bytes 52232 | tf_op jit(solution)/shard_map/ppermute | solution.py:20
  153.2 4.7 %collective-permute-start.10 = (bf16[34,1,256]{2,1,0:T(2,128)(2,1)S(1)}, bf16[34,1,256]{2,1,0:T(2,128)(2,1)S(1)}, u32[]{:S(2)}, u32[]{:S(2)}) collective-permute-start(bf16[34,1,256]{2,1,0:T(2,128)(2,1)S(1)} %get-tuple-element.40), channel_id=1, source_target_pairs={{1,0},{2,1},{3,2},{4,3},{5,4},{6,5},{7,6},{8,7},{9,8},{10,9},{11,1... | collective-permute-start | bytes 52232 | tf_op jit(solution)/shard_map/ppermute | solution.py:21
  162.2 1.0 copy-start.9
  162.2 1.4 copy-start.13
  164.9 1.2 copy-start.11
  166.9 1.0 copy-start.17
  390.6 9.8 %copy-start.15 = (f32[3,3,256,256]{3,2,1,0:T(8,128)S(1)}, f32[3,3,256,256]{3,2,1,0:T(8,128)}, u32[]{:S(2)}) copy-start(f32[3,3,256,256]{3,2,1,0:T(8,128)} %get-tuple-element.66) | copy-start | bytes 7077892
Sparse Core Ops, SparseCore 0:
  162.3 228.2 all-reduce.2
where the time goes:
time: 410 us; the launch traced here: 409 us
  waiting for transfers between devices  251 us (61%)
  starting transfers between devices  49.3 us (12%)
  matrix products  32 us (8%)
  local copies, waits for them, and re-layouts  31.2 us (8%)
  between operations  25.1 us (6%)
  other arithmetic  20.2 us (5%)
    psum x1, waiting for transfers between devices, shards(): merge_grad, out_grad = lax.psum((local_merge, local_out), ('row', 'col'))  222 us
    ppermute x6, starting transfers between devices, extended(): before = lax.ppermute(last, axis, up)  26.9 us
    ppermute x3, waiting for transfers between devices, shifted(): return lax.ppermute(x, axis, pairs)  19.2 us
    unnamed x53, local copies, waits for them, and re-layouts  18.8 us
    dot_general x18, matrix products, conv_apply(): jnp.dot(window, weight[row_step, col_step], preferred_element_type=jnp.fl...  14.9 us
    ppermute x3, starting transfers between devices, shifted(): return lax.ppermute(x, axis, pairs)  12.6 us
    dot_general x18, matrix products, weight_grad(): lax.dot_general(window, flat_back, (((0,), (0,)), ((), ())), preferred_el...  11.3 us
    slice x3, local copies, waits for them, and re-layouts, conv_apply(): padded[row_step:row_step + out_rows, col_step:col_step + out_cols]  10.4 us
  transfers between devices with their start and end apart: 16, of which 4 were waited for; matrix products, arithmetic and copies ran while one was open for 5% of the time, Pallas kernels for 0%

commit v1 on v0

v1 whole, which is shorter than its diff:
```python
import jax
import jax.numpy as jnp
from jax import lax
from jax.experimental import pallas as pl
from jax.experimental.pallas import tpu as pltpu
from jax.sharding import Mesh, PartitionSpec as P

CHIPS = ("xh", "xl", "z", "y")
ROW = ("xh", "core")
COL = ("xl", "z", "y")
BF16 = jnp.bfloat16
F32 = jnp.float32
SWAP = [(0, 1), (1, 0)]
PARAMS = pltpu.CompilerParams(
    dimension_semantics=("arbitrary",), vmem_limit_bytes=56 * 1024 * 1024
)
WHOLE = pl.BlockSpec(memory_space=pltpu.VMEM)


def moved(x, axis, by):
    peers = lax.axis_size(axis)
    return lax.ppermute(x, axis, [(i, i + by) for i in range(peers) if 0 <= i + by < peers])


def forward_kernel(start_ref, joined_ref, weight_ref, out_weight_ref, stacked_ref, hidden_ref,
                   back_ref, wide, grads, total, back_total):
    step = pl.program_id(0)
    rows, cols, width = stacked_ref.shape[1], stacked_ref.shape[2], wide.shape[-1]
    tile = rows - 2
    layers = stacked_ref.shape[-1] // width

    def spread(write):
        start = start_ref[step]

        turn = jnp.where(start == 0, 0, 2 * cols - start)

        def widen(i, carry):
            wide[i] = pltpu.roll(joined_ref[0, i].astype(F32), turn, 0)
            return carry

        lax.fori_loop(0, rows, widen, 0)

        def shift(i, carry):
            for col_step in range(3):
                write(i, col_step, wide[i, col_step : col_step + cols, :].astype(BF16))
            return carry

        lax.fori_loop(0, rows, shift, 0)

    @pl.when(step < layers)
    def _():
        place = pl.multiple_of(step * width, width)

        def write(i, col_step, value):
            stacked_ref[col_step, i, :, pl.ds(place, width)] = value

        spread(write)

    @pl.when(step == layers)
    def _():
        def write(i, col_step, value):
            grads[col_step, i] = value

        spread(write)
        total[...] = jnp.zeros_like(total)
        back_total[...] = jnp.zeros_like(back_total)

    @pl.when(step > layers)
    def _():
        tap = step - layers - 1
        row_step, col_step = tap // 3, tap % 3
        window = stacked_ref[col_step, pl.ds(row_step, tile)].reshape(tile * cols, -1)
        total[...] += jnp.dot(window, weight_ref[0], preferred_element_type=F32)
        other = grads[2 - col_step, pl.ds(2 - row_step, tile)].reshape(tile * cols, width)
        back_total[...] += lax.dot_general(
            other, out_weight_ref[0], (((1,), (1,)), ((), ())), preferred_element_type=F32
        )

    @pl.when(step == layers + 9)
    def _():
        pre = total[...]
        sigma = jax.nn.sigmoid(pre)
        hidden_ref[...] = (pre * sigma).astype(BF16)
        back_ref[...] = (back_total[...] * (sigma * (1.0 + pre * (1.0 - sigma)))).astype(BF16)


def forward(starts, joined, merge_weight, out_weight, tile, cols):
    layers, rows, _, width = joined.shape
    frames = layers - 1
    cells = tile * cols
    return pl.pallas_call(
        forward_kernel,
        grid=(layers + 9,),
        in_specs=[
            pl.BlockSpec(memory_space=pltpu.SMEM),
            pl.BlockSpec((1,) + joined.shape[1:], lambda i: (jnp.minimum(i, frames), 0, 0, 0)),
            pl.BlockSpec(
                (1, frames * width, width), lambda i: (jnp.maximum(i - layers, 0), 0, 0)
            ),
            pl.BlockSpec((1, width, width), lambda i: (jnp.maximum(i - layers, 0), 0, 0)),
        ],
        out_specs=[
            pl.BlockSpec((3, rows, cols, frames * width), lambda i: (0, 0, 0, 0)),
            pl.BlockSpec((cells, width), lambda i: (0, 0)),
            pl.BlockSpec((cells, width), lambda i: (0, 0)),
        ],
        out_shape=[
            jax.ShapeDtypeStruct((3, rows, cols, frames * width), BF16),
            jax.ShapeDtypeStruct((cells, width), BF16),
            jax.ShapeDtypeStruct((cells, width), BF16),
        ],
        scratch_shapes=[
            pltpu.VMEM(joined.shape[1:], F32),
            pltpu.VMEM((3, rows, cols, width), BF16),
            pltpu.VMEM((cells, width), F32),
            pltpu.VMEM((cells, width), F32),
        ],
        compiler_params=PARAMS,
        name="forward",
    )(starts, joined, merge_weight, out_weight)


def split_halves(core, value, keep_ref, send_ref):
    half = value.shape[-1] // 2
    low, high = value[:, :half], value[:, half:]
    first = core == 0
    keep_ref[...] = jnp.where(first, low, high)
    send_ref[...] = jnp.where(first, high, low).astype(BF16)


def merge_grad_kernel(core_ref, stacked_ref, back_ref, keep_ref, send_ref):
    row_step = pl.program_id(0) % 3
    tile = stacked_ref.shape[1] - 2
    window = stacked_ref[0, pl.ds(row_step, tile)].reshape(back_ref.shape[0], -1)
    value = lax.dot_general(
        window, back_ref[...], (((0,), (0,)), ((), ())), preferred_element_type=F32
    )
    split_halves(core_ref[0], value, keep_ref, send_ref)


def merge_gradient(core, stacked, back_pre):
    _, rows, cols, depth = stacked.shape
    half = back_pre.shape[-1] // 2

    def place(i):
        return ((i % 3) * 3 + i // 3, 0)

    return pl.pallas_call(
        merge_grad_kernel,
        grid=(9,),
        in_specs=[
            pl.BlockSpec(memory_space=pltpu.SMEM),
            pl.BlockSpec((1, rows, cols, depth), lambda i: (i // 3, 0, 0, 0)),
            pl.BlockSpec(back_pre.shape, lambda i: (0, 0)),
        ],
        out_specs=[pl.BlockSpec((depth, half), place), pl.BlockSpec((depth, half), place)],
        out_shape=[
            jax.ShapeDtypeStruct((9 * depth, half), F32),
            jax.ShapeDtypeStruct((9 * depth, half), BF16),
        ],
        compiler_params=PARAMS,
        name="merge_gradient",
    )(core, stacked, back_pre)


def out_kernel(core_ref, hidden_ref, current_ref, cotangent_ref, weight_ref, merged_ref, keep_ref,
               send_ref, shifted, total):
    step = pl.program_id(0)
    _, rows, cols, width = shifted.shape
    tile = rows - 2

    @pl.when(step == 0)
    def _():
        for col_step in range(3):
            shifted[col_step] = hidden_ref[:, col_step : col_step + cols, :].astype(BF16)
        total[...] = current_ref[...].reshape(tile * cols, width).astype(F32)

    row_step, col_step = step // 3, step % 3
    window = shifted[col_step, pl.ds(row_step, tile)].reshape(tile * cols, width)
    value = lax.dot_general(
        window,
        cotangent_ref[...].reshape(tile * cols, width),
        (((0,), (0,)), ((), ())),
        preferred_element_type=F32,
    )
    split_halves(core_ref[0], value, keep_ref, send_ref)
    total[...] += jnp.dot(window, weight_ref[0], preferred_element_type=F32)

    @pl.when(step == 8)
    def _():
        merged_ref[...] = total[...].astype(BF16).reshape(merged_ref.shape)


def out_step(core, hidden_pad, current, cotangent, out_weight):
    tile, cols, width = current.shape
    half = width // 2
    whole3 = pl.BlockSpec(current.shape, lambda i: (0, 0, 0))
    return pl.pallas_call(
        out_kernel,
        grid=(9,),
        in_specs=[
            pl.BlockSpec(memory_space=pltpu.SMEM),
            pl.BlockSpec(hidden_pad.shape, lambda i: (0, 0, 0)),
            whole3,
            whole3,
            pl.BlockSpec((1, width, width), lambda i: (i, 0, 0)),
        ],
        out_specs=[
            whole3,
            pl.BlockSpec((width, half), lambda i: (i, 0)),
            pl.BlockSpec((width, half), lambda i: (i, 0)),
        ],
        out_shape=[
            jax.ShapeDtypeStruct(current.shape, BF16),
            jax.ShapeDtypeStruct((9 * width, half), F32),
            jax.ShapeDtypeStruct((9 * width, half), BF16),
        ],
        scratch_shapes=[
            pltpu.VMEM((3, tile + 2, cols, width), BF16),
            pltpu.VMEM((tile * cols, width), F32),
        ],
        compiler_params=PARAMS,
        name="out_step",
    )(core, hidden_pad, current, cotangent, out_weight)


def shards(current, history, validity, offsets, merge_weight, out_weight, cotangent):
    tile, cols, width = current.shape
    frames = history.shape[0]
    ext = tile + 2
    core = lax.axis_index("core").astype(jnp.int32).reshape(1)
    valid = validity.astype(BF16)[..., None]
    masked = [history[k] * valid[k] for k in range(frames)]

    above3 = moved(masked[3][1:], ROW, 1)
    above2 = moved(masked[2][1:], ROW, 1)
    packed = moved(
        jnp.concatenate([masked[1][1:], masked[0][-3:], current[-1:], cotangent[-1:]], axis=0), ROW, 1
    )
    below = moved(jnp.concatenate([current[:1], cotangent[:1]], axis=0), ROW, -1)
    above1, above0 = packed[: tile - 1], packed[tile - 1 : tile + 2]
    row_last = lax.axis_index(ROW) == lax.axis_size(ROW) - 1
    col_last = lax.axis_index(COL) == lax.axis_size(COL) - 1
    row_inside = (jnp.arange(ext) < ext - 1) | ~row_last
    row_keep = row_inside.astype(BF16)[:, None, None]

    def rows_of(above, k):
        both = jnp.concatenate([above, masked[k]], axis=0)
        start = (tile - 2 - offsets[k, 0], jnp.int32(0), jnp.int32(0))
        return lax.dynamic_slice(both, start, (ext, cols, width)) * row_keep

    near3 = jnp.concatenate([above3, masked[3][:3]], axis=0) * row_keep
    near2 = rows_of(above2, 2)
    near1 = rows_of(above1, 1)
    near0 = jnp.concatenate([above0, masked[0][: tile - 1]], axis=0) * row_keep
    now = jnp.concatenate([packed[tile + 2 : tile + 3], current, below[:1]], axis=0)
    cot = jnp.concatenate([packed[tile + 3 :], cotangent, below[1:]], axis=0)

    left3 = moved(near3, COL, 1)
    left2 = moved(near2, COL, 1)
    side = moved(
        jnp.concatenate([near1, near0[:, -3:], now[:, -1:], cot[:, -1:]], axis=1), COL, 1
    )
    right = moved(jnp.concatenate([now[:, :1], cot[:, :1]], axis=1), COL, -1)

    blank = jnp.zeros((ext, cols - 2, width), BF16)
    joined = jnp.stack(
        [
            jnp.concatenate([side[:, cols + 3 : cols + 4], now, right[:, :1], blank], axis=1),
            jnp.concatenate([jnp.zeros((ext, cols - 3, width), BF16), side[:, cols : cols + 3], near0], axis=1),
            jnp.concatenate([side[:, :cols], near1], axis=1),
            jnp.concatenate([left2, near2], axis=1),
            jnp.concatenate([left3, near3], axis=1),
            jnp.concatenate([side[:, cols + 4 :], cot, right[:, 1:], blank], axis=1),
        ]
    )
    zero = jnp.zeros((1,), jnp.int32)
    frame_starts = cols - 1 - offsets[:, 1].astype(jnp.int32)
    starts = jnp.concatenate([zero, frame_starts, zero])
    outside = jnp.where(col_last, frame_starts + ext - 1, -1)
    outside = jnp.concatenate([zero - 1, outside, zero - 1])[:, None, None, None]
    place = jnp.arange(2 * cols, dtype=jnp.int32)[None, None, :, None]
    joined = joined * (place != outside).astype(BF16)

    stacked, hidden, back_pre = forward(
        starts,
        joined,
        merge_weight.reshape(9, -1, width),
        out_weight.reshape(9, width, width),
        tile,
        cols,
    )
    hidden = hidden.reshape(tile, cols, width)
    hidden_above = moved(hidden[-1:], ROW, 1)
    hidden_below = moved(hidden[:1], ROW, -1)
    hidden_pad = jnp.concatenate([hidden_above, hidden, hidden_below], axis=0)
    hidden_left = moved(hidden_pad[:, -1:], COL, 1)
    hidden_right = moved(hidden_pad[:, :1], COL, -1)
    hidden_pad = jnp.concatenate([hidden_left, hidden_pad, hidden_right], axis=1).astype(F32)

    merge_keep, merge_send = merge_gradient(core, stacked, back_pre)
    merge_got = lax.ppermute(merge_send, "core", SWAP)
    merged, out_keep, out_send = out_step(
        core, hidden_pad, current, cotangent, out_weight.reshape(9, width, width)
    )
    out_got = lax.ppermute(out_send, "core", SWAP)

    chips = lax.axis_size(CHIPS)
    half = width // 2
    pair = jnp.concatenate(
        [
            (merge_keep + merge_got.astype(F32)).astype(BF16),
            (out_keep + out_got.astype(F32)).astype(BF16),
        ],
        axis=0,
    )
    blocks = pair.reshape(chips, -1, half)
    got = lax.all_to_all(blocks, CHIPS, split_axis=0, concat_axis=0)
    share = jnp.sum(got.astype(F32), axis=0).astype(BF16)
    spread = jnp.broadcast_to(share[None], blocks.shape)
    own = lax.all_to_all(spread, CHIPS, split_axis=0, concat_axis=0).reshape(-1, half)
    other = lax.ppermute(own, "core", SWAP)
    first = core[0] == 0
    merge_rows = merge_keep.shape[0]

    def both(begin, end):
        a, b = own[begin:end], other[begin:end]
        return jnp.concatenate([jnp.where(first, a, b), jnp.where(first, b, a)], axis=1).astype(F32)

    merge_grad = both(0, merge_rows).reshape(merge_weight.shape)
    out_grad = both(merge_rows, own.shape[0]).reshape(out_weight.shape)
    return (merged, merge_grad, out_grad)


def solution(mesh):
    parts = Mesh(mesh.devices.reshape(2, 2, 2, 4, 4), ("xh", "core", "xl", "z", "y"))
    return jax.shard_map(
        shards,
        mesh=parts,
        in_specs=(
            P(ROW, COL, None),
            P(None, ROW, COL, None),
            P(None, ROW, COL),
            P(),
            P(),
            P(),
            P(ROW, COL, None),
        ),
        out_specs=(P(ROW, COL, None), P(), P()),
        check_vma=False,
    )
```

time: 410 us -> 288 us (0.70)
  waiting for transfers between devices: 251 us -> 45.6 us
  blocking collectives: 0 us -> 114 us
  Pallas kernels: 0 us -> 46.4 us
  matrix products: 32 us -> 0 us
  local copies, waits for them, and re-layouts: 31.2 us -> 4.83 us
  between operations: 25.1 us -> 3.67 us
  other arithmetic: 20.2 us -> 35.1 us
  starting transfers between devices: 49.3 us -> 37.2 us
    psum x1 -> x0, waiting for transfers between devices: 222 us -> none  [shards(): merge_grad, out_grad = lax.psum((local_merge, local_out), ('row', 'col'))]
    all_to_all x0 -> x2, blocking collectives: none -> 114 us  [the longest x1 63.9 us: shards(): got = lax.all_to_all(blocks, CHIPS, split_axis=0, concat_axis=0)]
    pallas_call x0 -> x3, Pallas kernels: none -> 46.4 us  [the longest x1 22.5 us: forward(): pl.pallas_call(forward_kernel, grid=(layers + 9,), in_specs=[pl.BlockSpec...]
    dot_general x45 -> x0, matrix products: 32 us -> none  [the longest x18 14.9 us: conv_apply(): jnp.dot(window, weight[row_step, col_step], preferred_element_type=jnp.fl...]
    unnamed x53 -> x10, local copies, waits for them, and re-layouts: 18.8 us -> 0.03 us
    ppermute x15, waiting for transfers between devices: 29.1 us -> 45.6 us  [the longest x12 37.4 us: moved(): lax.ppermute(x, axis, [(i, i + by) for i in range(peers) if 0 <= i + by <...]
    ppermute x15, starting transfers between devices: 49.3 us -> 37.2 us  [the longest x12 33.4 us: moved(): lax.ppermute(x, axis, [(i, i + by) for i in range(peers) if 0 <= i + by <...]
    convert_element_type x4 -> x8, other arithmetic: 2.48 us -> 12.7 us  [the longest x2 6.93 us: both(): jnp.concatenate([jnp.where(first, a, b), jnp.where(first, b, a)], axis=1)]
  transfers between devices with their start and end apart: 16 -> 15, of which waited for: 4 -> 8; matrix products, arithmetic and copies ran while one was open for 5% -> 4% of each run, Pallas kernels for 0% -> 3%
where the time goes in v1:
time: 288 us; the launch traced here: 286 us
  blocking collectives  114 us (40%)
  Pallas kernels  46.4 us (16%)
  waiting for transfers between devices  45.6 us (16%)
  starting transfers between devices  37.2 us (13%)
  other arithmetic  35.1 us (12%)
  local copies, waits for them, and re-layouts  4.83 us (2%)
  between operations  3.67 us (1%)
    all_to_all x1, blocking collectives, shards(): got = lax.all_to_all(blocks, CHIPS, split_axis=0, concat_axis=0)  63.9 us
    all_to_all x1, blocking collectives, shards(): lax.all_to_all(spread, CHIPS, split_axis=0, concat_axis=0).reshape(-1, half)  49.6 us
    ppermute x12, waiting for transfers between devices, moved(): lax.ppermute(x, axis, [(i, i + by) for i in range(peers) if 0 <= i + by <...  37.4 us
    ppermute x12, starting transfers between devices, moved(): lax.ppermute(x, axis, [(i, i + by) for i in range(peers) if 0 <= i + by <...  33.4 us
    pallas_call x1, Pallas kernels, forward(): pl.pallas_call(forward_kernel, grid=(layers + 9,), in_specs=[pl.BlockSpec...  22.5 us
    pallas_call x1, Pallas kernels, merge_gradient(): pl.pallas_call(merge_grad_kernel, grid=(9,), in_specs=[pl.BlockSpec(memor...  14.5 us
    pallas_call x1, Pallas kernels, out_step(): pl.pallas_call(out_kernel, grid=(9,), in_specs=[pl.BlockSpec(memory_space...  9.43 us
    concatenate x1, other arithmetic, shards(): jnp.concatenate([(merge_keep + merge_got.astype(F32)).astype(BF16), (out_...  8.41 us
  transfers between devices with their start and end apart: 15, of which 8 were waited for; matrix products, arithmetic and copies ran while one was open for 4% of the time, Pallas kernels for 3%

profile of v1, /device:TPU:1, one launch (start us, length us, event | category | flops | bytes accessed | tf_op | source)
XLA Modules:
  0.0 286.3 jit_solution(7828490124283930685)
XLA Ops:
  0.6 0.8 fusion.33
  1.4 3.3 %collective-permute-start.1 = (bf16[2,32,256]{2,1,0:T(8,128)(2,1)S(1)}, bf16[2,32,256]{2,1,0:T(8,128)(2,1)S(1)}, u32[]{:S(2)}, u32[]{:S(2)}) collective-permute-start(bf16[2,32,256]{2,1,0:T(8,128)(2,1)S(1)} %pad_maximum_fusion.7), channel_id=1, source_target_pairs={{32,0},{64,32},{96,64},{33,1},{65,33},{97,65},{34,2},{66,34},{98,6... | collective-permute-start | bytes 98312 | tf_op jit(solution)/shard_map/ppermute | solution.py:22
  4.8 0.8 convert_element_type.43
  5.6 1.9 bitcast_multiply_fusion
  7.5 0.0 copy-start.4
  7.5 0.8 slice.213
  8.4 4.6 %collective-permute-start.4 = (bf16[31,32,256]{2,1,0:T(8,128)(2,1)}, bf16[31,32,256]{2,1,0:T(8,128)(2,1)}, u32[]{:S(2)}, u32[]{:S(2)}) collective-permute-start(bf16[31,32,256]{2,1,0:T(8,128)(2,1)} %slice.213), channel_id=1, source_target_pairs={{0,32},{32,64},{64,96},{1,33},{33,65},{65,97},{2,34},{34,66},{66,9... | collective-permute-start | bytes 1523720 | tf_op jit(solution)/shard_map/ppermute | solution.py:22
  13.0 0.8 slice.215
  13.8 2.4 collective-permute-start.6
  16.3 0.1 pad_maximum_fusion.1
  16.4 1.9 collective-permute-start
  18.3 0.7 fusion.37
  19.0 0.1 pad_add_fusion.1
  21.7 9.2 %collective-permute-done = bf16[36,32,256]{2,1,0:T(8,128)(2,1)S(1)} collective-permute-done((bf16[36,32,256]{2,1,0:T(8,128)(2,1)S(1)}, bf16[36,32,256]{2,1,0:T(8,128)(2,1)S(1)}, u32[]{:S(2)}, u32[]{:S(2)}) %collective-permute-start) | collective-permute-done | bytes 589856 | tf_op jit(solution)/shard_map/ppermute | solution.py:22
  30.9 0.0 copy-start.1
  31.0 1.7 maximum_multiply_fusion.1
  32.8 0.2 fusion.16
  33.0 3.2 %collective-permute-start.2 = (bf16[34,37,256]{2,1,0:T(8,128)(2,1)S(1)}, bf16[34,37,256]{2,1,0:T(8,128)(2,1)S(1)}, u32[]{:S(2)}, u32[]{:S(2)}) collective-permute-start(bf16[34,37,256]{2,1,0:T(8,128)(2,1)S(1)} %fusion.16), channel_id=1, source_target_pairs={{0,1},{1,2},{2,3},{3,4},{4,5},{5,6},{6,7},{7,8},{8,9},{9,10},{10,1... | collective-permute-start | bytes 1932296 | tf_op jit(solution)/shard_map/ppermute | solution.py:22
  36.2 0.1 fusion.29
  36.3 0.1 fusion.28
  36.4 1.3 collective-permute-start.3
  37.7 0.6 pad_add_fusion.start_ref
  38.3 0.1 pad.41.clone
  38.4 4.0 %collective-permute-start.7 = (bf16[34,32,256]{2,1,0:T(8,128)(2,1)S(1)}, bf16[34,32,256]{2,1,0:T(8,128)(2,1)S(1)}, u32[]{:S(2)}, u32[]{:S(2)}) collective-permute-start(bf16[34,32,256]{2,1,0:T(8,128)(2,1)S(1)} %get-tuple-element.51), channel_id=1, source_target_pairs={{0,1},{1,2},{2,3},{3,4},{4,5},{5,6},{6,7},{7,8},{8,9},{9,10},{10,1... | collective-permute-start | bytes 1671176 | tf_op jit(solution)/shard_map/ppermute | solution.py:22
  42.4 3.2 %collective-permute-start.5 = (bf16[34,32,256]{2,1,0:T(8,128)(2,1)S(1)}, bf16[34,32,256]{2,1,0:T(8,128)(2,1)S(1)}, u32[]{:S(2)}, u32[]{:S(2)}) collective-permute-start(bf16[34,32,256]{2,1,0:T(8,128)(2,1)S(1)} %get-tuple-element.53), channel_id=1, source_target_pairs={{0,1},{1,2},{2,3},{3,4},{4,5},{5,6},{6,7},{7,8},{8,9},{9,10},{10,1... | collective-permute-start | bytes 1671176 | tf_op jit(solution)/shard_map/ppermute | solution.py:22
  45.6 0.1 fusion.35
  45.6 6.0 %collective-permute-done.2 = bf16[34,37,256]{2,1,0:T(8,128)(2,1)S(1)} collective-permute-done((bf16[34,37,256]{2,1,0:T(8,128)(2,1)S(1)}, bf16[34,37,256]{2,1,0:T(8,128)(2,1)S(1)}, u32[]{:S(2)}, u32[]{:S(2)}) %collective-permute-start.2) | collective-permute-done | bytes 644128 | tf_op jit(solution)/shard_map/ppermute | solution.py:22
  51.7 0.1 fusion.31
  51.7 0.4 fusion.4
  52.2 0.1 slice.211
  52.3 0.3 fusion.5
  52.6 0.1 fusion.6
  52.7 14.7 %collective-permute-done.5 = bf16[34,32,256]{2,1,0:T(8,128)(2,1)S(1)} collective-permute-done((bf16[34,32,256]{2,1,0:T(8,128)(2,1)S(1)}, bf16[34,32,256]{2,1,0:T(8,128)(2,1)S(1)}, u32[]{:S(2)}, u32[]{:S(2)}) %collective-permute-start.5) | collective-permute-done | bytes 557088 | tf_op jit(solution)/shard_map/ppermute | solution.py:22
  67.3 0.1 fusion.7
  67.4 0.1 fusion.8
  67.5 0.6 fusion.9
  68.1 3.3 %broadcast_multiply_fusion.joined_ref = bf16[6,34,64,256]{3,2,1,0:T(8,128)(2,1)} fusion(bf16[6,34,64,256]{3,2,1,0:T(8,128)(2,1)S(1)} %fusion.9, bf16[6,64]{1,0:T(8,128)(2,1)S(1)} %fusion.29), kind=kLoop, calls=%fused_computation.3 | loop fusion | flops 3342336 | bytes 13370112 | tf_op jit(solution)/shard_map/mul | solution.py:283
  71.4 22.5 %forward.1 = (bf16[3,34,32,1280]{3,2,1,0:T(8,128)(2,1)}, bf16[1024,256]{1,0:T(8,128)(2,1)}, bf16[1024,256]{1,0:T(8,128)(2,1)}) custom-call(s32[6]{0:T(128)} %pad_add_fusion.start_ref, bf16[6,34,64,256]{3,2,1,0:T(8,128)(2,1)} %broadcast_multiply_fusion.joined_ref, bf16[9,1280,256]{2,1,0:T(8,128)(2,1)} %bitcast.68, bf16[9,256,256]{2,1,0:T(8,128)(2,1)} %bitcast.69), custom_call_target="tpu_custom_call" | custom-call | tf_op jit(solution)/shard_map/forward/pallas_call | solution.py:91
  93.9 14.5 %merge_gradient.1 = (f32[11520,128]{1,0:T(8,128)}, bf16[11520,128]{1,0:T(8,128)(2,1)}) custom-call(s32[1]{0:T(128)} %bitcast.core_ref, bf16[3,34,32,1280]{3,2,1,0:T(8,128)(2,1)} %get-tuple-element.13.stacked_ref, bf16[1024,256]{1,0:T(8,128)(2,1)} %get-tuple-element.14.back_ref), custom_call_target="tpu_custom_call" | custom-call | tf_op jit(solution)/shard_map/merge_gradient/pallas_call | solution.py:148
  108.4 1.9 collective-permute-start.8
  110.4 2.4 collective-permute-start.9
  112.8 1.0 collective-permute-done.8
  113.8 3.1 %collective-permute-done.9 = bf16[1,32,256]{2,1,0:T(8,128)(2,1)S(1)} collective-permute-done((bf16[1,32,256]{2,1,0:T(8,128)(2,1)S(1)}, bf16[1,32,256]{2,1,0:T(8,128)(2,1)S(1)}, u32[]{:S(2)}, u32[]{:S(2)}) %collective-permute-start.9) | collective-permute-done | bytes 16416 | tf_op jit(solution)/shard_map/ppermute | solution.py:22
  116.9 0.1 pad_maximum_fusion.4
  117.0 3.8 %collective-permute-start.10 = (bf16[34,1,256]{2,1,0:T(2,128)(2,1)S(1)}, bf16[34,1,256]{2,1,0:T(2,128)(2,1)S(1)}, u32[]{:S(2)}, u32[]{:S(2)}) collective-permute-start(bf16[34,1,256]{2,1,0:T(2,128)(2,1)S(1)} %get-tuple-element.31), channel_id=1, source_target_pairs={{0,1},{1,2},{2,3},{3,4},{4,5},{5,6},{6,7},{7,8},{8,9},{9,10},{10,1... | collective-permute-start | bytes 52232 | tf_op jit(solution)/shard_map/ppermute | solution.py:22
  120.8 1.3 collective-permute-start.11
  122.1 3.4 %collective-permute-done.11 = bf16[34,1,256]{2,1,0:T(2,128)(2,1)S(1)} collective-permute-done((bf16[34,1,256]{2,1,0:T(2,128)(2,1)S(1)}, bf16[34,1,256]{2,1,0:T(2,128)(2,1)S(1)}, u32[]{:S(2)}, u32[]{:S(2)}) %collective-permute-start.11) | collective-permute-done | bytes 17440 | tf_op jit(solution)/shard_map/ppermute | solution.py:22
  125.5 1.4 maximum_convert_fusion.2.hidden_ref
  126.9 9.4 %out_step.1 = (bf16[32,32,256]{2,1,0:T(8,128)(2,1)}, f32[2304,128]{1,0:T(8,128)}, bf16[2304,128]{1,0:T(8,128)(2,1)}) custom-call(s32[1]{0:T(128)} %bitcast.core_ref, f32[34,34,256]{2,1,0:T(8,128)} %maximum_convert_fusion.2.hidden_ref, bf16[32,32,256]{2,1,0:T(8,128)(2,1)} %current_ref.1, bf16[32,32,256]{2,1,0:T(8,128)(2,1)} %cotangent_ref.1, ...), custom_call_target="tpu_custom_call" | custom-call | tf_op jit(solution)/shard_map/out_step/pallas_call | solution.py:198
  136.3 0.2 collective-permute-start.13
  136.5 2.2 collective-permute-done.13
  138.7 1.4 add_convert_fusion.1
  140.1 2.1 add_convert_fusion
  142.3 8.4 %pad_maximum_fusion = bf16[13824,128]{1,0:T(8,128)(2,1)S(1)} fusion(bf16[2304,128]{1,0:T(8,128)(2,1)S(1)} %add_convert_fusion.1, bf16[11520,128]{1,0:T(8,128)(2,1)S(1)} %add_convert_fusion), kind=kLoop, calls=%fused_computation.2 | loop fusion | flops 7077888 | bytes 7077888 | tf_op jit(solution)/shard_map/concatenate | solution.py:310
  150.7 63.9 %all_to_all.10 = bf16[64,216,128]{2,1,0:T(8,128)(2,1)S(1)} all-to-all(bf16[64,216,128]{2,1,0:T(8,128)(2,1)S(1)} %bitcast.65), channel_id=1, replica_groups=mesh['xh'=2,'core'=2,'xl'=2,'z'=4,'y'=4] {'xh','xl','z','y'}, dimensions={0} | all-to-all | bytes 7077888 | tf_op jit(solution)/shard_map/all_to_all | solution.py:318
  214.6 1.1 reduce_sum.12
  215.7 1.3 broadcast_in_dim.10
  217.0 49.6 %all_to_all.11 = bf16[64,216,128]{2,1,0:T(8,128)(2,1)S(1)} all-to-all(bf16[64,216,128]{2,1,0:T(8,128)(2,1)S(1)} %broadcast_in_dim.10), channel_id=1, replica_groups=mesh['xh'=2,'core'=2,'xl'=2,'z'=4,'y'=4] {'xh','xl','z','y'}, dimensions={0} | all-to-all | bytes 7077888 | tf_op jit(solution)/shard_map/all_to_all | solution.py:321
  266.7 3.6 %collective-permute-start.14 = (bf16[13824,128]{1,0:T(8,128)(2,1)S(1)}, bf16[13824,128]{1,0:T(8,128)(2,1)}, u32[]{:S(2)}, u32[]{:S(2)}) collective-permute-start(bf16[13824,128]{1,0:T(8,128)(2,1)S(1)} %bitcast.62), channel_id=1, source_target_pairs={{0,32},{32,0},{1,33},{33,1},{2,34},{34,2},{3,35},{35,3},{4,36},{36... | collective-permute-start | bytes 10616840 | tf_op jit(solution)/shard_map/ppermute | solution.py:322
  270.2 6.0 %collective-permute-done.14 = bf16[13824,128]{1,0:T(8,128)(2,1)} collective-permute-done((bf16[13824,128]{1,0:T(8,128)(2,1)S(1)}, bf16[13824,128]{1,0:T(8,128)(2,1)}, u32[]{:S(2)}, u32[]{:S(2)}) %collective-permute-start.14) | collective-permute-done | bytes 3538976 | tf_op jit(solution)/shard_map/ppermute | solution.py:322
  276.2 1.1 broadcast_select_fusion.3
  277.3 1.6 maximum_convert_fusion.1
  278.9 2.0 broadcast_select_fusion.1
  281.0 5.4 %maximum_convert_fusion = f32[3,3,1280,256]{3,2,1,0:T(8,128)} fusion(bf16[3,3,1280,128]{3,2,1,0:T(8,128)(2,1)S(1)} %bitcast.67, bf16[3,3,1280,128]{3,2,1,0:T(8,128)(2,1)S(1)} %bitcast.66), kind=kLoop, calls=%fused_computation | loop fusion | flops 11796480 | bytes 17694720 | tf_op jit(solution)/shard_map/convert_element_type | solution.py:328
  (34 shorter events, 0.3 us)
Async XLA Ops:
  1.4 20.3 %collective-permute-start.1 = (bf16[2,32,256]{2,1,0:T(8,128)(2,1)S(1)}, bf16[2,32,256]{2,1,0:T(8,128)(2,1)S(1)}, u32[]{:S(2)}, u32[]{:S(2)}) collective-permute-start(bf16[2,32,256]{2,1,0:T(8,128)(2,1)S(1)} %pad_maximum_fusion.7), channel_id=1, source_target_pairs={{32,0},{64,32},{96,64},{33,1},{65,33},{97,65},{34,2},{66,34},{98,6... | collective-permute-start | bytes 98312 | tf_op jit(solution)/shard_map/ppermute | solution.py:22
  7.5 10.8 %copy-start.4 = (s32[4,2]{0,1:T(2,128)S(1)}, s32[4,2]{0,1:T(2,128)}, u32[]{:S(2)}) copy-start(s32[4,2]{0,1:T(2,128)} %param.10) | copy-start | bytes 100
  8.4 22.6 %collective-permute-start.4 = (bf16[31,32,256]{2,1,0:T(8,128)(2,1)}, bf16[31,32,256]{2,1,0:T(8,128)(2,1)}, u32[]{:S(2)}, u32[]{:S(2)}) collective-permute-start(bf16[31,32,256]{2,1,0:T(8,128)(2,1)} %slice.213), channel_id=1, source_target_pairs={{0,32},{32,64},{64,96},{1,33},{33,65},{65,97},{2,34},{34,66},{66,9... | collective-permute-start | bytes 1523720 | tf_op jit(solution)/shard_map/ppermute | solution.py:22
  13.8 17.2 %collective-permute-start.6 = (bf16[31,32,256]{2,1,0:T(8,128)(2,1)}, bf16[31,32,256]{2,1,0:T(8,128)(2,1)}, u32[]{:S(2)}, u32[]{:S(2)}) collective-permute-start(bf16[31,32,256]{2,1,0:T(8,128)(2,1)} %slice.215), channel_id=1, source_target_pairs={{0,32},{32,64},{64,96},{1,33},{33,65},{65,97},{2,34},{34,66},{66,9... | collective-permute-start | bytes 1523720 | tf_op jit(solution)/shard_map/ppermute | solution.py:22
  16.4 14.5 %collective-permute-start = (bf16[36,32,256]{2,1,0:T(8,128)(2,1)S(1)}, bf16[36,32,256]{2,1,0:T(8,128)(2,1)S(1)}, u32[]{:S(2)}, u32[]{:S(2)}) collective-permute-start(bf16[36,32,256]{2,1,0:T(8,128)(2,1)S(1)} %pad_maximum_fusion.1), channel_id=1, source_target_pairs={{0,32},{32,64},{64,96},{1,33},{33,65},{65,97},{2,34},{34,66},{66,9... | collective-permute-start | bytes 1769480 | tf_op jit(solution)/shard_map/ppermute | solution.py:22
  30.9 1.8 copy-start
  30.9 1.8 copy-start.1
  33.0 18.7 %collective-permute-start.2 = (bf16[34,37,256]{2,1,0:T(8,128)(2,1)S(1)}, bf16[34,37,256]{2,1,0:T(8,128)(2,1)S(1)}, u32[]{:S(2)}, u32[]{:S(2)}) collective-permute-start(bf16[34,37,256]{2,1,0:T(8,128)(2,1)S(1)} %fusion.16), channel_id=1, source_target_pairs={{0,1},{1,2},{2,3},{3,4},{4,5},{5,6},{6,7},{7,8},{8,9},{9,10},{10,1... | collective-permute-start | bytes 1932296 | tf_op jit(solution)/shard_map/ppermute | solution.py:22
  36.4 9.2 %collective-permute-start.3 = (bf16[34,2,256]{2,1,0:T(2,128)(2,1)S(1)}, bf16[34,2,256]{2,1,0:T(2,128)(2,1)S(1)}, u32[]{:S(2)}, u32[]{:S(2)}) collective-permute-start(bf16[34,2,256]{2,1,0:T(2,128)(2,1)S(1)} %fusion.28), channel_id=1, source_target_pairs={{1,0},{2,1},{3,2},{4,3},{5,4},{6,5},{7,6},{8,7},{9,8},{10,9},{11,1... | collective-permute-start | bytes 104456 | tf_op jit(solution)/shard_map/ppermute | solution.py:22
  38.4 29.1 %collective-permute-start.7 = (bf16[34,32,256]{2,1,0:T(8,128)(2,1)S(1)}, bf16[34,32,256]{2,1,0:T(8,128)(2,1)S(1)}, u32[]{:S(2)}, u32[]{:S(2)}) collective-permute-start(bf16[34,32,256]{2,1,0:T(8,128)(2,1)S(1)} %get-tuple-element.51), channel_id=1, source_target_pairs={{0,1},{1,2},{2,3},{3,4},{4,5},{5,6},{6,7},{7,8},{8,9},{9,10},{10,1... | collective-permute-start | bytes 1671176 | tf_op jit(solution)/shard_map/ppermute | solution.py:22
  42.4 24.9 %collective-permute-start.5 = (bf16[34,32,256]{2,1,0:T(8,128)(2,1)S(1)}, bf16[34,32,256]{2,1,0:T(8,128)(2,1)S(1)}, u32[]{:S(2)}, u32[]{:S(2)}) collective-permute-start(bf16[34,32,256]{2,1,0:T(8,128)(2,1)S(1)} %get-tuple-element.53), channel_id=1, source_target_pairs={{0,1},{1,2},{2,3},{3,4},{4,5},{5,6},{6,7},{7,8},{8,9},{9,10},{10,1... | collective-permute-start | bytes 1671176 | tf_op jit(solution)/shard_map/ppermute | solution.py:22
  93.9 14.5 %copy-start.3 = (bf16[1024,256]{1,0:T(8,128)(2,1)S(1)}, bf16[1024,256]{1,0:T(8,128)(2,1)}, u32[]{:S(2)}) copy-start(bf16[1024,256]{1,0:T(8,128)(2,1)} %get-tuple-element.11) | copy-start | bytes 1572868
  108.4 31.7 %collective-permute-start.12 = (bf16[11520,128]{1,0:T(8,128)(2,1)}, bf16[11520,128]{1,0:T(8,128)(2,1)}, u32[]{:S(2)}, u32[]{:S(2)}) collective-permute-start(bf16[11520,128]{1,0:T(8,128)(2,1)} %get-tuple-element.16), channel_id=1, source_target_pairs={{0,32},{32,0},{1,33},{33,1},{2,34},{34,2},{3,35},{35,3},{4,36},{36... | collective-permute-start | bytes 8847368 | tf_op jit(solution)/shard_map/ppermute | solution.py:302
  108.4 5.4 %collective-permute-start.8 = (bf16[1,32,256]{2,1,0:T(8,128)(2,1)S(1)}, bf16[1,32,256]{2,1,0:T(8,128)(2,1)S(1)}, u32[]{:S(2)}, u32[]{:S(2)}) collective-permute-start(bf16[1,32,256]{2,1,0:T(8,128)(2,1)S(1)} %get-tuple-element.33), channel_id=1, source_target_pairs={{0,32},{32,64},{64,96},{1,33},{33,65},{65,97},{2,34},{34,66},{66,9... | collective-permute-start | bytes 49160 | tf_op jit(solution)/shard_map/ppermute | solution.py:22
  110.4 6.6 %collective-permute-start.9 = (bf16[1,32,256]{2,1,0:T(8,128)(2,1)S(1)}, bf16[1,32,256]{2,1,0:T(8,128)(2,1)S(1)}, u32[]{:S(2)}, u32[]{:S(2)}) collective-permute-start(bf16[1,32,256]{2,1,0:T(8,128)(2,1)S(1)} %get-tuple-element.34), channel_id=1, source_target_pairs={{32,0},{64,32},{96,64},{33,1},{65,33},{97,65},{34,2},{66,34},{98,6... | collective-permute-start | bytes 49160 | tf_op jit(solution)/shard_map/ppermute | solution.py:22
  117.0 5.1 %collective-permute-start.10 = (bf16[34,1,256]{2,1,0:T(2,128)(2,1)S(1)}, bf16[34,1,256]{2,1,0:T(2,128)(2,1)S(1)}, u32[]{:S(2)}, u32[]{:S(2)}) collective-permute-start(bf16[34,1,256]{2,1,0:T(2,128)(2,1)S(1)} %get-tuple-element.31), channel_id=1, source_target_pairs={{0,1},{1,2},{2,3},{3,4},{4,5},{5,6},{6,7},{7,8},{8,9},{9,10},{10,1... | collective-permute-start | bytes 52232 | tf_op jit(solution)/shard_map/ppermute | solution.py:22
  120.8 4.7 %collective-permute-start.11 = (bf16[34,1,256]{2,1,0:T(2,128)(2,1)S(1)}, bf16[34,1,256]{2,1,0:T(2,128)(2,1)S(1)}, u32[]{:S(2)}, u32[]{:S(2)}) collective-permute-start(bf16[34,1,256]{2,1,0:T(2,128)(2,1)S(1)} %get-tuple-element.32), channel_id=1, source_target_pairs={{1,0},{2,1},{3,2},{4,3},{5,4},{6,5},{7,6},{8,7},{9,8},{10,9},{11,1... | collective-permute-start | bytes 52232 | tf_op jit(solution)/shard_map/ppermute | solution.py:22
  126.9 13.3 %copy-start.2 = (f32[11520,128]{1,0:T(8,128)S(1)}, f32[11520,128]{1,0:T(8,128)}, u32[]{:S(2)}) copy-start(f32[11520,128]{1,0:T(8,128)} %get-tuple-element.15) | copy-start | bytes 17694724
  136.3 2.4 collective-permute-start.13
  266.7 9.5 %collective-permute-start.14 = (bf16[13824,128]{1,0:T(8,128)(2,1)S(1)}, bf16[13824,128]{1,0:T(8,128)(2,1)}, u32[]{:S(2)}, u32[]{:S(2)}) collective-permute-start(bf16[13824,128]{1,0:T(8,128)(2,1)S(1)} %bitcast.62), channel_id=1, source_target_pairs={{0,32},{32,0},{1,33},{33,1},{2,34},{34,2},{3,35},{35,3},{4,36},{36... | collective-permute-start | bytes 10616840 | tf_op jit(solution)/shard_map/ppermute | solution.py:322

commit v2 on v1

v2 whole, which is shorter than its diff:
```python
import functools

import jax
import jax.numpy as jnp
from jax import lax
from jax.experimental import pallas as pl
from jax.experimental.pallas import tpu as pltpu
from jax.sharding import Mesh, PartitionSpec as P

CHIPS = ("xh", "xl", "z", "y")
ROW = ("xh", "core")
COL = ("xl", "z", "y")
BF16 = jnp.bfloat16
F32 = jnp.float32
SWAP = [(0, 1), (1, 0)]


def work(products, moved_bytes):
    return pl.CostEstimate(flops=2 * products, transcendentals=0, bytes_accessed=moved_bytes)


PARAMS = pltpu.CompilerParams(
    dimension_semantics=("arbitrary",), vmem_limit_bytes=56 * 1024 * 1024
)
WHOLE = pl.BlockSpec(memory_space=pltpu.VMEM)


def moved(x, axis, by):
    peers = lax.axis_size(axis)
    return lax.ppermute(x, axis, [(i, i + by) for i in range(peers) if 0 <= i + by < peers])


def own_half_first(core, value):
    half = value.shape[-1] // 2
    low, high = value[:, :half], value[:, half:]
    first = core == 0
    return jnp.concatenate([jnp.where(first, low, high), jnp.where(first, high, low)], axis=1)


def forward_kernel(core_ref, joined_ref, weight_ref, out_weight_ref, stacked_ref, hidden_ref,
                   back_ref, even, odd, total, back_total):
    step = pl.program_id(0)
    steps = pl.num_programs(0)
    _, rows, cols, width = even.shape
    tile = rows - 2

    def taps(now, before, shifting, multiply):
        def tap(t, carry):
            if multiply is not None:
                multiply(t, before)
            if shifting:
                for more in range(4):
                    row = jnp.minimum(4 * t + more, rows - 1)
                    value = joined_ref[0, row]
                    wide = value.astype(F32)
                    for col_step in range(3):
                        if col_step == 0:
                            part = value[:cols]
                        else:
                            part = wide[col_step : col_step + cols].astype(BF16)
                        now[col_step, row] = part
                        stacked_ref[0, col_step, row] = part
            return carry

        lax.fori_loop(0, 9, tap, 0, unroll=True)

    def forward_tap(t, before):
        window = before[t % 3, pl.ds(t // 3, tile)].reshape(tile * cols, width)
        total[...] += jnp.dot(window, weight_ref[t], preferred_element_type=F32)

    def back_tap(t, before):
        window = before[2 - t % 3, pl.ds(2 - t // 3, tile)].reshape(tile * cols, width)
        back_total[...] += lax.dot_general(
            window, out_weight_ref[t], (((1,), (1,)), ((), ())), preferred_element_type=F32
        )

    @pl.when(step == 0)
    def _():
        total[...] = jnp.zeros_like(total)
        back_total[...] = jnp.zeros_like(back_total)
        taps(even, odd, True, None)

    @pl.when(step == 1)
    def _():
        taps(odd, even, True, back_tap)

    @pl.when((step > 1) & (step < steps - 1) & (step % 2 == 0))
    def _():
        taps(even, odd, True, forward_tap)

    @pl.when((step > 1) & (step < steps - 1) & (step % 2 == 1))
    def _():
        taps(odd, even, True, forward_tap)

    @pl.when(step == steps - 1)
    def _():
        taps(even, odd, False, forward_tap)
        pre = total[...]
        sigma = jax.nn.sigmoid(pre)
        hidden_ref[...] = (pre * sigma).astype(BF16)
        back = back_total[...] * (sigma * (1.0 + pre * (1.0 - sigma)))
        back_ref[...] = own_half_first(core_ref[0], back).astype(BF16)


def forward(core, joined, merge_weight, out_weight):
    layers, rows, wide_cols, width = joined.shape
    cols = wide_cols - 2
    frames = layers - 1
    cells = (rows - 2) * cols
    return pl.pallas_call(
        forward_kernel,
        grid=(layers + 1,),
        in_specs=[
            pl.BlockSpec(memory_space=pltpu.SMEM),
            pl.BlockSpec((1,) + joined.shape[1:], lambda i: (jnp.minimum(i, frames), 0, 0, 0)),
            pl.BlockSpec((9, width, width), lambda i: (0, jnp.maximum(i - 2, 0), 0)),
            pl.BlockSpec((9, width, width), lambda i: (0, 0, 0)),
        ],
        out_specs=[
            pl.BlockSpec(
                (1, 3, rows, cols, width),
                lambda i: (jnp.clip(i - 1, 0, frames - 1), 0, 0, 0, 0),
            ),
            pl.BlockSpec((cells, width), lambda i: (0, 0)),
            pl.BlockSpec((cells, width), lambda i: (0, 0)),
        ],
        out_shape=[
            jax.ShapeDtypeStruct((frames, 3, rows, cols, width), BF16),
            jax.ShapeDtypeStruct((cells, width), BF16),
            jax.ShapeDtypeStruct((cells, width), BF16),
        ],
        scratch_shapes=[
            pltpu.VMEM((3, rows, cols, width), BF16),
            pltpu.VMEM((3, rows, cols, width), BF16),
            pltpu.VMEM((cells, width), F32),
            pltpu.VMEM((cells, width), F32),
        ],
        compiler_params=PARAMS,
        cost_estimate=work(9 * cells * width * width * layers, 25_000_000),
        name="forward",
    )(core, joined, merge_weight, out_weight)


def merge_grad_kernel(stacked_ref, back_ref, *refs):
    keep_ref, send_ref = refs[-2:]
    row_step = pl.program_id(0) % 3
    frames, _, rows, _, width = stacked_ref.shape
    half = keep_ref.shape[-1]
    for frame in range(frames):
        window = stacked_ref[frame, 0, pl.ds(row_step, rows - 2)].reshape(-1, width)
        value = lax.dot_general(
            window, back_ref[...], (((0,), (0,)), ((), ())), preferred_element_type=F32
        )
        keep_ref[frame * width : (frame + 1) * width] = value[:, :half]
        send_ref[frame * width : (frame + 1) * width] = value[:, half:].astype(BF16)


def merge_gradient(stacked, back_pre, begin, end, into=()):
    frames, _, rows, cols, width = stacked.shape
    depth = frames * width
    half = width // 2

    def place(i):
        return ((i % 3) * 3 + begin + i // 3, 0)

    return pl.pallas_call(
        merge_grad_kernel,
        grid=(3 * (end - begin),),
        in_specs=[
            pl.BlockSpec(
                (frames, 1, rows, cols, width), lambda i: (0, begin + i // 3, 0, 0, 0)
            ),
            pl.BlockSpec(back_pre.shape, lambda i: (0, 0)),
        ]
        + [pl.BlockSpec(memory_space=pl.ANY)] * len(into),
        out_specs=[pl.BlockSpec((depth, half), place), pl.BlockSpec((depth, half), place)],
        out_shape=[
            jax.ShapeDtypeStruct((9 * depth, half), F32),
            jax.ShapeDtypeStruct((9 * depth, half), BF16),
        ],
        input_output_aliases={2 + k: k for k in range(len(into))},
        compiler_params=PARAMS,
        cost_estimate=work(
            3 * (end - begin) * back_pre.shape[0] * depth * back_pre.shape[1],
            8_000_000 * (end - begin),
        ),
        name="merge_gradient",
    )(stacked, back_pre, *into)


def out_kernel(core_ref, hidden_ref, current_ref, cotangent_ref, weight_ref, merged_ref, keep_ref,
               send_ref, shifted, turned, total):
    row_step = pl.program_id(0)
    _, rows, cols, width = shifted.shape
    tile = rows - 2
    half = width // 2

    @pl.when(row_step == 0)
    def _():
        for col_step in range(3):
            shifted[col_step] = hidden_ref[:, col_step : col_step + cols, :].astype(BF16)
        total[...] = current_ref[...].reshape(tile * cols, width).astype(F32)
        turned[...] = own_half_first(core_ref[0], cotangent_ref[...].reshape(tile * cols, width))

    summed = total[...]
    for col_step in range(3):
        window = shifted[col_step, pl.ds(row_step, tile)].reshape(tile * cols, width)
        value = lax.dot_general(
            window, turned[...], (((0,), (0,)), ((), ())), preferred_element_type=F32
        )
        keep_ref[col_step * width : (col_step + 1) * width] = value[:, :half]
        send_ref[col_step * width : (col_step + 1) * width] = value[:, half:].astype(BF16)
        summed = summed + jnp.dot(window, weight_ref[col_step], preferred_element_type=F32)
    total[...] = summed

    @pl.when(row_step == 2)
    def _():
        merged_ref[...] = total[...].astype(BF16).reshape(merged_ref.shape)


def out_step(core, hidden_pad, current, cotangent, out_weight):
    tile, cols, width = current.shape
    half = width // 2
    whole3 = pl.BlockSpec(current.shape, lambda i: (0, 0, 0))
    return pl.pallas_call(
        out_kernel,
        grid=(3,),
        in_specs=[
            pl.BlockSpec(memory_space=pltpu.SMEM),
            pl.BlockSpec(hidden_pad.shape, lambda i: (0, 0, 0)),
            whole3,
            whole3,
            pl.BlockSpec((3, width, width), lambda i: (i, 0, 0)),
        ],
        out_specs=[
            whole3,
            pl.BlockSpec((3 * width, half), lambda i: (i, 0)),
            pl.BlockSpec((3 * width, half), lambda i: (i, 0)),
        ],
        out_shape=[
            jax.ShapeDtypeStruct(current.shape, BF16),
            jax.ShapeDtypeStruct((9 * width, half), F32),
            jax.ShapeDtypeStruct((9 * width, half), BF16),
        ],
        scratch_shapes=[
            pltpu.VMEM((3, tile + 2, cols, width), BF16),
            pltpu.VMEM((tile * cols, width), BF16),
            pltpu.VMEM((tile * cols, width), F32),
        ],
        compiler_params=PARAMS,
        cost_estimate=work(18 * tile * cols * width * width, 8_000_000),
        name="out_step",
    )(core, hidden_pad, current, cotangent, out_weight)


def pair_kernel(many, keep_a, got_a, keep_b, got_b, pair_ref):
    step = pl.program_id(0)

    @pl.when(step < many)
    def _():
        pair_ref[...] = (keep_a[...] + got_a[...].astype(F32)).astype(BF16)

    @pl.when(step >= many)
    def _():
        pair_ref[...] = (keep_b[...] + got_b[...].astype(F32)).astype(BF16)


BLOCK = 2304


def pair_sums(keep_a, got_a, keep_b, got_b):
    half = keep_a.shape[1]
    many, more = keep_a.shape[0] // BLOCK, keep_b.shape[0] // BLOCK
    at_a = pl.BlockSpec((BLOCK, half), lambda i: (jnp.minimum(i, many - 1), 0))
    at_b = pl.BlockSpec((BLOCK, half), lambda i: (jnp.maximum(i - many, 0), 0))
    return pl.pallas_call(
        functools.partial(pair_kernel, many),
        grid=(many + more,),
        in_specs=[at_a, at_a, at_b, at_b],
        out_specs=pl.BlockSpec((BLOCK, half), lambda i: (i, 0)),
        out_shape=jax.ShapeDtypeStruct(((many + more) * BLOCK, half), BF16),
        compiler_params=PARAMS,
        name="pair_sums",
    )(keep_a, got_a, keep_b, got_b)


def shards(current, history, validity, offsets, merge_weight, out_weight, cotangent):
    tile, cols, width = current.shape
    frames = history.shape[0]
    ext = tile + 2
    core = lax.axis_index("core").astype(jnp.int32).reshape(1)
    valid = validity.astype(BF16)[..., None]
    masked = [history[k] * valid[k] for k in range(frames)]

    row_last = lax.axis_index(ROW) == lax.axis_size(ROW) - 1
    col_last = lax.axis_index(COL) == lax.axis_size(COL) - 1
    row_inside = (jnp.arange(ext) < ext - 1) | ~row_last
    ext_cols = cols + 2
    col_inside = (jnp.arange(ext_cols) < ext_cols - 1) | ~col_last
    inside = (row_inside[:, None] & col_inside[None, :]).astype(BF16)[..., None]

    own12 = jnp.concatenate([masked[1], masked[2]], axis=0)
    left12 = moved(own12, COL, 1)
    packed = moved(
        jnp.concatenate([masked[3][1:], masked[0][-3:], current[-1:], cotangent[-1:]], axis=0), ROW, 1
    )
    below = moved(jnp.concatenate([current[:1], cotangent[:1]], axis=0), ROW, -1)
    above3, above0 = packed[: tile - 1], packed[tile - 1 : tile + 2]
    near3 = jnp.concatenate([above3, masked[3][:3]], axis=0)
    near0 = jnp.concatenate([above0, masked[0][: tile - 1]], axis=0)
    now = jnp.concatenate([packed[tile + 2 : tile + 3], current, below[:1]], axis=0)
    cot = jnp.concatenate([packed[tile + 3 :], cotangent, below[1:]], axis=0)
    side = moved(
        jnp.concatenate([near3, near0[:, -3:], now[:, -1:], cot[:, -1:]], axis=1), COL, 1
    )
    right = moved(jnp.concatenate([now[:, :1], cot[:, :1]], axis=1), COL, -1)

    left12, right = lax.optimization_barrier((left12, right))

    def cols_of(k):
        part = slice((k - 1) * tile, k * tile)
        wide = jnp.concatenate([left12[part], masked[k]], axis=1)
        start = cols - 1 - offsets[k, 1]
        return lax.dynamic_slice(wide, (jnp.int32(0), start, jnp.int32(0)), (tile, ext_cols, width))

    wide1, wide2 = cols_of(1), cols_of(2)
    above12 = moved(jnp.concatenate([wide1[1:], wide2[1:]], axis=0), ROW, 1)

    def rows_of(above, wide, k):
        both = jnp.concatenate([above, wide], axis=0)
        start = tile - 2 - offsets[k, 0]
        return lax.dynamic_slice(both, (start, jnp.int32(0), jnp.int32(0)), (ext, ext_cols, width)) * inside

    joined = jnp.stack(
        [
            jnp.concatenate([side[:, cols + 4 :], cot, right[:, 1:]], axis=1),
            jnp.concatenate([side[:, cols + 3 : cols + 4], now, right[:, :1]], axis=1),
            jnp.concatenate([side[:, cols : cols + 3], near0[:, : cols - 1]], axis=1) * inside,
            rows_of(above12[: tile - 1], wide1, 1),
            rows_of(above12[tile - 1 :], wide2, 2),
            jnp.concatenate([side[:, 1:cols], near3[:, :3]], axis=1) * inside,
        ]
    )
    stacked, hidden, back_pre = forward(
        core, joined, merge_weight.reshape(9, -1, width), out_weight.reshape(9, width, width)
    )
    hidden = hidden.reshape(tile, cols, width)
    hidden_above = moved(hidden[-1:], ROW, 1)
    hidden_below = moved(hidden[:1], ROW, -1)
    first_taps = merge_gradient(stacked, back_pre, 0, 1)
    back_pre, hidden_above, hidden_below = lax.optimization_barrier(
        (back_pre, hidden_above, hidden_below)
    )
    hidden_pad = jnp.concatenate([hidden_above, hidden, hidden_below], axis=0)
    hidden_left = moved(hidden_pad[:, -1:], COL, 1)
    hidden_right = moved(hidden_pad[:, :1], COL, -1)
    more_taps = merge_gradient(stacked, back_pre, 1, 2, first_taps)
    back_pre, hidden_left, hidden_right = lax.optimization_barrier(
        (back_pre, hidden_left, hidden_right)
    )
    hidden_pad = jnp.concatenate([hidden_left, hidden_pad, hidden_right], axis=1).astype(F32)

    merge_keep, merge_send = merge_gradient(stacked, back_pre, 2, 3, more_taps)
    merge_got = lax.ppermute(merge_send, "core", SWAP)
    merged, out_keep, out_send = out_step(
        core, hidden_pad, current, cotangent, out_weight.reshape(9, width, width)
    )
    out_got = lax.ppermute(out_send, "core", SWAP)

    chips = lax.axis_size(CHIPS)
    half = width // 2
    pair = pair_sums(merge_keep, merge_got, out_keep, out_got)
    blocks = pair.reshape(chips, -1, half)
    got = lax.all_to_all(blocks, CHIPS, split_axis=0, concat_axis=0)
    share = jnp.sum(got.astype(F32), axis=0).astype(BF16)
    spread = jnp.broadcast_to(share[None], blocks.shape)
    own = lax.all_to_all(spread, CHIPS, split_axis=0, concat_axis=0).reshape(-1, half)
    other = lax.ppermute(own, "core", SWAP)
    first = core[0] == 0
    merge_rows = merge_keep.shape[0]

    def both(begin, end):
        a, b = own[begin:end], other[begin:end]
        return jnp.concatenate([jnp.where(first, a, b), jnp.where(first, b, a)], axis=1).astype(F32)

    merge_grad = both(0, merge_rows).reshape(merge_weight.shape)
    out_grad = both(merge_rows, own.shape[0]).reshape(out_weight.shape)
    return (merged, merge_grad, out_grad)


def solution(mesh):
    parts = Mesh(mesh.devices.reshape(2, 2, 2, 4, 4), ("xh", "core", "xl", "z", "y"))
    return jax.shard_map(
        shards,
        mesh=parts,
        in_specs=(
            P(ROW, COL, None),
            P(None, ROW, COL, None),
            P(None, ROW, COL),
            P(),
            P(),
            P(),
            P(ROW, COL, None),
        ),
        out_specs=(P(ROW, COL, None), P(), P()),
        check_vma=False,
    )
```

time: 288 us -> 268 us (0.931)
  waiting for transfers between devices: 45.6 us -> 26 us
  other arithmetic: 35.1 us -> 21.5 us
  local copies, waits for them, and re-layouts: 4.83 us -> 13.9 us
  starting transfers between devices: 37.2 us -> 40.9 us
    ppermute x12 -> x10, waiting for transfers between devices: 37.4 us -> 18.2 us  [moved(): lax.ppermute(x, axis, [(i, i + by) for i in range(peers) if 0 <= i + by <...]
    concatenate x5 -> x8, other arithmetic: 9.39 us -> 3.51 us  [the longest x1 1.06 us: shards(): own12 = jnp.concatenate([masked[1], masked[2]], axis=0)]
    unnamed x10 -> x18, local copies, waits for them, and re-layouts: 0.03 us -> 5.18 us
    mul x2 -> x0, other arithmetic: 5.02 us -> none  [the longest x1 3.3 us: shards(): joined = joined * (place != outside).astype(BF16)]
    ppermute x12 -> x10, starting transfers between devices: 33.4 us -> 37 us  [moved(): lax.ppermute(x, axis, [(i, i + by) for i in range(peers) if 0 <= i + by <...]
    convert_element_type x4 -> x1, other arithmetic: 3.6 us -> 0.08 us  [shards(): inside = (row_inside[:, None] & col_inside[None, :]).astype(BF16)[..., None]]
    slice x14, local copies, waits for them, and re-layouts: 2.64 us -> 6.16 us  [the longest x2 1.87 us: shards(): above3, above0 = (packed[:tile - 1], packed[tile - 1:tile + 2])]
    pallas_call x3 -> x6, Pallas kernels: 46.4 us -> 44.8 us  [the longest x3 17.2 us: merge_gradient(): pl.pallas_call(merge_grad_kernel, grid=(3 * (end - begin),), in_specs=[pl...]
  transfers between devices with their start and end apart: 15 -> 13, of which waited for: 8 -> 5; matrix products, arithmetic and copies ran while one was open for 4% -> 4% of each run, Pallas kernels for 3% -> 7%
where the time goes in v2:
time: 268 us; the launch traced here: 266 us
  blocking collectives  113 us (42%)
  Pallas kernels  44.8 us (17%)
  starting transfers between devices  40.9 us (15%)
  waiting for transfers between devices  26 us (10%)
  other arithmetic  21.5 us (8%)
  local copies, waits for them, and re-layouts  13.9 us (5%)
  between operations  5.75 us (2%)
    all_to_all x1, blocking collectives, shards(): got = lax.all_to_all(blocks, CHIPS, split_axis=0, concat_axis=0)  62.7 us
    all_to_all x1, blocking collectives, shards(): lax.all_to_all(spread, CHIPS, split_axis=0, concat_axis=0).reshape(-1, half)  50.7 us
    ppermute x10, starting transfers between devices, moved(): lax.ppermute(x, axis, [(i, i + by) for i in range(peers) if 0 <= i + by <...  37 us
    ppermute x10, waiting for transfers between devices, moved(): lax.ppermute(x, axis, [(i, i + by) for i in range(peers) if 0 <= i + by <...  18.2 us
    pallas_call x3, Pallas kernels, merge_gradient(): pl.pallas_call(merge_grad_kernel, grid=(3 * (end - begin),), in_specs=[pl...  17.2 us
    pallas_call x1, Pallas kernels, forward(): pl.pallas_call(forward_kernel, grid=(layers + 1,), in_specs=[pl.BlockSpec...  14 us
    pallas_call x1, Pallas kernels, pair_sums(): pl.pallas_call(functools.partial(pair_kernel, many), grid=(many + more,),...  7.25 us
    convert_element_type x2, other arithmetic, both(): jnp.concatenate([jnp.where(first, a, b), jnp.where(first, b, a)], axis=1)  6.93 us
  transfers between devices with their start and end apart: 13, of which 5 were waited for; matrix products, arithmetic and copies ran while one was open for 4% of the time, Pallas kernels for 7%

profile of v2, /device:TPU:1, one launch (start us, length us, event | category | flops | bytes accessed | tf_op | source)
XLA Modules:
  0.0 266.2 jit_solution(4355757823833865641)
XLA Ops:
  0.6 0.8 convert_element_type.23
  1.5 2.0 bitcast_multiply_fusion.3
  3.6 0.7 copy-done.4
  4.3 0.9 pad_maximum_fusion.2
  5.3 6.2 %collective-permute-start = (bf16[36,32,256]{2,1,0:T(8,128)(2,1)}, bf16[36,32,256]{2,1,0:T(8,128)(2,1)}, u32[]{:S(2)}, u32[]{:S(2)}) collective-permute-start(bf16[36,32,256]{2,1,0:T(8,128)(2,1)} %pad_maximum_fusion.2), channel_id=1, source_target_pairs={{0,32},{32,64},{64,96},{1,33},{33,65},{65,97},{2,34},{34,66},{66,9... | collective-permute-start | bytes 1769480 | tf_op jit(solution)/shard_map/ppermute | solution.py:30
  11.5 1.9 collective-permute-start.1
  13.4 1.1 pad_maximum_fusion.1
  14.4 4.2 %collective-permute-start.3 = (bf16[64,32,256]{2,1,0:T(8,128)(2,1)}, bf16[64,32,256]{2,1,0:T(8,128)(2,1)}, u32[]{:S(2)}, u32[]{:S(2)}) collective-permute-start(bf16[64,32,256]{2,1,0:T(8,128)(2,1)} %pad_maximum_fusion.1), channel_id=1, source_target_pairs={{0,1},{1,2},{2,3},{3,4},{4,5},{5,6},{6,7},{7,8},{8,9},{9,10},{10,1... | collective-permute-start | bytes 3145736 | tf_op jit(solution)/shard_map/ppermute | solution.py:30
  18.6 0.1 and_convert_fusion
  18.7 0.7 fusion.48
  21.6 1.1 slice.231
  25.2 0.7 fusion.43
  26.0 0.1 fusion.39
  26.0 1.3 collective-permute-start.4
  27.3 1.1 slice.228
  28.4 0.8 slice.230
  29.3 0.2 fusion.13
  29.5 4.0 %collective-permute-start.2 = (bf16[34,37,256]{2,1,0:T(8,128)(2,1)S(1)}, bf16[34,37,256]{2,1,0:T(8,128)(2,1)S(1)}, u32[]{:S(2)}, u32[]{:S(2)}) collective-permute-start(bf16[34,37,256]{2,1,0:T(8,128)(2,1)S(1)} %fusion.13), channel_id=1, source_target_pairs={{0,1},{1,2},{2,3},{3,4},{4,5},{5,6},{6,7},{7,8},{8,9},{9,10},{10,1... | collective-permute-start | bytes 1932296 | tf_op jit(solution)/shard_map/ppermute | solution.py:30
  33.6 7.4 %collective-permute-done.3 = bf16[64,32,256]{2,1,0:T(8,128)(2,1)} collective-permute-done((bf16[64,32,256]{2,1,0:T(8,128)(2,1)}, bf16[64,32,256]{2,1,0:T(8,128)(2,1)}, u32[]{:S(2)}, u32[]{:S(2)}) %collective-permute-start.3) | collective-permute-done | bytes 1048608 | tf_op jit(solution)/shard_map/ppermute | solution.py:30
  41.0 1.3 fusion.41
  42.3 1.0 fusion.30
  43.4 0.1 pad_maximum_fusion
  43.5 0.3 copy.14
  43.8 6.2 %collective-permute-start.5 = (bf16[62,34,256]{2,0,1:T(8,128)(2,1)S(1)}, bf16[62,34,256]{2,0,1:T(8,128)(2,1)S(1)}, u32[]{:S(2)}, u32[]{:S(2)}) collective-permute-start(bf16[62,34,256]{2,0,1:T(8,128)(2,1)S(1)} %copy.14), channel_id=1, source_target_pairs={{0,32},{32,64},{64,96},{1,33},{33,65},{65,97},{2,34},{34,66},{66,9... | collective-permute-start | bytes 3237896 | tf_op jit(solution)/shard_map/ppermute | solution.py:30
  50.0 3.5 %collective-permute-done.2 = bf16[34,37,256]{2,1,0:T(8,128)(2,1)S(1)} collective-permute-done((bf16[34,37,256]{2,1,0:T(8,128)(2,1)S(1)}, bf16[34,37,256]{2,1,0:T(8,128)(2,1)S(1)}, u32[]{:S(2)}, u32[]{:S(2)}) %collective-permute-start.2) | collective-permute-done | bytes 644128 | tf_op jit(solution)/shard_map/ppermute | solution.py:30
  53.6 0.1 fusion.42
  53.6 0.3 fusion.26
  53.9 0.4 fusion.27
  54.3 0.4 fusion.28
  54.7 0.3 slice_bitcast_fusion
  55.0 7.2 %collective-permute-done.5 = bf16[62,34,256]{2,0,1:T(8,128)(2,1)S(1)} collective-permute-done((bf16[62,34,256]{2,0,1:T(8,128)(2,1)S(1)}, bf16[62,34,256]{2,0,1:T(8,128)(2,1)S(1)}, u32[]{:S(2)}, u32[]{:S(2)}) %collective-permute-start.5) | collective-permute-done | bytes 1079328 | tf_op jit(solution)/shard_map/ppermute | solution.py:30
  62.2 0.3 fusion.40
  62.5 0.3 copy.17
  62.8 0.3 copy.18
  63.1 0.5 fusion.23
  63.7 0.5 fusion.19
  64.2 0.3 fusion.29.joined_ref
  64.5 2.0 copy-done.6
  66.5 14.0 %forward.1 = (bf16[5,3,34,32,256]{4,3,2,1,0:T(8,128)(2,1)}, bf16[1024,256]{1,0:T(8,128)(2,1)}, bf16[1024,256]{1,0:T(8,128)(2,1)}) custom-call(s32[1]{0:T(128)} %bitcast.core_ref, bf16[6,34,34,256]{3,2,1,0:T(8,128)(2,1)} %copy-done.6, bf16[9,1280,256]{2,1,0:T(8,128)(2,1)} %bitcast.72, bf16[9,256,256]{2,1,0:T(8,128)(2,1)} %bitcast.73), custom_call_target="tpu_custom_call" | custom-call | flops 7247757312 | bytes 25000000 | tf_op jit(solution)/shard_map/forward/pallas_call | solution.py:110
  80.5 0.7 slice_bitcast_fusion.2
  81.2 5.9 %collective-permute-start.6 = (bf16[1,32,256]{2,1,0:T(8,128)(2,1)S(1)}, bf16[1,32,256]{2,1,0:T(8,128)(2,1)S(1)}, u32[]{:S(2)}, u32[]{:S(2)}) collective-permute-start(bf16[1,32,256]{2,1,0:T(8,128)(2,1)S(1)} %get-tuple-element.62), channel_id=1, source_target_pairs={{0,32},{32,64},{64,96},{1,33},{33,65},{65,97},{2,34},{34,66},{66,9... | collective-permute-start | bytes 49160 | tf_op jit(solution)/shard_map/ppermute | solution.py:30
  87.1 1.9 collective-permute-start.7
  89.1 5.8 %merge_gradient.3 = (f32[11520,128]{1,0:T(8,128)}, bf16[11520,128]{1,0:T(8,128)(2,1)}) custom-call(bf16[5,3,34,32,256]{4,3,2,1,0:T(8,128)(2,1)} %get-tuple-element.33.stacked_ref, bf16[1024,256]{1,0:T(8,128)(2,1)} %get-tuple-element.34.back_ref), custom_call_target="tpu_custom_call" | custom-call | flops 2013265920 | bytes 8000000 | tf_op jit(solution)/shard_map/merge_gradient/pallas_call | solution.py:166
  94.9 4.1 %collective-permute-start.8 = (bf16[34,1,256]{2,1,0:T(2,128)(2,1)S(1)}, bf16[34,1,256]{2,1,0:T(2,128)(2,1)S(1)}, u32[]{:S(2)}, u32[]{:S(2)}) collective-permute-start(bf16[34,1,256]{2,1,0:T(2,128)(2,1)S(1)} %get-tuple-element.60), channel_id=1, source_target_pairs={{0,1},{1,2},{2,3},{3,4},{4,5},{5,6},{6,7},{7,8},{8,9},{9,10},{10,1... | collective-permute-start | bytes 52232 | tf_op jit(solution)/shard_map/ppermute | solution.py:30
  99.0 1.3 collective-permute-start.9
  100.3 5.7 %merge_gradient.4 = (f32[11520,128]{1,0:T(8,128)}, bf16[11520,128]{1,0:T(8,128)(2,1)}) custom-call(bf16[5,3,34,32,256]{4,3,2,1,0:T(8,128)(2,1)} %get-tuple-element.33.stacked_ref, bf16[1024,256]{1,0:T(8,128)(2,1)} %get-tuple-element.34.back_ref, f32[11520,128]{1,0:T(8,128)} %get-tuple-element.35.refs_0_, ...), custom_call_target="tpu_custom_call", output_to_operand_aliasing={{0}: (2, {}), {1}: (3, {})} | custom-call | flops 2013265920 | bytes 8000000 | tf_op jit(solution)/shard_map/merge_gradient/pallas_call | solution.py:166
  106.0 5.7 %merge_gradient.5 = (f32[11520,128]{1,0:T(8,128)}, bf16[11520,128]{1,0:T(8,128)(2,1)}) custom-call(bf16[5,3,34,32,256]{4,3,2,1,0:T(8,128)(2,1)} %get-tuple-element.33.stacked_ref, bf16[1024,256]{1,0:T(8,128)(2,1)} %get-tuple-element.34.back_ref, f32[11520,128]{1,0:T(8,128)} %get-tuple-element.37.refs_0_, ...), custom_call_target="tpu_custom_call", output_to_operand_aliasing={{0}: (2, {}), {1}: (3, {})} | custom-call | flops 2013265920 | bytes 8000000 | tf_op jit(solution)/shard_map/merge_gradient/pallas_call | solution.py:166
  111.7 1.4 maximum_convert_fusion.2.hidden_ref
  113.1 6.4 %out_step.1 = (bf16[32,32,256]{2,1,0:T(8,128)(2,1)}, f32[2304,128]{1,0:T(8,128)}, bf16[2304,128]{1,0:T(8,128)(2,1)}) custom-call(s32[1]{0:T(128)} %bitcast.core_ref, f32[34,34,256]{2,1,0:T(8,128)} %maximum_convert_fusion.2.hidden_ref, bf16[32,32,256]{2,1,0:T(8,128)(2,1)} %current_ref.1, bf16[32,32,256]{2,1,0:T(8,128)(2,1)} %cotangent_ref.1, ...), custom_call_target="tpu_custom_call" | custom-call | flops 2415919104 | bytes 8000000 | tf_op jit(solution)/shard_map/out_step/pallas_call | solution.py:225
  119.5 0.5 collective-permute-start.11
  120.0 1.8 collective-permute-done.11.got_b
  121.9 0.8 copy-done.5
  122.7 1.0 copy-done.2
  123.7 7.2 %pair_sums.1 = bf16[13824,128]{1,0:T(8,128)(2,1)} custom-call(f32[11520,128]{1,0:T(8,128)} %get-tuple-element.39.keep_a, bf16[11520,128]{1,0:T(8,128)(2,1)} %copy-done.2, f32[2304,128]{1,0:T(8,128)} %get-tuple-element.41.keep_b, bf16[2304,128]{1,0:T(8,128)(2,1)} %copy-done.5), custom_call_target="tpu_custom_call" | custom-call | tf_op jit(solution)/shard_map/pair_sums/pallas_call | solution.py:276
  130.9 62.7 %all_to_all.10 = bf16[64,216,128]{2,1,0:T(8,128)(2,1)S(1)} all-to-all(bf16[64,216,128]{2,1,0:T(8,128)(2,1)} %bitcast.62), channel_id=1, replica_groups=mesh['xh'=2,'core'=2,'xl'=2,'z'=4,'y'=4] {'xh','xl','z','y'}, dimensions={0} | all-to-all | bytes 7077888 | tf_op jit(solution)/shard_map/all_to_all | solution.py:374
  193.6 1.1 reduce_sum.12
  194.8 1.3 broadcast_in_dim.2
  196.0 50.7 %all_to_all.11 = bf16[64,216,128]{2,1,0:T(8,128)(2,1)S(1)} all-to-all(bf16[64,216,128]{2,1,0:T(8,128)(2,1)S(1)} %broadcast_in_dim.2), channel_id=1, replica_groups=mesh['xh'=2,'core'=2,'xl'=2,'z'=4,'y'=4] {'xh','xl','z','y'}, dimensions={0} | all-to-all | bytes 7077888 | tf_op jit(solution)/shard_map/all_to_all | solution.py:377
  246.7 3.4 %collective-permute-start.12 = (bf16[13824,128]{1,0:T(8,128)(2,1)S(1)}, bf16[13824,128]{1,0:T(8,128)(2,1)}, u32[]{:S(2)}, u32[]{:S(2)}) collective-permute-start(bf16[13824,128]{1,0:T(8,128)(2,1)S(1)} %bitcast.63), channel_id=1, source_target_pairs={{0,32},{32,0},{1,33},{33,1},{2,34},{34,2},{3,35},{35,3},{4,36},{36... | collective-permute-start | bytes 10616840 | tf_op jit(solution)/shard_map/ppermute | solution.py:378
  250.2 6.0 %collective-permute-done.12 = bf16[13824,128]{1,0:T(8,128)(2,1)} collective-permute-done((bf16[13824,128]{1,0:T(8,128)(2,1)S(1)}, bf16[13824,128]{1,0:T(8,128)(2,1)}, u32[]{:S(2)}, u32[]{:S(2)}) %collective-permute-start.12) | collective-permute-done | bytes 3538976 | tf_op jit(solution)/shard_map/ppermute | solution.py:378
  256.1 1.1 broadcast_select_fusion.3
  257.3 1.6 maximum_convert_fusion.1
  258.9 2.0 broadcast_select_fusion.1
  260.9 5.4 %maximum_convert_fusion = f32[3,3,1280,256]{3,2,1,0:T(8,128)} fusion(bf16[3,3,1280,128]{3,2,1,0:T(8,128)(2,1)S(1)} %bitcast.67, bf16[3,3,1280,128]{3,2,1,0:T(8,128)(2,1)S(1)} %bitcast.66), kind=kLoop, calls=%fused_computation | loop fusion | flops 11796480 | bytes 17694720 | tf_op jit(solution)/shard_map/convert_element_type | solution.py:384
  (37 shorter events, 0.4 us)
Async XLA Ops:
  1.5 2.8 %copy-start.1 = (bf16[32,32,256]{2,1,0:T(8,128)(2,1)S(1)}, bf16[32,32,256]{2,1,0:T(8,128)(2,1)}, u32[]{:S(2)}) copy-start(bf16[32,32,256]{2,1,0:T(8,128)(2,1)} %current_ref.1) | copy-start | bytes 1572868
  1.5 2.8 %copy-start = (bf16[32,32,256]{2,1,0:T(8,128)(2,1)S(1)}, bf16[32,32,256]{2,1,0:T(8,128)(2,1)}, u32[]{:S(2)}) copy-start(bf16[32,32,256]{2,1,0:T(8,128)(2,1)} %cotangent_ref.1) | copy-start | bytes 1572868
  3.5 0.8 copy-start.4
  5.3 13.4 %copy-start.7 = (s32[4,2]{0,1:T(2,128)S(1)}, s32[4,2]{0,1:T(2,128)}, u32[]{:S(2)}) copy-start(s32[4,2]{0,1:T(2,128)} %param.10) | copy-start | bytes 100
  5.3 20.0 %collective-permute-start = (bf16[36,32,256]{2,1,0:T(8,128)(2,1)}, bf16[36,32,256]{2,1,0:T(8,128)(2,1)}, u32[]{:S(2)}, u32[]{:S(2)}) collective-permute-start(bf16[36,32,256]{2,1,0:T(8,128)(2,1)} %pad_maximum_fusion.2), channel_id=1, source_target_pairs={{0,32},{32,64},{64,96},{1,33},{33,65},{65,97},{2,34},{34,66},{66,9... | collective-permute-start | bytes 1769480 | tf_op jit(solution)/shard_map/ppermute | solution.py:30
  11.5 13.8 %collective-permute-start.1 = (bf16[2,32,256]{2,1,0:T(8,128)(2,1)S(1)}, bf16[2,32,256]{2,1,0:T(8,128)(2,1)S(1)}, u32[]{:S(2)}, u32[]{:S(2)}) collective-permute-start(bf16[2,32,256]{2,1,0:T(8,128)(2,1)S(1)} %pad_maximum_fusion.10), channel_id=1, source_target_pairs={{32,0},{64,32},{96,64},{33,1},{65,33},{97,65},{34,2},{66,34},{98,6... | collective-permute-start | bytes 98312 | tf_op jit(solution)/shard_map/ppermute | solution.py:30
  14.4 26.5 %collective-permute-start.3 = (bf16[64,32,256]{2,1,0:T(8,128)(2,1)}, bf16[64,32,256]{2,1,0:T(8,128)(2,1)}, u32[]{:S(2)}, u32[]{:S(2)}) collective-permute-start(bf16[64,32,256]{2,1,0:T(8,128)(2,1)} %pad_maximum_fusion.1), channel_id=1, source_target_pairs={{0,1},{1,2},{2,3},{3,4},{4,5},{5,6},{6,7},{7,8},{8,9},{9,10},{10,1... | collective-permute-start | bytes 3145736 | tf_op jit(solution)/shard_map/ppermute | solution.py:30
  26.0 7.5 %collective-permute-start.4 = (bf16[34,2,256]{2,1,0:T(2,128)(2,1)S(1)}, bf16[34,2,256]{2,1,0:T(2,128)(2,1)S(1)}, u32[]{:S(2)}, u32[]{:S(2)}) collective-permute-start(bf16[34,2,256]{2,1,0:T(2,128)(2,1)S(1)} %fusion.39), channel_id=1, source_target_pairs={{1,0},{2,1},{3,2},{4,3},{5,4},{6,5},{7,6},{8,7},{9,8},{10,9},{11,1... | collective-permute-start | bytes 104456 | tf_op jit(solution)/shard_map/ppermute | solution.py:30
  29.5 24.0 %collective-permute-start.2 = (bf16[34,37,256]{2,1,0:T(8,128)(2,1)S(1)}, bf16[34,37,256]{2,1,0:T(8,128)(2,1)S(1)}, u32[]{:S(2)}, u32[]{:S(2)}) collective-permute-start(bf16[34,37,256]{2,1,0:T(8,128)(2,1)S(1)} %fusion.13), channel_id=1, source_target_pairs={{0,1},{1,2},{2,3},{3,4},{4,5},{5,6},{6,7},{7,8},{8,9},{9,10},{10,1... | collective-permute-start | bytes 1932296 | tf_op jit(solution)/shard_map/ppermute | solution.py:30
  43.8 18.4 %collective-permute-start.5 = (bf16[62,34,256]{2,0,1:T(8,128)(2,1)S(1)}, bf16[62,34,256]{2,0,1:T(8,128)(2,1)S(1)}, u32[]{:S(2)}, u32[]{:S(2)}) collective-permute-start(bf16[62,34,256]{2,0,1:T(8,128)(2,1)S(1)} %copy.14), channel_id=1, source_target_pairs={{0,32},{32,64},{64,96},{1,33},{33,65},{65,97},{2,34},{34,66},{66,9... | collective-permute-start | bytes 3237896 | tf_op jit(solution)/shard_map/ppermute | solution.py:30
  64.5 2.0 copy-start.6
  81.2 13.6 %collective-permute-start.6 = (bf16[1,32,256]{2,1,0:T(8,128)(2,1)S(1)}, bf16[1,32,256]{2,1,0:T(8,128)(2,1)S(1)}, u32[]{:S(2)}, u32[]{:S(2)}) collective-permute-start(bf16[1,32,256]{2,1,0:T(8,128)(2,1)S(1)} %get-tuple-element.62), channel_id=1, source_target_pairs={{0,32},{32,64},{64,96},{1,33},{33,65},{65,97},{2,34},{34,66},{66,9... | collective-permute-start | bytes 49160 | tf_op jit(solution)/shard_map/ppermute | solution.py:30
  87.1 7.7 %collective-permute-start.7 = (bf16[1,32,256]{2,1,0:T(8,128)(2,1)S(1)}, bf16[1,32,256]{2,1,0:T(8,128)(2,1)S(1)}, u32[]{:S(2)}, u32[]{:S(2)}) collective-permute-start(bf16[1,32,256]{2,1,0:T(8,128)(2,1)S(1)} %get-tuple-element.61), channel_id=1, source_target_pairs={{32,0},{64,32},{96,64},{33,1},{65,33},{97,65},{34,2},{66,34},{98,6... | collective-permute-start | bytes 49160 | tf_op jit(solution)/shard_map/ppermute | solution.py:30
  89.1 5.8 %copy-start.3 = (bf16[1024,256]{1,0:T(8,128)(2,1)S(1)}, bf16[1024,256]{1,0:T(8,128)(2,1)}, u32[]{:S(2)}) copy-start(bf16[1024,256]{1,0:T(8,128)(2,1)} %get-tuple-element.26) | copy-start | bytes 1572868
  94.9 11.1 %collective-permute-start.8 = (bf16[34,1,256]{2,1,0:T(2,128)(2,1)S(1)}, bf16[34,1,256]{2,1,0:T(2,128)(2,1)S(1)}, u32[]{:S(2)}, u32[]{:S(2)}) collective-permute-start(bf16[34,1,256]{2,1,0:T(2,128)(2,1)S(1)} %get-tuple-element.60), channel_id=1, source_target_pairs={{0,1},{1,2},{2,3},{3,4},{4,5},{5,6},{6,7},{7,8},{8,9},{9,10},{10,1... | collective-permute-start | bytes 52232 | tf_op jit(solution)/shard_map/ppermute | solution.py:30
  99.0 7.0 %collective-permute-start.9 = (bf16[34,1,256]{2,1,0:T(2,128)(2,1)S(1)}, bf16[34,1,256]{2,1,0:T(2,128)(2,1)S(1)}, u32[]{:S(2)}, u32[]{:S(2)}) collective-permute-start(bf16[34,1,256]{2,1,0:T(2,128)(2,1)S(1)} %get-tuple-element.59), channel_id=1, source_target_pairs={{1,0},{2,1},{3,2},{4,3},{5,4},{6,5},{7,6},{8,7},{9,8},{10,9},{11,1... | collective-permute-start | bytes 52232 | tf_op jit(solution)/shard_map/ppermute | solution.py:30
  111.7 10.1 %collective-permute-start.10 = (bf16[11520,128]{1,0:T(8,128)(2,1)}, bf16[11520,128]{1,0:T(8,128)(2,1)S(1)}, u32[]{:S(2)}, u32[]{:S(2)}) collective-permute-start(bf16[11520,128]{1,0:T(8,128)(2,1)} %get-tuple-element.40), channel_id=1, source_target_pairs={{0,32},{32,0},{1,33},{33,1},{2,34},{34,2},{3,35},{35,3},{4,36},{36... | collective-permute-start | bytes 8847368 | tf_op jit(solution)/shard_map/ppermute | solution.py:364
  119.5 2.3 collective-permute-start.11
  121.9 0.8 copy-start.5
  121.9 1.8 copy-start.2
  246.7 9.4 %collective-permute-start.12 = (bf16[13824,128]{1,0:T(8,128)(2,1)S(1)}, bf16[13824,128]{1,0:T(8,128)(2,1)}, u32[]{:S(2)}, u32[]{:S(2)}) collective-permute-start(bf16[13824,128]{1,0:T(8,128)(2,1)S(1)} %bitcast.63), channel_id=1, source_target_pairs={{0,32},{32,0},{1,33},{33,1},{2,34},{34,2},{3,35},{35,3},{4,36},{36... | collective-permute-start | bytes 10616840 | tf_op jit(solution)/shard_map/ppermute | solution.py:378

commit v3 on v2

v3 whole, which is shorter than its diff:
```python
import functools

import jax
import jax.numpy as jnp
from jax import lax
from jax.experimental import pallas as pl
from jax.experimental.pallas import tpu as pltpu
from jax.sharding import Mesh, PartitionSpec as P

CHIPS = ("xh", "xl", "z", "y")
ROW = ("xh", "core")
COL = ("xl", "z", "y")
BF16 = jnp.bfloat16
F32 = jnp.float32
SWAP = [(0, 1), (1, 0)]


def work(products, moved_bytes):
    return pl.CostEstimate(flops=2 * products, transcendentals=0, bytes_accessed=moved_bytes)


PARAMS = pltpu.CompilerParams(
    dimension_semantics=("arbitrary",), vmem_limit_bytes=56 * 1024 * 1024
)
WHOLE = pl.BlockSpec(memory_space=pltpu.VMEM)


def moved(x, axis, by):
    peers = lax.axis_size(axis)
    return lax.ppermute(x, axis, [(i, i + by) for i in range(peers) if 0 <= i + by < peers])


def shift_row(source, at, target):
    cols = target.shape[2]
    value = source[at]
    wide = value.astype(F32)
    target[0, at[-1]] = value[:cols]
    for col_step in (1, 2):
        target[col_step, at[-1]] = wide[col_step : col_step + cols].astype(BF16)


def forward_kernel(joined_ref, weight_ref, out_weight_ref, hidden_ref, back_ref, even, odd, total,
                   back_total):
    step = pl.program_id(0)
    steps = pl.num_programs(0)
    _, rows, cols, width = even.shape
    tile = rows - 2

    def taps(now, before, shifting, multiply):
        def tap(t, carry):
            if multiply is not None:
                multiply(t, before)
            if shifting:
                for more in range(4):
                    shift_row(joined_ref, (0, jnp.minimum(4 * t + more, rows - 1)), now)
            return carry

        lax.fori_loop(0, 9, tap, 0, unroll=True)

    def forward_tap(t, before):
        window = before[t % 3, pl.ds(t // 3, tile)].reshape(tile * cols, width)
        total[...] += jnp.dot(window, weight_ref[t], preferred_element_type=F32)

    def back_tap(t, before):
        window = before[2 - t % 3, pl.ds(2 - t // 3, tile)].reshape(tile * cols, width)
        back_total[...] += lax.dot_general(
            window, out_weight_ref[t], (((1,), (1,)), ((), ())), preferred_element_type=F32
        )

    @pl.when(step == 0)
    def _():
        total[...] = jnp.zeros_like(total)
        back_total[...] = jnp.zeros_like(back_total)
        taps(even, odd, True, None)

    @pl.when(step == 1)
    def _():
        taps(odd, even, True, back_tap)

    @pl.when((step > 1) & (step < steps - 1) & (step % 2 == 0))
    def _():
        taps(even, odd, True, forward_tap)

    @pl.when((step > 1) & (step < steps - 1) & (step % 2 == 1))
    def _():
        taps(odd, even, True, forward_tap)

    @pl.when(step == steps - 1)
    def _():
        taps(even, odd, False, forward_tap)
        pre = total[...]
        sigma = jax.nn.sigmoid(pre)
        hidden_ref[...] = (pre * sigma).astype(BF16)
        back = back_total[...] * (sigma * (1.0 + pre * (1.0 - sigma)))
        back_ref[...] = back.astype(BF16)


def forward(joined, merge_weight, out_weight):
    layers, rows, wide_cols, width = joined.shape
    cols = wide_cols - 2
    frames = layers - 1
    cells = (rows - 2) * cols
    return pl.pallas_call(
        forward_kernel,
        grid=(layers + 1,),
        in_specs=[
            pl.BlockSpec((1,) + joined.shape[1:], lambda i: (jnp.minimum(i, frames), 0, 0, 0)),
            pl.BlockSpec((9, width, width), lambda i: (0, jnp.maximum(i - 2, 0), 0)),
            pl.BlockSpec((9, width, width), lambda i: (0, 0, 0)),
        ],
        out_specs=[
            pl.BlockSpec((cells, width), lambda i: (0, 0)),
            pl.BlockSpec((cells, width), lambda i: (0, 0)),
        ],
        out_shape=[
            jax.ShapeDtypeStruct((cells, width), BF16),
            jax.ShapeDtypeStruct((cells, width), BF16),
        ],
        scratch_shapes=[
            pltpu.VMEM((3, rows, cols, width), BF16),
            pltpu.VMEM((3, rows, cols, width), BF16),
            pltpu.VMEM((cells, width), F32),
            pltpu.VMEM((cells, width), F32),
        ],
        compiler_params=PARAMS,
        cost_estimate=work(9 * cells * width * width * layers, 25_000_000),
        name="forward",
    )(joined, merge_weight, out_weight)


def layer_kernel(at_ref, own_ref, other_ref, own_right, other_right, *refs):
    out_ref, own_copies, other_copies, held = refs[-4:]
    _, rows, cols, width = own_copies.shape
    tile, half = rows - 2, width // 2

    def product(copies, tap, right):
        window = copies[tap % 3, tap // 3 : tap // 3 + tile].reshape(tile * cols, width)
        return lax.dot_general(
            window, right[...], (((0,), (0,)), ((), ())), preferred_element_type=F32
        )

    for row in range(rows):
        shift_row(own_ref, (0, row), own_copies)
    for tap in range(9):
        held[tap] = product(own_copies, tap, own_right)
        for row in range(4 * tap, min(4 * tap + 4, rows)):
            shift_row(other_ref, (0, row), other_copies)
    for tap in range(9):
        value = held[tap] + product(other_copies, tap, other_right)
        for side in range(2):
            part = value[:, side * half : (side + 1) * half]
            out_ref[0, side, tap * width : (tap + 1) * width] = part.astype(BF16)


def layer_gradient(place, at, own, other, own_right, other_right, into=()):
    _, rows, wide_cols, width = own.shape
    cols = wide_cols - 2
    shape = (3, 2, 9 * width, width // 2)
    window = (1,) + own.shape[1:]
    right = pl.BlockSpec(own_right.shape, lambda i, at: (0, 0))
    return pl.pallas_call(
        layer_kernel,
        grid_spec=pltpu.PrefetchScalarGridSpec(
            num_scalar_prefetch=1,
            grid=(1,),
            in_specs=[
                pl.BlockSpec(window, lambda i, at: (at[0], 0, 0, 0)),
                pl.BlockSpec(window, lambda i, at: (at[1], 0, 0, 0)),
                right,
                right,
            ]
            + [pl.BlockSpec(memory_space=pl.ANY)] * len(into),
            out_specs=pl.BlockSpec((1,) + shape[1:], lambda i, at: (place, 0, 0, 0)),
            scratch_shapes=[
                pltpu.VMEM((3, rows, cols, width), BF16),
                pltpu.VMEM((3, rows, cols, width), BF16),
                pltpu.VMEM((9, width, width), F32),
            ],
        ),
        out_shape=jax.ShapeDtypeStruct(shape, BF16),
        input_output_aliases={5: 0} if into else {},
        compiler_params=PARAMS,
        cost_estimate=work(18 * own_right.shape[0] * width * width, 5_000_000),
        name="layer_gradient",
    )(at, own, other, own_right, other_right, *into)


def merged_kernel(hidden_ref, current_ref, weight_ref, merged_ref, copies, total):
    _, rows, cols, width = copies.shape
    tile = rows - 2
    for row in range(rows):
        shift_row(hidden_ref, (row,), copies)
    total[...] = current_ref[...].reshape(tile * cols, width).astype(F32)
    for tap in range(9):
        window = copies[tap % 3, tap // 3 : tap // 3 + tile].reshape(tile * cols, width)
        total[...] += jnp.dot(window, weight_ref[tap], preferred_element_type=F32)
    merged_ref[...] = total[...].astype(BF16).reshape(merged_ref.shape)


def merged_step(hidden_pad, current, out_weight):
    tile, cols, width = current.shape
    whole = [pl.BlockSpec(x.shape, lambda i: (0, 0, 0)) for x in (hidden_pad, current, out_weight)]
    return pl.pallas_call(
        merged_kernel,
        grid=(1,),
        in_specs=whole,
        out_specs=whole[1],
        out_shape=jax.ShapeDtypeStruct(current.shape, BF16),
        scratch_shapes=[
            pltpu.VMEM((3, tile + 2, cols, width), BF16),
            pltpu.VMEM((tile * cols, width), F32),
        ],
        compiler_params=PARAMS,
        cost_estimate=work(9 * tile * cols * width * width, 4_000_000),
        name="merged_step",
    )(hidden_pad, current, out_weight)


def final_kernel(base_ref, sums_ref, *refs):
    out_ref = refs[-1]
    taps, width, _ = out_ref.shape
    half = sums_ref.shape[-1]

    @pl.when(base_ref[0] + pl.program_id(0) < 5)
    def _():
        for side in range(2):
            part = sums_ref[0, side].reshape(taps, width, half)
            out_ref[:, :, side * half : (side + 1) * half] = part.astype(F32)


def final(base, sums, into=()):
    width = 2 * sums.shape[-1]
    return pl.pallas_call(
        final_kernel,
        grid_spec=pltpu.PrefetchScalarGridSpec(
            num_scalar_prefetch=1,
            grid=(3,),
            in_specs=[pl.BlockSpec((1,) + sums.shape[1:], lambda i, at: (i, 0, 0, 0))]
            + [pl.BlockSpec(memory_space=pl.ANY)] * len(into),
            out_specs=pl.BlockSpec(
                (9, width, width), lambda i, at: (0, jnp.minimum(at[0] + i, 4), 0)
            ),
        ),
        out_shape=jax.ShapeDtypeStruct((9, 5 * width, width), F32),
        input_output_aliases={2: 0} if into else {},
        compiler_params=PARAMS,
        cost_estimate=work(0, 12_000_000),
        name="final",
    )(base, sums, *into)


def shards(current, history, validity, offsets, merge_weight, out_weight, cotangent):
    tile, cols, width = current.shape
    frames = history.shape[0]
    ext = tile + 2
    core = lax.axis_index("core").astype(jnp.int32).reshape(1)
    valid = validity.astype(BF16)[..., None]
    masked12 = history[1:3] * valid[1:3]
    masked12, valid = lax.optimization_barrier((masked12, valid))
    masked = [history[0] * valid[0], masked12[0], masked12[1], history[3] * valid[3]]

    row_last = lax.axis_index(ROW) == lax.axis_size(ROW) - 1
    col_last = lax.axis_index(COL) == lax.axis_size(COL) - 1
    row_inside = (jnp.arange(ext) < ext - 1) | ~row_last
    ext_cols = cols + 2
    col_inside = (jnp.arange(ext_cols) < ext_cols - 1) | ~col_last
    inside = (row_inside[:, None] & col_inside[None, :]).astype(BF16)[..., None]

    left12 = moved(masked12, COL, 1)
    packed = moved(
        jnp.concatenate([masked[3][1:], masked[0][-3:], current[-1:], cotangent[-1:]], axis=0), ROW, 1
    )
    below = moved(jnp.concatenate([current[:1], cotangent[:1]], axis=0), ROW, -1)
    above3, above0 = packed[: tile - 1], packed[tile - 1 : tile + 2]
    near3 = jnp.concatenate([above3, masked[3][:3]], axis=0)
    near0 = jnp.concatenate([above0, masked[0][: tile - 1]], axis=0)
    now = jnp.concatenate([packed[tile + 2 : tile + 3], current, below[:1]], axis=0)
    cot = jnp.concatenate([packed[tile + 3 :], cotangent, below[1:]], axis=0)
    side = moved(
        jnp.concatenate([near3, near0[:, -3:], now[:, -1:], cot[:, -1:]], axis=1), COL, 1
    )
    right = moved(jnp.concatenate([now[:, :1], cot[:, :1]], axis=1), COL, -1)

    left12, right = lax.optimization_barrier((left12, right))

    def cols_of(k):
        wide = jnp.concatenate([left12[k - 1], masked[k]], axis=1)
        start = cols - 1 - offsets[k, 1]
        return lax.dynamic_slice(wide, (jnp.int32(0), start, jnp.int32(0)), (tile, ext_cols, width))

    wide1, wide2 = cols_of(1), cols_of(2)
    above12 = moved(jnp.concatenate([wide1[1:], wide2[1:]], axis=0), ROW, 1)

    def rows_of(above, wide, k):
        both = jnp.concatenate([above, wide], axis=0)
        start = tile - 2 - offsets[k, 0]
        return lax.dynamic_slice(both, (start, jnp.int32(0), jnp.int32(0)), (ext, ext_cols, width)) * inside

    joined = jnp.stack(
        [
            jnp.concatenate([side[:, cols + 4 :], cot, right[:, 1:]], axis=1),
            jnp.concatenate([side[:, cols + 3 : cols + 4], now, right[:, :1]], axis=1),
            jnp.concatenate([side[:, cols : cols + 3], near0[:, : cols - 1]], axis=1) * inside,
            rows_of(above12[: tile - 1], wide1, 1),
            rows_of(above12[tile - 1 :], wide2, 2),
            jnp.concatenate([side[:, 1:cols], near3[:, :3]], axis=1) * inside,
        ]
    )
    hidden, back_pre = forward(
        joined, merge_weight.reshape(9, -1, width), out_weight.reshape(9, width, width)
    )
    first = core[0] == 0

    def swapped(x):
        return lax.ppermute(x, "core", SWAP)

    flat_cot = cotangent.reshape(tile * cols, width)
    other_two = swapped(jnp.where(first, joined[4:6], joined[1:3]))

    hidden = hidden.reshape(tile, cols, width)
    hidden_above = moved(hidden[-1:], ROW, 1)
    hidden_below = moved(hidden[:1], ROW, -1)
    other_back = swapped(back_pre)
    at = jnp.concatenate([3 * core + 1, jnp.zeros((1,), jnp.int32)])
    sums = layer_gradient(0, at, joined, other_two, back_pre, other_back)
    sums, hidden_above, hidden_below, flat_cot = lax.optimization_barrier(
        (sums, hidden_above, hidden_below, flat_cot)
    )
    other_cot = swapped(flat_cot)
    hidden_pad = jnp.concatenate([hidden_above, hidden, hidden_below], axis=0)
    hidden_left = moved(hidden_pad[:, -1:], COL, 1)
    hidden_right = moved(hidden_pad[:, :1], COL, -1)
    sums = layer_gradient(1, at + 1, joined, other_two, back_pre, other_back, (sums,))
    sums, hidden_left, hidden_right = lax.optimization_barrier((sums, hidden_left, hidden_right))
    hidden_pad = jnp.concatenate([hidden_left, hidden_pad, hidden_right], axis=1)
    own_third = jnp.where(first, joined[3], hidden_pad)
    other_third = swapped(jnp.where(first, hidden_pad, joined[3]))
    sums = layer_gradient(
        2,
        jnp.zeros((2,), jnp.int32),
        own_third[None],
        other_third[None],
        jnp.where(first, back_pre, flat_cot),
        jnp.where(first, other_back, other_cot),
        (sums,),
    )
    merged = merged_step(hidden_pad, current, out_weight.reshape(9, width, width))

    chips = lax.axis_size(CHIPS)
    half = width // 2
    blocks = sums.reshape(chips, -1, half)
    got = lax.all_to_all(blocks, CHIPS, split_axis=0, concat_axis=0)
    got, merged = lax.optimization_barrier((got, merged))
    share = jnp.sum(got.astype(F32), axis=0).astype(BF16)
    spread = jnp.broadcast_to(share[None], blocks.shape)
    own = lax.all_to_all(spread, CHIPS, split_axis=0, concat_axis=0).reshape(sums.shape)
    other = swapped(own)
    merge_grad = final(3 * (1 - core), other, (final(3 * core, own),))
    merge_grad = merge_grad.reshape(merge_weight.shape)
    third = jnp.where(first, other[2], own[2])
    out_grad = jnp.concatenate([third[0], third[1]], axis=1).astype(F32).reshape(out_weight.shape)
    return (merged, merge_grad, out_grad)


def solution(mesh):
    parts = Mesh(mesh.devices.reshape(2, 2, 2, 4, 4), ("xh", "core", "xl", "z", "y"))
    return jax.shard_map(
        shards,
        mesh=parts,
        in_specs=(
            P(ROW, COL, None),
            P(None, ROW, COL, None),
            P(None, ROW, COL),
            P(),
            P(),
            P(),
            P(ROW, COL, None),
        ),
        out_specs=(P(ROW, COL, None), P(), P()),
        check_vma=False,
    )
```

time: 268 us -> 267 us (level)
  blocking collectives: 113 us -> 57.3 us
  waiting for transfers between devices: 26 us -> 58.2 us
  starting transfers between devices: 40.9 us -> 62.9 us
  local copies, waits for them, and re-layouts: 13.9 us -> 18.5 us
  other arithmetic: 21.5 us -> 18.4 us
    all_to_all x2 -> x1, blocking collectives: 113 us -> 57.3 us  [shards(): lax.all_to_all(spread, CHIPS, split_axis=0, concat_axis=0)]
    all_to_all x0 -> x1, waiting for transfers between devices: none -> 40.9 us  [shards(): got = lax.all_to_all(blocks, CHIPS, split_axis=0, concat_axis=0)]
    all_to_all x0 -> x1, starting transfers between devices: none -> 23.8 us  [shards(): got = lax.all_to_all(blocks, CHIPS, split_axis=0, concat_axis=0)]
    ppermute x3 -> x5, waiting for transfers between devices: 7.82 us -> 1.01 us  [swapped(): return lax.ppermute(x, 'core', SWAP)]
    convert_element_type x3 -> x1, other arithmetic: 8.28 us -> 1.57 us  [shards(): jnp.concatenate([third[0], third[1]], axis=1).astype(F32)]
    select_n x2 -> x5, other arithmetic: 3.17 us -> 5.42 us  [the longest x1 1.75 us: shards(): third = jnp.where(first, other[2], own[2])]
    pallas_call x5 -> x6, Pallas kernels: 30.8 us -> 32.1 us  [the longest x3 18 us: layer_gradient(): pl.pallas_call(layer_kernel, grid_spec=pltpu.PrefetchScalarGridSpec(num_s...]
  transfers between devices with their start and end apart: 13 -> 16, of which waited for: 5 -> 6; matrix products, arithmetic and copies ran while one was open for 4% -> 9% of each run, Pallas kernels for 7% -> 12%
where the time goes in v3:
time: 267 us; the launch traced here: 266 us
  starting transfers between devices  62.9 us (24%)
  waiting for transfers between devices  58.2 us (22%)
  blocking collectives  57.3 us (21%)
  Pallas kernels  44.3 us (17%)
  local copies, waits for them, and re-layouts  18.5 us (7%)
  other arithmetic  18.4 us (7%)
  between operations  6 us (2%)
    all_to_all x1, blocking collectives, shards(): lax.all_to_all(spread, CHIPS, split_axis=0, concat_axis=0)  57.3 us
    all_to_all x1, waiting for transfers between devices, shards(): got = lax.all_to_all(blocks, CHIPS, split_axis=0, concat_axis=0)  40.9 us
    ppermute x10, starting transfers between devices, moved(): lax.ppermute(x, axis, [(i, i + by) for i in range(peers) if 0 <= i + by <...  34.9 us
    all_to_all x1, starting transfers between devices, shards(): got = lax.all_to_all(blocks, CHIPS, split_axis=0, concat_axis=0)  23.8 us
    pallas_call x3, Pallas kernels, layer_gradient(): pl.pallas_call(layer_kernel, grid_spec=pltpu.PrefetchScalarGridSpec(num_s...  18 us
    ppermute x10, waiting for transfers between devices, moved(): lax.ppermute(x, axis, [(i, i + by) for i in range(peers) if 0 <= i + by <...  16.4 us
    pallas_call x1, Pallas kernels, forward(): pl.pallas_call(forward_kernel, grid=(layers + 1,), in_specs=[pl.BlockSpec...  12.2 us
    pallas_call x2, Pallas kernels, final(): pl.pallas_call(final_kernel, grid_spec=pltpu.PrefetchScalarGridSpec(num_s...  10.3 us
  transfers between devices with their start and end apart: 16, of which 6 were waited for; matrix products, arithmetic and copies ran while one was open for 9% of the time, Pallas kernels for 12%

profile of v3, /device:TPU:1, one launch (start us, length us, event | category | flops | bytes accessed | tf_op | source)
XLA Modules:
  0.0 265.5 jit_solution(17565791235326856696)
XLA Ops:
  0.6 0.9 fusion.40
  1.6 3.3 %collective-permute-start.2 = (bf16[2,32,256]{2,1,0:T(8,128)(2,1)S(1)}, bf16[2,32,256]{2,1,0:T(8,128)(2,1)S(1)}, u32[]{:S(2)}, u32[]{:S(2)}) collective-permute-start(bf16[2,32,256]{2,1,0:T(8,128)(2,1)S(1)} %pad_maximum_fusion.10), channel_id=1, source_target_pairs={{32,0},{64,32},{96,64},{33,1},{65,33},{97,65},{34,2},{66,34},{98,6... | collective-permute-start | bytes 98312 | tf_op jit(solution)/shard_map/ppermute | solution.py:30
  4.9 0.8 convert_bitcast_fusion
  5.8 0.8 convert_element_type.16
  6.6 1.6 slice_multiply_fusion
  8.2 0.3 bitcast_multiply_fusion.1
  8.6 0.9 pad_maximum_fusion.2
  9.5 4.6 %collective-permute-start.1 = (bf16[36,32,256]{2,1,0:T(8,128)(2,1)}, bf16[36,32,256]{2,1,0:T(8,128)(2,1)}, u32[]{:S(2)}, u32[]{:S(2)}) collective-permute-start(bf16[36,32,256]{2,1,0:T(8,128)(2,1)} %pad_maximum_fusion.2), channel_id=1, source_target_pairs={{0,32},{32,64},{64,96},{1,33},{33,65},{65,97},{2,34},{34,66},{66,9... | collective-permute-start | bytes 1769480 | tf_op jit(solution)/shard_map/ppermute | solution.py:30
  14.2 4.2 %collective-permute-start = (bf16[2,32,32,256]{3,2,1,0:T(8,128)(2,1)S(1)}, bf16[2,32,32,256]{3,2,1,0:T(8,128)(2,1)}, u32[]{:S(2)}, u32[]{:S(2)}) collective-permute-start(bf16[2,32,32,256]{3,2,1,0:T(8,128)(2,1)S(1)} %slice_multiply_fusion), channel_id=1, source_target_pairs={{0,1},{1,2},{2,3},{3,4},{4,5},{5,6},{6,7},{7,8},{8,9},{9,10},{10,1... | collective-permute-start | bytes 3145736 | tf_op jit(solution)/shard_map/ppermute | solution.py:30
  18.5 1.0 slice_bitcast_fusion.1
  19.5 0.7 fusion.44
  25.1 0.8 slice.238
  26.0 0.7 fusion.39
  26.8 1.3 collective-permute-start.3
  28.1 0.8 slice.239
  28.9 1.1 slice.237
  30.3 4.2 %collective-permute-start.5 = (bf16[34,37,256]{2,1,0:T(8,128)(2,1)S(1)}, bf16[34,37,256]{2,1,0:T(8,128)(2,1)S(1)}, u32[]{:S(2)}, u32[]{:S(2)}) collective-permute-start(bf16[34,37,256]{2,1,0:T(8,128)(2,1)S(1)} %fusion.13), channel_id=1, source_target_pairs={{0,1},{1,2},{2,3},{3,4},{4,5},{5,6},{6,7},{7,8},{8,9},{9,10},{10,1... | collective-permute-start | bytes 1932296 | tf_op jit(solution)/shard_map/ppermute | solution.py:30
  34.5 5.8 %collective-permute-done = bf16[2,32,32,256]{3,2,1,0:T(8,128)(2,1)} collective-permute-done((bf16[2,32,32,256]{3,2,1,0:T(8,128)(2,1)S(1)}, bf16[2,32,32,256]{3,2,1,0:T(8,128)(2,1)}, u32[]{:S(2)}, u32[]{:S(2)}) %collective-permute-start) | collective-permute-done | bytes 1048608 | tf_op jit(solution)/shard_map/ppermute | solution.py:30
  40.3 1.3 slice_bitcast_fusion.2
  41.6 0.5 fusion.25
  42.2 0.5 copy-done.10
  42.6 0.5 fusion.24
  43.6 3.3 %collective-permute-start.4 = (bf16[62,34,256]{2,0,1:T(8,128)(2,1)S(1)}, bf16[62,34,256]{2,0,1:T(8,128)(2,1)S(1)}, u32[]{:S(2)}, u32[]{:S(2)}) collective-permute-start(bf16[62,34,256]{2,0,1:T(8,128)(2,1)S(1)} %copy.13), channel_id=1, source_target_pairs={{0,32},{32,64},{64,96},{1,33},{33,65},{65,97},{2,34},{34,66},{66,9... | collective-permute-start | bytes 3237896 | tf_op jit(solution)/shard_map/ppermute | solution.py:30
  47.0 7.4 %collective-permute-done.5 = bf16[34,37,256]{2,1,0:T(8,128)(2,1)S(1)} collective-permute-done((bf16[34,37,256]{2,1,0:T(8,128)(2,1)S(1)}, bf16[34,37,256]{2,1,0:T(8,128)(2,1)S(1)}, u32[]{:S(2)}, u32[]{:S(2)}) %collective-permute-start.5) | collective-permute-done | bytes 644128 | tf_op jit(solution)/shard_map/ppermute | solution.py:30
  54.5 0.4 maximum_bitcast_fusion.1
  55.2 0.4 constant_dynamic-update-slice_fusion.3
  55.9 0.4 maximum_multiply_fusion
  56.3 3.1 %collective-permute-done.4 = bf16[62,34,256]{2,0,1:T(8,128)(2,1)S(1)} collective-permute-done((bf16[62,34,256]{2,0,1:T(8,128)(2,1)S(1)}, bf16[62,34,256]{2,0,1:T(8,128)(2,1)S(1)}, u32[]{:S(2)}, u32[]{:S(2)}) %collective-permute-start.4) | collective-permute-done | bytes 1079328 | tf_op jit(solution)/shard_map/ppermute | solution.py:30
  60.3 0.5 bitcast_dynamic-update-slice_fusion
  60.8 0.5 constant_dynamic-update-slice_fusion.1
  61.3 0.3 maximum_multiply_fusion.1
  62.0 1.7 copy-done
  63.7 0.9 copy.16
  64.9 12.2 %forward.1 = (bf16[1024,256]{1,0:T(8,128)(2,1)}, bf16[1024,256]{1,0:T(8,128)(2,1)}) custom-call(bf16[6,34,34,256]{3,2,1,0:T(8,128)(2,1)} %copy-done, bf16[9,1280,256]{2,1,0:T(8,128)(2,1)} %bitcast.77, bf16[9,256,256]{2,1,0:T(8,128)(2,1)} %bitcast.78), custom_call_target="tpu_custom_call" | custom-call | flops 7247757312 | bytes 25000000 | tf_op jit(solution)/shard_map/forward/pallas_call | solution.py:103
  77.0 0.5 collective-permute-start.7
  77.5 0.6 broadcast_add_fusion.at_ref
  78.1 0.6 pad_add_fusion.at_ref
  78.7 0.7 slice_bitcast_fusion.6
  79.5 1.9 collective-permute-start.9
  81.4 5.9 %collective-permute-start.8 = (bf16[1,32,256]{2,1,0:T(8,128)(2,1)S(1)}, bf16[1,32,256]{2,1,0:T(8,128)(2,1)S(1)}, u32[]{:S(2)}, u32[]{:S(2)}) collective-permute-start(bf16[1,32,256]{2,1,0:T(8,128)(2,1)S(1)} %get-tuple-element.61), channel_id=1, source_target_pairs={{0,32},{32,64},{64,96},{1,33},{33,65},{65,97},{2,34},{34,66},{66,9... | collective-permute-start | bytes 49160 | tf_op jit(solution)/shard_map/ppermute | solution.py:30
  87.3 2.6 copy.18.other_ref
  89.9 0.8 copy-done.4
  90.7 6.0 %layer_gradient.3.refs_0_ = bf16[3,2,2304,128]{3,2,1,0:T(8,128)(2,1)} custom-call(s32[2]{0:T(128)} %pad_add_fusion.at_ref, bf16[6,34,34,256]{3,2,1,0:T(8,128)(2,1)} %copy-done, bf16[2,34,34,256]{3,2,1,0:T(8,128)(2,1)} %copy.18.other_ref, bf16[1024,256]{1,0:T(8,128)(2,1)} %get-tuple-element.22.own_right, bf16[1024,256]{1,0:T(8,128)(2,1)} %copy-done.4), custom_call_target="tpu_custom_call" | custom-call | flops 2415919104 | bytes 5000000 | tf_op jit(solution)/shard_map/layer_gradient/pallas_call | solution.py:161
  96.7 1.3 collective-permute-start.11
  98.0 4.8 %collective-permute-start.10 = (bf16[34,1,256]{2,1,0:T(2,128)(2,1)S(1)}, bf16[34,1,256]{2,1,0:T(2,128)(2,1)S(1)}, u32[]{:S(2)}, u32[]{:S(2)}) collective-permute-start(bf16[34,1,256]{2,1,0:T(2,128)(2,1)S(1)} %get-tuple-element.59), channel_id=1, source_target_pairs={{0,1},{1,2},{2,3},{3,4},{4,5},{5,6},{6,7},{7,8},{8,9},{9,10},{10,1... | collective-permute-start | bytes 52232 | tf_op jit(solution)/shard_map/ppermute | solution.py:30
  103.0 6.0 %layer_gradient.4.refs_0_ = bf16[3,2,2304,128]{3,2,1,0:T(8,128)(2,1)} custom-call(s32[2]{0:T(128)} %broadcast_add_fusion.at_ref, bf16[6,34,34,256]{3,2,1,0:T(8,128)(2,1)} %copy-done, bf16[2,34,34,256]{3,2,1,0:T(8,128)(2,1)} %copy.18.other_ref, bf16[1024,256]{1,0:T(8,128)(2,1)} %get-tuple-element.22.own_right, ...), custom_call_target="tpu_custom_call", output_to_operand_aliasing={{}: (5, {})} | custom-call | flops 2415919104 | bytes 5000000 | tf_op jit(solution)/shard_map/layer_gradient/pallas_call | solution.py:161
  109.0 1.7 broadcast_select_fusion
  110.7 0.5 collective-permute-start.12
  111.2 0.9 broadcast_select_fusion.2.own_right
  112.0 0.9 broadcast_select_fusion.1.other_right
  112.9 0.5 broadcast_3_at_ref.2.at_ref
  113.8 6.0 %layer_gradient.5 = bf16[3,2,2304,128]{3,2,1,0:T(8,128)(2,1)} custom-call(s32[2]{0:T(128)} %broadcast_3_at_ref.2.at_ref, bf16[1,34,34,256]{3,2,1,0:T(8,128)(2,1)} %get-tuple-element.40.own_ref, bf16[1,34,34,256]{3,2,1,0:T(8,128)(2,1)} %bitcast.76, bf16[1024,256]{1,0:T(8,128)(2,1)} %broadcast_select_fusion.2.own_right, ...), custom_call_target="tpu_custom_call", output_to_operand_aliasing={{}: (5, {})} | custom-call | flops 2415919104 | bytes 5000000 | tf_op jit(solution)/shard_map/layer_gradient/pallas_call | solution.py:161
  119.8 23.8 %all-to-all-start = ((bf16[64,216,128]{2,1,0:T(8,128)(2,1)}), bf16[64,216,128]{2,1,0:T(8,128)(2,1)S(1)}, u32[]{:S(2)}, u32[]{:S(2)}) async-start(bf16[64,216,128]{2,1,0:T(8,128)(2,1)} %bitcast.65), calls=%async_computation | async-start | bytes 7077888 | tf_op jit(solution)/shard_map/all_to_all | solution.py:352
  143.5 3.8 %merged_step.1 = bf16[32,32,256]{2,1,0:T(8,128)(2,1)} custom-call(bf16[34,34,256]{2,1,0:T(8,128)(2,1)} %get-tuple-element.55.hidden_ref, bf16[32,32,256]{2,1,0:T(8,128)(2,1)} %current_ref.1, bf16[9,256,256]{2,1,0:T(8,128)(2,1)} %bitcast.79), custom_call_target="tpu_custom_call" | custom-call | flops 1207959552 | bytes 4000000 | tf_op jit(solution)/shard_map/merged_step/pallas_call | solution.py:203
  147.4 40.9 %all-to-all-done = bf16[64,216,128]{2,1,0:T(8,128)(2,1)S(1)} async-done(((bf16[64,216,128]{2,1,0:T(8,128)(2,1)}), bf16[64,216,128]{2,1,0:T(8,128)(2,1)S(1)}, u32[]{:S(2)}, u32[]{:S(2)}) %all-to-all-start) | async-done | bytes 3538976 | tf_op jit(solution)/shard_map/all_to_all | solution.py:352
  188.3 1.1 reduce_sum.12
  189.4 1.3 broadcast_in_dim.21
  190.7 57.3 %all_to_all.10 = bf16[64,216,128]{2,1,0:T(8,128)(2,1)S(1)} all-to-all(bf16[64,216,128]{2,1,0:T(8,128)(2,1)S(1)} %broadcast_in_dim.21), channel_id=1, replica_groups=mesh['xh'=2,'core'=2,'xl'=2,'z'=4,'y'=4] {'xh','xl','z','y'}, dimensions={0} | all-to-all | bytes 7077888 | tf_op jit(solution)/shard_map/all_to_all | solution.py:356
  247.9 3.0 %collective-permute-start.14 = (bf16[3,2,2304,128]{3,2,1,0:T(8,128)(2,1)S(1)}, bf16[3,2,2304,128]{3,2,1,0:T(8,128)(2,1)}, u32[]{:S(2)}, u32[]{:S(2)}) collective-permute-start(bf16[3,2,2304,128]{3,2,1,0:T(8,128)(2,1)S(1)} %bitcast.67), channel_id=1, source_target_pairs={{0,32},{32,0},{1,33},{33,1},{2,34},{34,2},{3,35},{35,3},{4,36},{36... | collective-permute-start | bytes 10616840 | tf_op jit(solution)/shard_map/ppermute | solution.py:315
  250.9 5.0 %final.2.refs_0_ = f32[9,1280,256]{2,1,0:T(8,128)} custom-call(s32[1]{0:T(128)} %bitcast.15.base_ref, bf16[3,2,2304,128]{3,2,1,0:T(8,128)(2,1)} %bitcast.68), custom_call_target="tpu_custom_call" | custom-call | bytes 12000000 | tf_op jit(solution)/shard_map/final/pallas_call | solution.py:233
  255.9 0.9 collective-permute-done.14.sums_ref
  256.9 1.7 slice_select_fusion
  258.7 1.6 maximum_convert_fusion
  260.3 5.2 %final.3 = f32[9,1280,256]{2,1,0:T(8,128)} custom-call(s32[1]{0:T(128)} %bitcast.35.base_ref, bf16[3,2,2304,128]{3,2,1,0:T(8,128)(2,1)} %collective-permute-done.14.sums_ref, f32[9,1280,256]{2,1,0:T(8,128)} %final.2.refs_0_), custom_call_target="tpu_custom_call", output_to_operand_aliasing={{}: (2, {})} | custom-call | bytes 12000000 | tf_op jit(solution)/shard_map/final/pallas_call | solution.py:233
  (66 shorter events, 3.9 us)
Async XLA Ops:
  0.6 7.6 %copy-start.9 = (bf16[4,32,32,256]{3,2,1,0:T(8,128)(2,1)S(1)}, bf16[4,32,32,256]{3,2,1,0:T(8,128)(2,1)}, u32[]{:S(2)}) copy-start(bf16[4,32,32,256]{3,2,1,0:T(8,128)(2,1)} %param.8) | copy-start | bytes 6291460
  1.6 24.4 %collective-permute-start.2 = (bf16[2,32,256]{2,1,0:T(8,128)(2,1)S(1)}, bf16[2,32,256]{2,1,0:T(8,128)(2,1)S(1)}, u32[]{:S(2)}, u32[]{:S(2)}) collective-permute-start(bf16[2,32,256]{2,1,0:T(8,128)(2,1)S(1)} %pad_maximum_fusion.10), channel_id=1, source_target_pairs={{32,0},{64,32},{96,64},{33,1},{65,33},{97,65},{34,2},{66,34},{98,6... | collective-permute-start | bytes 98312 | tf_op jit(solution)/shard_map/ppermute | solution.py:30
  8.5 1.0 copy-start.7
  8.6 10.9 %copy-start.13 = (s32[4,2]{0,1:T(2,128)S(1)}, s32[4,2]{0,1:T(2,128)}, u32[]{:S(2)}) copy-start(s32[4,2]{0,1:T(2,128)} %param.10) | copy-start | bytes 100
  9.5 16.4 %collective-permute-start.1 = (bf16[36,32,256]{2,1,0:T(8,128)(2,1)}, bf16[36,32,256]{2,1,0:T(8,128)(2,1)}, u32[]{:S(2)}, u32[]{:S(2)}) collective-permute-start(bf16[36,32,256]{2,1,0:T(8,128)(2,1)} %pad_maximum_fusion.2), channel_id=1, source_target_pairs={{0,32},{32,64},{64,96},{1,33},{33,65},{65,97},{2,34},{34,66},{66,9... | collective-permute-start | bytes 1769480 | tf_op jit(solution)/shard_map/ppermute | solution.py:30
  14.2 26.1 %collective-permute-start = (bf16[2,32,32,256]{3,2,1,0:T(8,128)(2,1)S(1)}, bf16[2,32,32,256]{3,2,1,0:T(8,128)(2,1)}, u32[]{:S(2)}, u32[]{:S(2)}) collective-permute-start(bf16[2,32,32,256]{3,2,1,0:T(8,128)(2,1)S(1)} %slice_multiply_fusion), channel_id=1, source_target_pairs={{0,1},{1,2},{2,3},{3,4},{4,5},{5,6},{6,7},{7,8},{8,9},{9,10},{10,1... | collective-permute-start | bytes 3145736 | tf_op jit(solution)/shard_map/ppermute | solution.py:30
  18.5 8.3 %copy-start.2 = (bf16[32,32,256]{2,1,0:T(8,128)(2,1)S(1)}, bf16[32,32,256]{2,1,0:T(8,128)(2,1)}, u32[]{:S(2)}) copy-start(bf16[32,32,256]{2,1,0:T(8,128)(2,1)} %param.13) | copy-start | bytes 1572868
  18.5 8.3 %copy-start.3 = (bf16[32,32,256]{2,1,0:T(8,128)(2,1)S(1)}, bf16[32,32,256]{2,1,0:T(8,128)(2,1)}, u32[]{:S(2)}) copy-start(bf16[32,32,256]{2,1,0:T(8,128)(2,1)} %current_ref.1) | copy-start | bytes 1572868
  26.8 7.7 %collective-permute-start.3 = (bf16[34,2,256]{2,1,0:T(2,128)(2,1)S(1)}, bf16[34,2,256]{2,1,0:T(2,128)(2,1)S(1)}, u32[]{:S(2)}, u32[]{:S(2)}) collective-permute-start(bf16[34,2,256]{2,1,0:T(2,128)(2,1)S(1)} %fusion.33), channel_id=1, source_target_pairs={{1,0},{2,1},{3,2},{4,3},{5,4},{6,5},{7,6},{8,7},{9,8},{10,9},{11,1... | collective-permute-start | bytes 104456 | tf_op jit(solution)/shard_map/ppermute | solution.py:30
  30.3 11.3 %copy-start.11 = (bf16[32,32,256]{2,1,0:T(8,128)(2,1)S(1)}, bf16[32,32,256]{2,1,0:T(8,128)(2,1)}, u32[]{:S(2)}) copy-start(bf16[32,32,256]{2,1,0:T(8,128)(2,1)} %get-tuple-element.46) | copy-start | bytes 1572868
  30.3 24.1 %collective-permute-start.5 = (bf16[34,37,256]{2,1,0:T(8,128)(2,1)S(1)}, bf16[34,37,256]{2,1,0:T(8,128)(2,1)S(1)}, u32[]{:S(2)}, u32[]{:S(2)}) collective-permute-start(bf16[34,37,256]{2,1,0:T(8,128)(2,1)S(1)} %fusion.13), channel_id=1, source_target_pairs={{0,1},{1,2},{2,3},{3,4},{4,5},{5,6},{6,7},{7,8},{8,9},{9,10},{10,1... | collective-permute-start | bytes 1932296 | tf_op jit(solution)/shard_map/ppermute | solution.py:30
  41.6 1.0 copy-start.10
  43.6 15.8 %collective-permute-start.4 = (bf16[62,34,256]{2,0,1:T(8,128)(2,1)S(1)}, bf16[62,34,256]{2,0,1:T(8,128)(2,1)S(1)}, u32[]{:S(2)}, u32[]{:S(2)}) collective-permute-start(bf16[62,34,256]{2,0,1:T(8,128)(2,1)S(1)} %copy.13), channel_id=1, source_target_pairs={{0,32},{32,64},{64,96},{1,33},{33,65},{65,97},{2,34},{34,66},{66,9... | collective-permute-start | bytes 3237896 | tf_op jit(solution)/shard_map/ppermute | solution.py:30
  61.7 2.0 copy-start
  64.6 22.7 %collective-permute-start.6 = (bf16[2,34,34,256]{3,0,2,1:T(2,128)(2,1)S(1)}, bf16[2,34,34,256]{3,0,2,1:T(2,128)(2,1)}, u32[]{:S(2)}, u32[]{:S(2)}) collective-permute-start(bf16[2,34,34,256]{3,0,2,1:T(2,128)(2,1)S(1)} %copy.16), channel_id=1, source_target_pairs={{0,32},{32,0},{1,33},{33,1},{2,34},{34,2},{3,35},{35,3},{4,36},{36... | collective-permute-start | bytes 3551240 | tf_op jit(solution)/shard_map/ppermute | solution.py:315
  77.0 12.8 %collective-permute-start.7 = (bf16[1024,256]{1,0:T(8,128)(2,1)}, bf16[1024,256]{1,0:T(8,128)(2,1)S(1)}, u32[]{:S(2)}, u32[]{:S(2)}) collective-permute-start(bf16[1024,256]{1,0:T(8,128)(2,1)} %get-tuple-element.22.own_right), channel_id=1, source_target_pairs={{0,32},{32,0},{1,33},{33,1},{2,34},{34,2},{3,35},{35,3},{4,36},{36... | collective-permute-start | bytes 1572872 | tf_op jit(solution)/shard_map/ppermute | solution.py:315
  79.5 17.2 %collective-permute-start.9 = (bf16[1,32,256]{2,1,0:T(8,128)(2,1)S(1)}, bf16[1,32,256]{2,1,0:T(8,128)(2,1)S(1)}, u32[]{:S(2)}, u32[]{:S(2)}) collective-permute-start(bf16[1,32,256]{2,1,0:T(8,128)(2,1)S(1)} %get-tuple-element.60), channel_id=1, source_target_pairs={{32,0},{64,32},{96,64},{33,1},{65,33},{97,65},{34,2},{66,34},{98,6... | collective-permute-start | bytes 49160 | tf_op jit(solution)/shard_map/ppermute | solution.py:30
  81.4 15.2 %collective-permute-start.8 = (bf16[1,32,256]{2,1,0:T(8,128)(2,1)S(1)}, bf16[1,32,256]{2,1,0:T(8,128)(2,1)S(1)}, u32[]{:S(2)}, u32[]{:S(2)}) collective-permute-start(bf16[1,32,256]{2,1,0:T(8,128)(2,1)S(1)} %get-tuple-element.61), channel_id=1, source_target_pairs={{0,32},{32,64},{64,96},{1,33},{33,65},{65,97},{2,34},{34,66},{66,9... | collective-permute-start | bytes 49160 | tf_op jit(solution)/shard_map/ppermute | solution.py:30
  89.9 6.8 %copy-start.8 = (bf16[1024,256]{1,0:T(8,128)(2,1)S(1)}, bf16[1024,256]{1,0:T(8,128)(2,1)}, u32[]{:S(2)}) copy-start(bf16[1024,256]{1,0:T(8,128)(2,1)} %get-tuple-element.23) | copy-start | bytes 1572868
  89.9 0.8 copy-start.4
  96.7 12.2 %collective-permute-start.11 = (bf16[34,1,256]{2,1,0:T(2,128)(2,1)S(1)}, bf16[34,1,256]{2,1,0:T(2,128)(2,1)S(1)}, u32[]{:S(2)}, u32[]{:S(2)}) collective-permute-start(bf16[34,1,256]{2,1,0:T(2,128)(2,1)S(1)} %get-tuple-element.58), channel_id=1, source_target_pairs={{1,0},{2,1},{3,2},{4,3},{5,4},{6,5},{7,6},{8,7},{9,8},{10,9},{11,1... | collective-permute-start | bytes 52232 | tf_op jit(solution)/shard_map/ppermute | solution.py:30
  98.0 10.9 %collective-permute-start.10 = (bf16[34,1,256]{2,1,0:T(2,128)(2,1)S(1)}, bf16[34,1,256]{2,1,0:T(2,128)(2,1)S(1)}, u32[]{:S(2)}, u32[]{:S(2)}) collective-permute-start(bf16[34,1,256]{2,1,0:T(2,128)(2,1)S(1)} %get-tuple-element.59), channel_id=1, source_target_pairs={{0,1},{1,2},{2,3},{3,4},{4,5},{5,6},{6,7},{7,8},{8,9},{9,10},{10,1... | collective-permute-start | bytes 52232 | tf_op jit(solution)/shard_map/ppermute | solution.py:30
  102.9 9.1 %collective-permute-start.13 = (bf16[1024,256]{1,0:T(8,128)(2,1)S(1)}, bf16[1024,256]{1,0:T(8,128)(2,1)S(1)}, u32[]{:S(2)}, u32[]{:S(2)}) collective-permute-start(bf16[1024,256]{1,0:T(8,128)(2,1)S(1)} %bitcast.70), channel_id=1, source_target_pairs={{0,32},{32,0},{1,33},{33,1},{2,34},{34,2},{3,35},{35,3},{4,36},{36... | collective-permute-start | bytes 1572872 | tf_op jit(solution)/shard_map/ppermute | solution.py:315
  109.0 2.2 copy-start.6
  110.7 1.4 copy-start.5
  110.7 2.3 collective-permute-start.12
  112.9 0.9 copy-start.12
  119.8 68.5 %all-to-all-start = ((bf16[64,216,128]{2,1,0:T(8,128)(2,1)}), bf16[64,216,128]{2,1,0:T(8,128)(2,1)S(1)}, u32[]{:S(2)}, u32[]{:S(2)}) async-start(bf16[64,216,128]{2,1,0:T(8,128)(2,1)} %bitcast.65), calls=%async_computation | async-start | bytes 7077888 | tf_op jit(solution)/shard_map/all_to_all | solution.py:352
  247.9 3.0 %copy-start.1 = (bf16[64,216,128]{2,1,0:T(8,128)(2,1)}, bf16[64,216,128]{2,1,0:T(8,128)(2,1)S(1)}, u32[]{:S(2)}) copy-start(bf16[64,216,128]{2,1,0:T(8,128)(2,1)S(1)} %all_to_all.10) | copy-start | bytes 10616836
  247.9 8.9 %collective-permute-start.14 = (bf16[3,2,2304,128]{3,2,1,0:T(8,128)(2,1)S(1)}, bf16[3,2,2304,128]{3,2,1,0:T(8,128)(2,1)}, u32[]{:S(2)}, u32[]{:S(2)}) collective-permute-start(bf16[3,2,2304,128]{3,2,1,0:T(8,128)(2,1)S(1)} %bitcast.67), channel_id=1, source_target_pairs={{0,32},{32,0},{1,33},{33,1},{2,34},{34,2},{3,35},{35,3},{4,36},{36... | collective-permute-start | bytes 10616840 | tf_op jit(solution)/shard_map/ppermute | solution.py:315

commit v4 on v3

--- a/solution.py
+++ b/solution.py
@@ -30,13 +30,12 @@
     return lax.ppermute(x, axis, [(i, i + by) for i in range(peers) if 0 <= i + by < peers])
 
 
-def shift_row(source, at, target):
+def shift_row(value, row, target):
     cols = target.shape[2]
-    value = source[at]
     wide = value.astype(F32)
-    target[0, at[-1]] = value[:cols]
+    target[0, row] = value[:cols]
     for col_step in (1, 2):
-        target[col_step, at[-1]] = wide[col_step : col_step + cols].astype(BF16)
+        target[col_step, row] = wide[col_step : col_step + cols].astype(BF16)
 
 
 def forward_kernel(joined_ref, weight_ref, out_weight_ref, hidden_ref, back_ref, even, odd, total,
@@ -52,7 +51,8 @@
                 multiply(t, before)
             if shifting:
                 for more in range(4):
-                    shift_row(joined_ref, (0, jnp.minimum(4 * t + more, rows - 1)), now)
+                    row = jnp.minimum(4 * t + more, rows - 1)
+                    shift_row(joined_ref[0, row], row, now)
             return carry
 
         lax.fori_loop(0, 9, tap, 0, unroll=True)
@@ -95,9 +95,8 @@
         back_ref[...] = back.astype(BF16)
 
 
-def forward(joined, merge_weight, out_weight):
-    layers, rows, wide_cols, width = joined.shape
-    cols = wide_cols - 2
+def forward(joined, cols, merge_weight, out_weight):
+    layers, rows, _, width = joined.shape
     frames = layers - 1
     cells = (rows - 2) * cols
     return pl.pallas_call(
@@ -128,8 +127,7 @@
     )(joined, merge_weight, out_weight)
 
 
-def layer_kernel(at_ref, own_ref, other_ref, own_right, other_right, *refs):
-    out_ref, own_copies, other_copies, held = refs[-4:]
+def layer_taps(own_row, other_row, own_right, other_right, out_ref, own_copies, other_copies, held):
     _, rows, cols, width = own_copies.shape
     tile, half = rows - 2, width // 2
 
@@ -140,11 +138,11 @@
         )
 
     for row in range(rows):
-        shift_row(own_ref, (0, row), own_copies)
+        shift_row(own_row(row), row, own_copies)
     for tap in range(9):
         held[tap] = product(own_copies, tap, own_right)
         for row in range(4 * tap, min(4 * tap + 4, rows)):
-            shift_row(other_ref, (0, row), other_copies)
+            shift_row(other_row(row), row, other_copies)
     for tap in range(9):
         value = held[tap] + product(other_copies, tap, other_right)
         for side in range(2):
@@ -152,44 +150,73 @@
             out_ref[0, side, tap * width : (tap + 1) * width] = part.astype(BF16)
 
 
-def layer_gradient(place, at, own, other, own_right, other_right, into=()):
-    _, rows, wide_cols, width = own.shape
-    cols = wide_cols - 2
+def layer_kernel(core_ref, own_ref, other_ref, own_right, other_right, *refs):
+    layer_taps(
+        lambda row: own_ref[0, row], lambda row: other_ref[0, row], own_right, other_right, *refs[-4:]
+    )
+
+
+def third_kernel(core_ref, own_ref, other_ref, own_hidden, other_hidden, own_back, other_back, own_cot,
+                 other_cot, into_ref, out_ref, own_copies, other_copies, held, own_right, other_right):
+    first = core_ref[0] == 0
+    own_right[...] = jnp.where(first, own_back[...], own_cot[...])
+    other_right[...] = jnp.where(first, other_back[...], other_cot[...])
+    layer_taps(
+        lambda row: jnp.where(first, own_ref[0, row], own_hidden[row]),
+        lambda row: jnp.where(first, other_ref[0, row], other_hidden[row]),
+        own_right,
+        other_right,
+        out_ref,
+        own_copies,
+        other_copies,
+        held,
+    )
+
+
+def layer_gradient(place, core, cols, windows, hidden, rights, into=()):
+    _, rows, wide_cols, width = windows[0].shape
     shape = (3, 2, 9 * width, width // 2)
-    window = (1,) + own.shape[1:]
-    right = pl.BlockSpec(own_right.shape, lambda i, at: (0, 0))
+    cells = (rows - 2) * cols
+    if hidden:
+        layer = pl.BlockSpec((1, rows, wide_cols, width), lambda i, at: (3, 0, 0, 0))
+    else:
+        layer = pl.BlockSpec(
+            (1, rows, wide_cols, width), lambda i, at: (3 * at[0] + 1 + place, 0, 0, 0)
+        )
+    whole = pl.BlockSpec((rows, wide_cols, width), lambda i, at: (0, 0, 0))
+    right = pl.BlockSpec((cells, width), lambda i, at: (0, 0))
+    operands = (core, *windows, *hidden, *rights, *into)
+    more = [pltpu.VMEM((cells, width), BF16)] * 2 if hidden else []
     return pl.pallas_call(
-        layer_kernel,
+        third_kernel if hidden else layer_kernel,
         grid_spec=pltpu.PrefetchScalarGridSpec(
             num_scalar_prefetch=1,
             grid=(1,),
-            in_specs=[
-                pl.BlockSpec(window, lambda i, at: (at[0], 0, 0, 0)),
-                pl.BlockSpec(window, lambda i, at: (at[1], 0, 0, 0)),
-                right,
-                right,
-            ]
+            in_specs=[layer] * 2
+            + [whole] * len(hidden)
+            + [right] * len(rights)
             + [pl.BlockSpec(memory_space=pl.ANY)] * len(into),
             out_specs=pl.BlockSpec((1,) + shape[1:], lambda i, at: (place, 0, 0, 0)),
             scratch_shapes=[
                 pltpu.VMEM((3, rows, cols, width), BF16),
                 pltpu.VMEM((3, rows, cols, width), BF16),
                 pltpu.VMEM((9, width, width), F32),
-            ],
+            ]
+            + more,
         ),
         out_shape=jax.ShapeDtypeStruct(shape, BF16),
-        input_output_aliases={5: 0} if into else {},
+        input_output_aliases={len(operands) - 1: 0} if into else {},
         compiler_params=PARAMS,
-        cost_estimate=work(18 * own_right.shape[0] * width * width, 5_000_000),
+        cost_estimate=work(18 * cells * width * width, 5_000_000),
         name="layer_gradient",
-    )(at, own, other, own_right, other_right, *into)
+    )(*operands)
 
 
 def merged_kernel(hidden_ref, current_ref, weight_ref, merged_ref, copies, total):
     _, rows, cols, width = copies.shape
     tile = rows - 2
     for row in range(rows):
-        shift_row(hidden_ref, (row,), copies)
+        shift_row(hidden_ref[row], row, copies)
     total[...] = current_ref[...].reshape(tile * cols, width).astype(F32)
     for tap in range(9):
         window = copies[tap % 3, tap // 3 : tap // 3 + tile].reshape(tile * cols, width)
@@ -296,18 +323,23 @@
         start = tile - 2 - offsets[k, 0]
         return lax.dynamic_slice(both, (start, jnp.int32(0), jnp.int32(0)), (ext, ext_cols, width)) * inside
 
+    blank = jnp.zeros((ext, -ext_cols % 8, width), BF16)
+
+    def filled(*pieces):
+        return jnp.concatenate([*pieces, blank], axis=1)
+
     joined = jnp.stack(
         [
-            jnp.concatenate([side[:, cols + 4 :], cot, right[:, 1:]], axis=1),
-            jnp.concatenate([side[:, cols + 3 : cols + 4], now, right[:, :1]], axis=1),
-            jnp.concatenate([side[:, cols : cols + 3], near0[:, : cols - 1]], axis=1) * inside,
-            rows_of(above12[: tile - 1], wide1, 1),
-            rows_of(above12[tile - 1 :], wide2, 2),
-            jnp.concatenate([side[:, 1:cols], near3[:, :3]], axis=1) * inside,
+            filled(side[:, cols + 4 :], cot, right[:, 1:]),
+            filled(side[:, cols + 3 : cols + 4], now, right[:, :1]),
+            filled(jnp.concatenate([side[:, cols : cols + 3], near0[:, : cols - 1]], axis=1) * inside),
+            filled(rows_of(above12[: tile - 1], wide1, 1)),
+            filled(rows_of(above12[tile - 1 :], wide2, 2)),
+            filled(jnp.concatenate([side[:, 1:cols], near3[:, :3]], axis=1) * inside),
         ]
     )
     hidden, back_pre = forward(
-        joined, merge_weight.reshape(9, -1, width), out_weight.reshape(9, width, width)
+        joined, cols, merge_weight.reshape(9, -1, width), out_weight.reshape(9, width, width)
     )
     first = core[0] == 0
 
@@ -315,14 +347,13 @@
         return lax.ppermute(x, "core", SWAP)
 
     flat_cot = cotangent.reshape(tile * cols, width)
-    other_two = swapped(jnp.where(first, joined[4:6], joined[1:3]))
+    windows = (joined, swapped(joined))
 
     hidden = hidden.reshape(tile, cols, width)
     hidden_above = moved(hidden[-1:], ROW, 1)
     hidden_below = moved(hidden[:1], ROW, -1)
-    other_back = swapped(back_pre)
-    at = jnp.concatenate([3 * core + 1, jnp.zeros((1,), jnp.int32)])
-    sums = layer_gradient(0, at, joined, other_two, back_pre, other_back)
+    backs = (back_pre, swapped(back_pre))
+    sums = layer_gradient(0, core, cols, windows, (), backs)
     sums, hidden_above, hidden_below, flat_cot = lax.optimization_barrier(
         (sums, hidden_above, hidden_below, flat_cot)
     )
@@ -330,27 +361,20 @@
     hidden_pad = jnp.concatenate([hidden_above, hidden, hidden_below], axis=0)
     hidden_left = moved(hidden_pad[:, -1:], COL, 1)
     hidden_right = moved(hidden_pad[:, :1], COL, -1)
-    sums = layer_gradient(1, at + 1, joined, other_two, back_pre, other_back, (sums,))
-    sums, hidden_left, hidden_right = lax.optimization_barrier((sums, hidden_left, hidden_right))
-    hidden_pad = jnp.concatenate([hidden_left, hidden_pad, hidden_right], axis=1)
-    own_third = jnp.where(first, joined[3], hidden_pad)
-    other_third = swapped(jnp.where(first, hidden_pad, joined[3]))
-    sums = layer_gradient(
-        2,
-        jnp.zeros((2,), jnp.int32),
-        own_third[None],
-        other_third[None],
-        jnp.where(first, back_pre, flat_cot),
-        jnp.where(first, other_back, other_cot),
-        (sums,),
-    )
+    sums = layer_gradient(1, core, cols, windows, (), backs, (sums,))
+    sums, hidden_left, hidden_right, other_cot = lax.optimization_barrier(
+        (sums, hidden_left, hidden_right, other_cot)
+    )
+    cots = (flat_cot, other_cot)
+    hidden_pad = filled(hidden_left, hidden_pad, hidden_right)
+    hiddens = (hidden_pad, swapped(hidden_pad))
+    sums = layer_gradient(2, core, cols, windows, hiddens, (*backs, *cots), (sums,))
     merged = merged_step(hidden_pad, current, out_weight.reshape(9, width, width))
 
     chips = lax.axis_size(CHIPS)
     half = width // 2
     blocks = sums.reshape(chips, -1, half)
     got = lax.all_to_all(blocks, CHIPS, split_axis=0, concat_axis=0)
-    got, merged = lax.optimization_barrier((got, merged))
     share = jnp.sum(got.astype(F32), axis=0).astype(BF16)
     spread = jnp.broadcast_to(share[None], blocks.shape)
     own = lax.all_to_all(spread, CHIPS, split_axis=0, concat_axis=0).reshape(sums.shape)

time: 267 us -> 256 us (0.959)
  blocking collectives: 57.3 us -> 117 us
  waiting for transfers between devices: 58.2 us -> 18.7 us
  starting transfers between devices: 62.9 us -> 40 us
  other arithmetic: 18.4 us -> 14.7 us
  local copies, waits for them, and re-layouts: 18.5 us -> 14.9 us
    all_to_all x0 -> x1, blocking collectives: none -> 67.1 us  [shards(): got = lax.all_to_all(blocks, CHIPS, split_axis=0, concat_axis=0)]
    all_to_all x1 -> x0, waiting for transfers between devices: 40.9 us -> none  [shards(): got = lax.all_to_all(blocks, CHIPS, split_axis=0, concat_axis=0)]
    all_to_all x1 -> x0, starting transfers between devices: 23.8 us -> none  [shards(): got = lax.all_to_all(blocks, CHIPS, split_axis=0, concat_axis=0)]
    all_to_all x1, blocking collectives: 57.3 us -> 49.6 us  [shards(): lax.all_to_all(spread, CHIPS, split_axis=0, concat_axis=0)]
    select_n x4 -> x0, other arithmetic: 3.67 us -> none  [the longest x1 1.66 us: shards(): other_third = swapped(jnp.where(first, hidden_pad, joined[3]))]
  transfers between devices with their start and end apart: 16 -> 15, of which waited for: 6 -> 4; matrix products, arithmetic and copies ran while one was open for 9% -> 6% of each run, Pallas kernels for 12% -> 12%
where the time goes in v4:
time: 256 us; the launch traced here: 254 us
  blocking collectives  117 us (46%)
  Pallas kernels  43.1 us (17%)
  starting transfers between devices  40 us (16%)
  waiting for transfers between devices  18.7 us (7%)
  local copies, waits for them, and re-layouts  14.9 us (6%)
  other arithmetic  14.7 us (6%)
  between operations  5.99 us (2%)
    all_to_all x1, blocking collectives, shards(): got = lax.all_to_all(blocks, CHIPS, split_axis=0, concat_axis=0)  67.1 us
    all_to_all x1, blocking collectives, shards(): lax.all_to_all(spread, CHIPS, split_axis=0, concat_axis=0)  49.6 us
    ppermute x10, starting transfers between devices, moved(): lax.ppermute(x, axis, [(i, i + by) for i in range(peers) if 0 <= i + by <...  35 us
    ppermute x10, waiting for transfers between devices, moved(): lax.ppermute(x, axis, [(i, i + by) for i in range(peers) if 0 <= i + by <...  17 us
    pallas_call x3, Pallas kernels, layer_gradient(): pl.pallas_call(third_kernel if hidden else layer_kernel, grid_spec=pltpu....  16.8 us
    pallas_call x1, Pallas kernels, forward(): pl.pallas_call(forward_kernel, grid=(layers + 1,), in_specs=[pl.BlockSpec...  12.2 us
    pallas_call x2, Pallas kernels, final(): pl.pallas_call(final_kernel, grid_spec=pltpu.PrefetchScalarGridSpec(num_s...  10.3 us
  transfers between devices with their start and end apart: 15, of which 4 were waited for; matrix products, arithmetic and copies ran while one was open for 6% of the time, Pallas kernels for 12%

profile of v4, /device:TPU:1, one launch (start us, length us, event | category | flops | bytes accessed | tf_op | source)
XLA Modules:
  0.0 254.2 jit_solution(7468909093476084883)
XLA Ops:
  0.6 0.9 fusion.40
  1.6 3.3 %collective-permute-start.1 = (bf16[2,32,256]{2,1,0:T(8,128)(2,1)S(1)}, bf16[2,32,256]{2,1,0:T(8,128)(2,1)S(1)}, u32[]{:S(2)}, u32[]{:S(2)}) collective-permute-start(bf16[2,32,256]{2,1,0:T(8,128)(2,1)S(1)} %pad_maximum_fusion.9), channel_id=1, source_target_pairs={{32,0},{64,32},{96,64},{33,1},{65,33},{97,65},{34,2},{66,34},{98,6... | collective-permute-start | bytes 98312 | tf_op jit(solution)/shard_map/ppermute | solution.py:30
  4.9 0.8 convert_bitcast_fusion
  5.8 0.8 convert_element_type.16
  6.6 1.6 slice_multiply_fusion
  8.2 0.3 bitcast_multiply_fusion.1
  8.6 0.9 pad_maximum_fusion.3
  9.5 4.8 %collective-permute-start = (bf16[36,32,256]{2,1,0:T(8,128)(2,1)}, bf16[36,32,256]{2,1,0:T(8,128)(2,1)}, u32[]{:S(2)}, u32[]{:S(2)}) collective-permute-start(bf16[36,32,256]{2,1,0:T(8,128)(2,1)} %pad_maximum_fusion.3), channel_id=1, source_target_pairs={{0,32},{32,64},{64,96},{1,33},{33,65},{65,97},{2,34},{34,66},{66,9... | collective-permute-start | bytes 1769480 | tf_op jit(solution)/shard_map/ppermute | solution.py:30
  14.3 4.2 %collective-permute-start.3 = (bf16[2,32,32,256]{3,2,1,0:T(8,128)(2,1)S(1)}, bf16[2,32,32,256]{3,2,1,0:T(8,128)(2,1)}, u32[]{:S(2)}, u32[]{:S(2)}) collective-permute-start(bf16[2,32,32,256]{3,2,1,0:T(8,128)(2,1)S(1)} %slice_multiply_fusion), channel_id=1, source_target_pairs={{0,1},{1,2},{2,3},{3,4},{4,5},{5,6},{6,7},{7,8},{8,9},{9,10},{10,1... | collective-permute-start | bytes 3145736 | tf_op jit(solution)/shard_map/ppermute | solution.py:30
  18.5 1.0 slice_bitcast_fusion.2
  19.6 0.6 fusion.44
  25.1 0.8 slice.227
  26.0 0.1 pad.40.clone
  26.1 0.7 fusion.39
  26.9 1.3 collective-permute-start.4
  28.2 0.8 slice.228
  29.0 1.1 slice.226
  30.0 0.2 fusion.13
  30.3 4.2 %collective-permute-start.2 = (bf16[34,37,256]{2,1,0:T(8,128)(2,1)S(1)}, bf16[34,37,256]{2,1,0:T(8,128)(2,1)S(1)}, u32[]{:S(2)}, u32[]{:S(2)}) collective-permute-start(bf16[34,37,256]{2,1,0:T(8,128)(2,1)S(1)} %fusion.13), channel_id=1, source_target_pairs={{0,1},{1,2},{2,3},{3,4},{4,5},{5,6},{6,7},{7,8},{8,9},{9,10},{10,1... | collective-permute-start | bytes 1932296 | tf_op jit(solution)/shard_map/ppermute | solution.py:30
  34.5 6.0 %collective-permute-done.3 = bf16[2,32,32,256]{3,2,1,0:T(8,128)(2,1)} collective-permute-done((bf16[2,32,32,256]{3,2,1,0:T(8,128)(2,1)S(1)}, bf16[2,32,32,256]{3,2,1,0:T(8,128)(2,1)}, u32[]{:S(2)}, u32[]{:S(2)}) %collective-permute-start.3) | collective-permute-done | bytes 1048608 | tf_op jit(solution)/shard_map/ppermute | solution.py:30
  40.5 1.3 slice_bitcast_fusion.3
  41.7 0.5 fusion.29
  42.2 0.5 fusion.28
  42.8 0.1 pad_maximum_fusion
  43.0 0.3 copy.13
  43.2 3.3 %collective-permute-start.5 = (bf16[62,34,256]{2,0,1:T(8,128)(2,1)S(1)}, bf16[62,34,256]{2,0,1:T(8,128)(2,1)S(1)}, u32[]{:S(2)}, u32[]{:S(2)}) collective-permute-start(bf16[62,34,256]{2,0,1:T(8,128)(2,1)S(1)} %copy.13), channel_id=1, source_target_pairs={{0,32},{32,64},{64,96},{1,33},{33,65},{65,97},{2,34},{34,66},{66,9... | collective-permute-start | bytes 3237896 | tf_op jit(solution)/shard_map/ppermute | solution.py:30
  46.6 0.1 and_convert_fusion
  46.7 7.8 %collective-permute-done.2 = bf16[34,37,256]{2,1,0:T(8,128)(2,1)S(1)} collective-permute-done((bf16[34,37,256]{2,1,0:T(8,128)(2,1)S(1)}, bf16[34,37,256]{2,1,0:T(8,128)(2,1)S(1)}, u32[]{:S(2)}, u32[]{:S(2)}) %collective-permute-start.2) | collective-permute-done | bytes 644128 | tf_op jit(solution)/shard_map/ppermute | solution.py:30
  54.6 0.3 slice.241
  54.9 0.4 fusion.26
  55.3 0.6 fusion.27
  55.9 3.2 %collective-permute-done.5 = bf16[62,34,256]{2,0,1:T(8,128)(2,1)S(1)} collective-permute-done((bf16[62,34,256]{2,0,1:T(8,128)(2,1)S(1)}, bf16[62,34,256]{2,0,1:T(8,128)(2,1)S(1)}, u32[]{:S(2)}, u32[]{:S(2)}) %collective-permute-start.5) | collective-permute-done | bytes 1079328 | tf_op jit(solution)/shard_map/ppermute | solution.py:30
  59.0 0.3 fusion.37
  59.3 0.3 copy.17
  59.6 0.3 copy.16
  59.9 2.6 %fusion.23 = (bf16[34,34,256]{2,1,0:T(8,128)(2,1)S(1)}, bf16[34,34,256]{2,1,0:T(8,128)(2,1)S(1)}, bf16[34,34,256]{2,1,0:T(8,128)(2,1)S(1)}, bf16[34,34,256]{2,1,0:T(8,128)(2,1)S(1)}) fusion(bf16[3,32,256]{2,1,0:T(8,128)(2,1)S(1)} %slice.227, bf16[31,32,256]{2,1,0:T(8,128)(2,1)S(1)} %slice.226, bf16[34,31,256]{2,1,0:T(8,128)(2,1)S(1)} %slice.241, ...), kind=kLoop, calls=%fused_computation.41 | loop fusion | flops 7398400 | bytes 6269200 | tf_op jit(solution)/shard_map/mul | solution.py:338
  62.9 0.3 collective-permute-start.6
  63.1 1.7 copy-done
  64.9 12.2 %forward.1 = (bf16[1024,256]{1,0:T(8,128)(2,1)}, bf16[1024,256]{1,0:T(8,128)(2,1)}) custom-call(bf16[6,34,40,256]{3,2,1,0:T(8,128)(2,1)} %copy-done, bf16[9,1280,256]{2,1,0:T(8,128)(2,1)} %bitcast.67, bf16[9,256,256]{2,1,0:T(8,128)(2,1)} %bitcast.68), custom_call_target="tpu_custom_call" | custom-call | flops 7247757312 | bytes 25000000 | tf_op jit(solution)/shard_map/forward/pallas_call | solution.py:102
  77.0 0.7 slice_bitcast_fusion.4
  77.7 2.4 collective-permute-start.9
  80.2 5.4 %collective-permute-start.8 = (bf16[1,32,256]{2,1,0:T(8,128)(2,1)S(1)}, bf16[1,32,256]{2,1,0:T(8,128)(2,1)S(1)}, u32[]{:S(2)}, u32[]{:S(2)}) collective-permute-start(bf16[1,32,256]{2,1,0:T(8,128)(2,1)S(1)} %get-tuple-element.48), channel_id=1, source_target_pairs={{0,32},{32,64},{64,96},{1,33},{33,65},{65,97},{2,34},{34,66},{66,9... | collective-permute-start | bytes 49160 | tf_op jit(solution)/shard_map/ppermute | solution.py:30
  85.6 0.8 copy-done.4
  86.4 5.4 %layer_gradient.3.refs_0_ = bf16[3,2,2304,128]{3,2,1,0:T(8,128)(2,1)} custom-call(s32[1]{0:T(128)} %bitcast.core_ref, bf16[6,34,40,256]{3,2,1,0:T(8,128)(2,1)} %copy-done, bf16[6,34,40,256]{3,2,1,0:T(8,128)(2,1)} %collective-permute-done.6.other_ref, bf16[1024,256]{1,0:T(8,128)(2,1)} %get-tuple-element.21.own_right.own_back, bf16[1024,256]{1,0:T(8,128)(2,1)} %copy-done.4), custom_call_target="tpu_custom_call" | custom-call | flops 2415919104 | bytes 5000000 | tf_op jit(solution)/shard_map/layer_gradient/pallas_call | solution.py:190
  91.8 0.1 collective-permute-start.12
  92.0 1.3 collective-permute-start.11
  93.3 4.8 %collective-permute-start.10 = (bf16[34,1,256]{2,1,0:T(2,128)(2,1)S(1)}, bf16[34,1,256]{2,1,0:T(2,128)(2,1)S(1)}, u32[]{:S(2)}, u32[]{:S(2)}) collective-permute-start(bf16[34,1,256]{2,1,0:T(2,128)(2,1)S(1)} %get-tuple-element.46), channel_id=1, source_target_pairs={{0,1},{1,2},{2,3},{3,4},{4,5},{5,6},{6,7},{7,8},{8,9},{9,10},{10,1... | collective-permute-start | bytes 52232 | tf_op jit(solution)/shard_map/ppermute | solution.py:30
  98.1 5.3 %layer_gradient.4.into_ref = bf16[3,2,2304,128]{3,2,1,0:T(8,128)(2,1)} custom-call(s32[1]{0:T(128)} %bitcast.core_ref, bf16[6,34,40,256]{3,2,1,0:T(8,128)(2,1)} %copy-done, bf16[6,34,40,256]{3,2,1,0:T(8,128)(2,1)} %collective-permute-done.6.other_ref, bf16[1024,256]{1,0:T(8,128)(2,1)} %get-tuple-element.21.own_right.own_back, ...), custom_call_target="tpu_custom_call", output_to_operand_aliasing={{}: (5, {})} | custom-call | flops 2415919104 | bytes 5000000 | tf_op jit(solution)/shard_map/layer_gradient/pallas_call | solution.py:190
  103.5 0.6 maximum_maximum_fusion.hidden_ref.own_hidden
  104.1 1.1 collective-permute-start.13
  105.2 1.8 collective-permute-done.13.other_hidden
  107.0 0.9 copy-done.11
  107.9 6.1 %layer_gradient.5 = bf16[3,2,2304,128]{3,2,1,0:T(8,128)(2,1)} custom-call(s32[1]{0:T(128)} %bitcast.core_ref, bf16[6,34,40,256]{3,2,1,0:T(8,128)(2,1)} %copy-done, bf16[6,34,40,256]{3,2,1,0:T(8,128)(2,1)} %collective-permute-done.6.other_ref, bf16[34,40,256]{2,1,0:T(8,128)(2,1)} %copy-done.5, ...), custom_call_target="tpu_custom_call", output_to_operand_aliasing={{}: (9, {})} | custom-call | flops 2415919104 | bytes 5000000 | tf_op jit(solution)/shard_map/layer_gradient/pallas_call | solution.py:190
  113.9 67.1 %all_to_all.10 = bf16[64,216,128]{2,1,0:T(8,128)(2,1)S(1)} all-to-all(bf16[64,216,128]{2,1,0:T(8,128)(2,1)} %bitcast.56), channel_id=1, replica_groups=mesh['xh'=2,'core'=2,'xl'=2,'z'=4,'y'=4] {'xh','xl','z','y'}, dimensions={0} | all-to-all | bytes 7077888 | tf_op jit(solution)/shard_map/all_to_all | solution.py:377
  181.0 1.1 reduce_sum.12
  182.2 1.3 broadcast_in_dim.8
  183.4 49.6 %all_to_all.11 = bf16[64,216,128]{2,1,0:T(8,128)(2,1)S(1)} all-to-all(bf16[64,216,128]{2,1,0:T(8,128)(2,1)S(1)} %broadcast_in_dim.8), channel_id=1, replica_groups=mesh['xh'=2,'core'=2,'xl'=2,'z'=4,'y'=4] {'xh','xl','z','y'}, dimensions={0} | all-to-all | bytes 7077888 | tf_op jit(solution)/shard_map/all_to_all | solution.py:380
  233.1 3.6 %collective-permute-start.14 = (bf16[3,2,2304,128]{3,2,1,0:T(8,128)(2,1)S(1)}, bf16[3,2,2304,128]{3,2,1,0:T(8,128)(2,1)}, u32[]{:S(2)}, u32[]{:S(2)}) collective-permute-start(bf16[3,2,2304,128]{3,2,1,0:T(8,128)(2,1)S(1)} %bitcast.58), channel_id=1, source_target_pairs={{0,32},{32,0},{1,33},{33,1},{2,34},{34,2},{3,35},{35,3},{4,36},{36... | collective-permute-start | bytes 10616840 | tf_op jit(solution)/shard_map/ppermute | solution.py:347
  236.6 3.8 %merged_step.1 = bf16[32,32,256]{2,1,0:T(8,128)(2,1)} custom-call(bf16[34,40,256]{2,1,0:T(8,128)(2,1)} %copy-done.5, bf16[32,32,256]{2,1,0:T(8,128)(2,1)} %current_ref.1, bf16[9,256,256]{2,1,0:T(8,128)(2,1)} %bitcast.69), custom_call_target="tpu_custom_call" | custom-call | flops 1207959552 | bytes 4000000 | tf_op jit(solution)/shard_map/merged_step/pallas_call | solution.py:230
  240.5 5.0 %final.2.refs_0_ = f32[9,1280,256]{2,1,0:T(8,128)} custom-call(s32[1]{0:T(128)S(6)} %mul.86.base_ref, bf16[3,2,2304,128]{3,2,1,0:T(8,128)(2,1)} %bitcast.59), custom_call_target="tpu_custom_call" | custom-call | bytes 12000000 | tf_op jit(solution)/shard_map/final/pallas_call | solution.py:260
  245.5 1.8 slice_select_fusion
  247.2 0.1 fusion.36
  247.3 1.6 maximum_convert_fusion
  248.9 5.2 %final.3 = f32[9,1280,256]{2,1,0:T(8,128)} custom-call(s32[1]{0:T(128)S(6)} %mul.85.base_ref, bf16[3,2,2304,128]{3,2,1,0:T(8,128)(2,1)} %collective-permute-done.14.sums_ref, f32[9,1280,256]{2,1,0:T(8,128)} %final.2.refs_0_), custom_call_target="tpu_custom_call", output_to_operand_aliasing={{}: (2, {})} | custom-call | bytes 12000000 | tf_op jit(solution)/shard_map/final/pallas_call | solution.py:260
  (57 shorter events, 0.8 us)
Async XLA Ops:
  0.6 7.6 %copy-start.8 = (bf16[4,32,32,256]{3,2,1,0:T(8,128)(2,1)S(1)}, bf16[4,32,32,256]{3,2,1,0:T(8,128)(2,1)}, u32[]{:S(2)}) copy-start(bf16[4,32,32,256]{3,2,1,0:T(8,128)(2,1)} %param.8) | copy-start | bytes 6291460
  1.6 24.5 %collective-permute-start.1 = (bf16[2,32,256]{2,1,0:T(8,128)(2,1)S(1)}, bf16[2,32,256]{2,1,0:T(8,128)(2,1)S(1)}, u32[]{:S(2)}, u32[]{:S(2)}) collective-permute-start(bf16[2,32,256]{2,1,0:T(8,128)(2,1)S(1)} %pad_maximum_fusion.9), channel_id=1, source_target_pairs={{32,0},{64,32},{96,64},{33,1},{65,33},{97,65},{34,2},{66,34},{98,6... | collective-permute-start | bytes 98312 | tf_op jit(solution)/shard_map/ppermute | solution.py:30
  8.5 11.0 %copy-start.7 = (bf16[32,32,256]{2,1,0:T(8,128)(2,1)}, bf16[32,32,256]{2,1,0:T(8,128)(2,1)S(1)}, u32[]{:S(2)}) copy-start(bf16[32,32,256]{2,1,0:T(8,128)(2,1)S(1)} %get-tuple-element.31) | copy-start | bytes 1572868
  8.6 10.9 %copy-start.13 = (s32[4,2]{0,1:T(2,128)S(1)}, s32[4,2]{0,1:T(2,128)}, u32[]{:S(2)}) copy-start(s32[4,2]{0,1:T(2,128)} %param.10) | copy-start | bytes 100
  9.5 17.3 %copy-start.2 = (bf16[32,32,256]{2,1,0:T(8,128)(2,1)S(1)}, bf16[32,32,256]{2,1,0:T(8,128)(2,1)}, u32[]{:S(2)}) copy-start(bf16[32,32,256]{2,1,0:T(8,128)(2,1)} %param.13) | copy-start | bytes 1572868
  9.5 17.3 %copy-start.3 = (bf16[32,32,256]{2,1,0:T(8,128)(2,1)S(1)}, bf16[32,32,256]{2,1,0:T(8,128)(2,1)}, u32[]{:S(2)}) copy-start(bf16[32,32,256]{2,1,0:T(8,128)(2,1)} %current_ref.1) | copy-start | bytes 1572868
  9.5 16.5 %collective-permute-start = (bf16[36,32,256]{2,1,0:T(8,128)(2,1)}, bf16[36,32,256]{2,1,0:T(8,128)(2,1)}, u32[]{:S(2)}, u32[]{:S(2)}) collective-permute-start(bf16[36,32,256]{2,1,0:T(8,128)(2,1)} %pad_maximum_fusion.3), channel_id=1, source_target_pairs={{0,32},{32,64},{64,96},{1,33},{33,65},{65,97},{2,34},{34,66},{66,9... | collective-permute-start | bytes 1769480 | tf_op jit(solution)/shard_map/ppermute | solution.py:30
  14.3 26.1 %collective-permute-start.3 = (bf16[2,32,32,256]{3,2,1,0:T(8,128)(2,1)S(1)}, bf16[2,32,32,256]{3,2,1,0:T(8,128)(2,1)}, u32[]{:S(2)}, u32[]{:S(2)}) collective-permute-start(bf16[2,32,32,256]{3,2,1,0:T(8,128)(2,1)S(1)} %slice_multiply_fusion), channel_id=1, source_target_pairs={{0,1},{1,2},{2,3},{3,4},{4,5},{5,6},{6,7},{7,8},{8,9},{9,10},{10,1... | collective-permute-start | bytes 3145736 | tf_op jit(solution)/shard_map/ppermute | solution.py:30
  26.9 7.6 %collective-permute-start.4 = (bf16[34,2,256]{2,1,0:T(2,128)(2,1)S(1)}, bf16[34,2,256]{2,1,0:T(2,128)(2,1)S(1)}, u32[]{:S(2)}, u32[]{:S(2)}) collective-permute-start(bf16[34,2,256]{2,1,0:T(2,128)(2,1)S(1)} %fusion.35), channel_id=1, source_target_pairs={{1,0},{2,1},{3,2},{4,3},{5,4},{6,5},{7,6},{8,7},{9,8},{10,9},{11,1... | collective-permute-start | bytes 104456 | tf_op jit(solution)/shard_map/ppermute | solution.py:30
  30.3 11.4 %copy-start.10 = (bf16[32,32,256]{2,1,0:T(8,128)(2,1)S(1)}, bf16[32,32,256]{2,1,0:T(8,128)(2,1)}, u32[]{:S(2)}) copy-start(bf16[32,32,256]{2,1,0:T(8,128)(2,1)} %get-tuple-element.37) | copy-start | bytes 1572868
  30.3 11.9 %copy-start.9 = (bf16[32,32,256]{2,1,0:T(8,128)(2,1)S(1)}, bf16[32,32,256]{2,1,0:T(8,128)(2,1)}, u32[]{:S(2)}) copy-start(bf16[32,32,256]{2,1,0:T(8,128)(2,1)} %get-tuple-element.38) | copy-start | bytes 1572868
  30.3 24.2 %collective-permute-start.2 = (bf16[34,37,256]{2,1,0:T(8,128)(2,1)S(1)}, bf16[34,37,256]{2,1,0:T(8,128)(2,1)S(1)}, u32[]{:S(2)}, u32[]{:S(2)}) collective-permute-start(bf16[34,37,256]{2,1,0:T(8,128)(2,1)S(1)} %fusion.13), channel_id=1, source_target_pairs={{0,1},{1,2},{2,3},{3,4},{4,5},{5,6},{6,7},{7,8},{8,9},{9,10},{10,1... | collective-permute-start | bytes 1932296 | tf_op jit(solution)/shard_map/ppermute | solution.py:30
  43.2 15.8 %collective-permute-start.5 = (bf16[62,34,256]{2,0,1:T(8,128)(2,1)S(1)}, bf16[62,34,256]{2,0,1:T(8,128)(2,1)S(1)}, u32[]{:S(2)}, u32[]{:S(2)}) collective-permute-start(bf16[62,34,256]{2,0,1:T(8,128)(2,1)S(1)} %copy.13), channel_id=1, source_target_pairs={{0,32},{32,64},{64,96},{1,33},{33,65},{65,97},{2,34},{34,66},{66,9... | collective-permute-start | bytes 3237896 | tf_op jit(solution)/shard_map/ppermute | solution.py:30
  62.8 2.0 copy-start
  62.9 22.7 %collective-permute-start.6 = (bf16[6,34,40,256]{3,2,1,0:T(8,128)(2,1)S(1)}, bf16[6,34,40,256]{3,2,1,0:T(8,128)(2,1)}, u32[]{:S(2)}, u32[]{:S(2)}) collective-permute-start(bf16[6,34,40,256]{3,2,1,0:T(8,128)(2,1)S(1)} %bitcast_dynamic-update-slice_fusion.joined_ref.own_ref), channel_id=1, source_target_pairs={{0,32},{32,0},{1,33},{33,1},{2,34},{34,2},{3,35},{35,3},{4,36},{36... | collective-permute-start | bytes 12533768 | tf_op jit(solution)/shard_map/ppermute | solution.py:347
  77.0 8.6 %collective-permute-start.7 = (bf16[1024,256]{1,0:T(8,128)(2,1)}, bf16[1024,256]{1,0:T(8,128)(2,1)S(1)}, u32[]{:S(2)}, u32[]{:S(2)}) collective-permute-start(bf16[1024,256]{1,0:T(8,128)(2,1)} %get-tuple-element.21.own_right.own_back), channel_id=1, source_target_pairs={{0,32},{32,0},{1,33},{33,1},{2,34},{34,2},{3,35},{35,3},{4,36},{36... | collective-permute-start | bytes 1572872 | tf_op jit(solution)/shard_map/ppermute | solution.py:347
  77.7 14.1 %collective-permute-start.9 = (bf16[1,32,256]{2,1,0:T(8,128)(2,1)S(1)}, bf16[1,32,256]{2,1,0:T(8,128)(2,1)S(1)}, u32[]{:S(2)}, u32[]{:S(2)}) collective-permute-start(bf16[1,32,256]{2,1,0:T(8,128)(2,1)S(1)} %get-tuple-element.47), channel_id=1, source_target_pairs={{32,0},{64,32},{96,64},{33,1},{65,33},{97,65},{34,2},{66,34},{98,6... | collective-permute-start | bytes 49160 | tf_op jit(solution)/shard_map/ppermute | solution.py:30
  80.2 11.7 %collective-permute-start.8 = (bf16[1,32,256]{2,1,0:T(8,128)(2,1)S(1)}, bf16[1,32,256]{2,1,0:T(8,128)(2,1)S(1)}, u32[]{:S(2)}, u32[]{:S(2)}) collective-permute-start(bf16[1,32,256]{2,1,0:T(8,128)(2,1)S(1)} %get-tuple-element.48), channel_id=1, source_target_pairs={{0,32},{32,64},{64,96},{1,33},{33,65},{65,97},{2,34},{34,66},{66,9... | collective-permute-start | bytes 49160 | tf_op jit(solution)/shard_map/ppermute | solution.py:30
  85.6 0.8 copy-start.4
  86.4 5.5 %copy-start.6 = (bf16[1024,256]{1,0:T(8,128)(2,1)S(1)}, bf16[1024,256]{1,0:T(8,128)(2,1)}, u32[]{:S(2)}) copy-start(bf16[1024,256]{1,0:T(8,128)(2,1)} %get-tuple-element.22) | copy-start | bytes 1572868
  91.8 11.7 %collective-permute-start.12 = (bf16[1024,256]{1,0:T(8,128)(2,1)S(1)}, bf16[1024,256]{1,0:T(8,128)(2,1)S(1)}, u32[]{:S(2)}, u32[]{:S(2)}) collective-permute-start(bf16[1024,256]{1,0:T(8,128)(2,1)S(1)} %bitcast.62), channel_id=1, source_target_pairs={{0,32},{32,0},{1,33},{33,1},{2,34},{34,2},{3,35},{35,3},{4,36},{36... | collective-permute-start | bytes 1572872 | tf_op jit(solution)/shard_map/ppermute | solution.py:347
  92.0 11.5 %collective-permute-start.11 = (bf16[34,1,256]{2,1,0:T(2,128)(2,1)S(1)}, bf16[34,1,256]{2,1,0:T(2,128)(2,1)S(1)}, u32[]{:S(2)}, u32[]{:S(2)}) collective-permute-start(bf16[34,1,256]{2,1,0:T(2,128)(2,1)S(1)} %get-tuple-element.45), channel_id=1, source_target_pairs={{1,0},{2,1},{3,2},{4,3},{5,4},{6,5},{7,6},{8,7},{9,8},{10,9},{11,1... | collective-permute-start | bytes 52232 | tf_op jit(solution)/shard_map/ppermute | solution.py:30
  93.3 10.2 %collective-permute-start.10 = (bf16[34,1,256]{2,1,0:T(2,128)(2,1)S(1)}, bf16[34,1,256]{2,1,0:T(2,128)(2,1)S(1)}, u32[]{:S(2)}, u32[]{:S(2)}) collective-permute-start(bf16[34,1,256]{2,1,0:T(2,128)(2,1)S(1)} %get-tuple-element.46), channel_id=1, source_target_pairs={{0,1},{1,2},{2,3},{3,4},{4,5},{5,6},{6,7},{7,8},{8,9},{9,10},{10,1... | collective-permute-start | bytes 52232 | tf_op jit(solution)/shard_map/ppermute | solution.py:30
  103.5 3.5 %copy-start.12 = (bf16[1024,256]{1,0:T(8,128)(2,1)}, bf16[1024,256]{1,0:T(8,128)(2,1)S(1)}, u32[]{:S(2)}) copy-start(bf16[1024,256]{1,0:T(8,128)(2,1)S(1)} %collective-permute-done.12.other_cot) | copy-start | bytes 1572868
  104.1 2.9 %copy-start.5 = (bf16[34,40,256]{2,1,0:T(8,128)(2,1)}, bf16[34,40,256]{2,1,0:T(8,128)(2,1)S(1)}, u32[]{:S(2)}) copy-start(bf16[34,40,256]{2,1,0:T(8,128)(2,1)S(1)} %maximum_maximum_fusion.hidden_ref.own_hidden) | copy-start | bytes 2088964
  104.1 2.8 %collective-permute-start.13 = (bf16[34,40,256]{2,1,0:T(8,128)(2,1)S(1)}, bf16[34,40,256]{2,1,0:T(8,128)(2,1)S(1)}, u32[]{:S(2)}, u32[]{:S(2)}) collective-permute-start(bf16[34,40,256]{2,1,0:T(8,128)(2,1)S(1)} %maximum_maximum_fusion.hidden_ref.own_hidden), channel_id=1, source_target_pairs={{0,32},{32,0},{1,33},{33,1},{2,34},{34,2},{3,35},{35,3},{4,36},{36... | collective-permute-start | bytes 2088968 | tf_op jit(solution)/shard_map/ppermute | solution.py:347
  107.0 0.9 copy-start.11
  233.1 7.4 %copy-start.1 = (bf16[64,216,128]{2,1,0:T(8,128)(2,1)}, bf16[64,216,128]{2,1,0:T(8,128)(2,1)S(1)}, u32[]{:S(2)}) copy-start(bf16[64,216,128]{2,1,0:T(8,128)(2,1)S(1)} %all_to_all.11) | copy-start | bytes 10616836
  233.1 12.4 %collective-permute-start.14 = (bf16[3,2,2304,128]{3,2,1,0:T(8,128)(2,1)S(1)}, bf16[3,2,2304,128]{3,2,1,0:T(8,128)(2,1)}, u32[]{:S(2)}, u32[]{:S(2)}) collective-permute-start(bf16[3,2,2304,128]{3,2,1,0:T(8,128)(2,1)S(1)} %bitcast.58), channel_id=1, source_target_pairs={{0,32},{32,0},{1,33},{33,1},{2,34},{34,2},{3,35},{35,3},{4,36},{36... | collective-permute-start | bytes 10616840 | tf_op jit(solution)/shard_map/ppermute | solution.py:347

commit v5 on v4

--- a/solution.py
+++ b/solution.py
@@ -282,9 +282,7 @@
     ext = tile + 2
     core = lax.axis_index("core").astype(jnp.int32).reshape(1)
     valid = validity.astype(BF16)[..., None]
-    masked12 = history[1:3] * valid[1:3]
-    masked12, valid = lax.optimization_barrier((masked12, valid))
-    masked = [history[0] * valid[0], masked12[0], masked12[1], history[3] * valid[3]]
+    masked = [history[k] * valid[k] for k in range(frames)]
 
     row_last = lax.axis_index(ROW) == lax.axis_size(ROW) - 1
     col_last = lax.axis_index(COL) == lax.axis_size(COL) - 1
@@ -293,35 +291,39 @@
     col_inside = (jnp.arange(ext_cols) < ext_cols - 1) | ~col_last
     inside = (row_inside[:, None] & col_inside[None, :]).astype(BF16)[..., None]
 
-    left12 = moved(masked12, COL, 1)
     packed = moved(
-        jnp.concatenate([masked[3][1:], masked[0][-3:], current[-1:], cotangent[-1:]], axis=0), ROW, 1
-    )
+        jnp.concatenate(
+            [masked[3][1:], masked[2][1:], masked[0][-3:], current[-1:], cotangent[-1:]], axis=0
+        ),
+        ROW,
+        1,
+    )
+    left1 = moved(masked[1], COL, 1)
     below = moved(jnp.concatenate([current[:1], cotangent[:1]], axis=0), ROW, -1)
-    above3, above0 = packed[: tile - 1], packed[tile - 1 : tile + 2]
+    above3, above2, rest = packed[: tile - 1], packed[tile - 1 : 2 * tile - 2], packed[2 * tile - 2 :]
+
+    def rows_of(above, window, k):
+        both = jnp.concatenate([above, window], axis=0)
+        start = (tile - 2 - offsets[k, 0], jnp.int32(0), jnp.int32(0))
+        return lax.dynamic_slice(both, start, (ext,) + window.shape[1:])
+
+    def cols_of(left, window, k):
+        both = jnp.concatenate([left, window], axis=1)
+        start = (jnp.int32(0), cols - 1 - offsets[k, 1], jnp.int32(0))
+        return lax.dynamic_slice(both, start, (window.shape[0], ext_cols, width))
+
     near3 = jnp.concatenate([above3, masked[3][:3]], axis=0)
-    near0 = jnp.concatenate([above0, masked[0][: tile - 1]], axis=0)
-    now = jnp.concatenate([packed[tile + 2 : tile + 3], current, below[:1]], axis=0)
-    cot = jnp.concatenate([packed[tile + 3 :], cotangent, below[1:]], axis=0)
-    side = moved(
-        jnp.concatenate([near3, near0[:, -3:], now[:, -1:], cot[:, -1:]], axis=1), COL, 1
-    )
+    near2 = rows_of(above2, masked[2], 2)
+    near0 = jnp.concatenate([rest[:3], masked[0][: tile - 1]], axis=0)
+    now = jnp.concatenate([rest[3:4], current, below[:1]], axis=0)
+    cot = jnp.concatenate([rest[4:], cotangent, below[1:]], axis=0)
+    rims = jnp.concatenate([near0[:, -3:], now[:, -1:], cot[:, -1:]], axis=1)
+    side = moved(jnp.concatenate([near3, near2, rims], axis=1), COL, 1)
+    left3, left2, rims = side[:, :cols], side[:, cols : 2 * cols], side[:, 2 * cols :]
     right = moved(jnp.concatenate([now[:, :1], cot[:, :1]], axis=1), COL, -1)
-
-    left12, right = lax.optimization_barrier((left12, right))
-
-    def cols_of(k):
-        wide = jnp.concatenate([left12[k - 1], masked[k]], axis=1)
-        start = cols - 1 - offsets[k, 1]
-        return lax.dynamic_slice(wide, (jnp.int32(0), start, jnp.int32(0)), (tile, ext_cols, width))
-
-    wide1, wide2 = cols_of(1), cols_of(2)
-    above12 = moved(jnp.concatenate([wide1[1:], wide2[1:]], axis=0), ROW, 1)
-
-    def rows_of(above, wide, k):
-        both = jnp.concatenate([above, wide], axis=0)
-        start = tile - 2 - offsets[k, 0]
-        return lax.dynamic_slice(both, (start, jnp.int32(0), jnp.int32(0)), (ext, ext_cols, width)) * inside
+    left1, right = lax.optimization_barrier((left1, right))
+    wide1 = cols_of(left1, masked[1], 1)
+    above1 = moved(wide1[1:], ROW, 1)
 
     blank = jnp.zeros((ext, -ext_cols % 8, width), BF16)
 
@@ -330,12 +332,12 @@
 
     joined = jnp.stack(
         [
-            filled(side[:, cols + 4 :], cot, right[:, 1:]),
-            filled(side[:, cols + 3 : cols + 4], now, right[:, :1]),
-            filled(jnp.concatenate([side[:, cols : cols + 3], near0[:, : cols - 1]], axis=1) * inside),
-            filled(rows_of(above12[: tile - 1], wide1, 1)),
-            filled(rows_of(above12[tile - 1 :], wide2, 2)),
-            filled(jnp.concatenate([side[:, 1:cols], near3[:, :3]], axis=1) * inside),
+            filled(rims[:, 4:], cot, right[:, 1:]),
+            filled(rims[:, 3:4], now, right[:, :1]),
+            filled(jnp.concatenate([rims[:, :3], near0[:, : cols - 1]], axis=1) * inside),
+            filled(rows_of(above1, wide1, 1) * inside),
+            filled(cols_of(left2, near2, 2) * inside),
+            filled(jnp.concatenate([left3[:, 1:], near3[:, :3]], axis=1) * inside),
         ]
     )
     hidden, back_pre = forward(

time: 256 us -> 259 us (1.012)
  local copies, waits for them, and re-layouts: 14.9 us -> 24.3 us
  waiting for transfers between devices: 18.7 us -> 13 us
    concatenate x1 -> x2, local copies, waits for them, and re-layouts: 0.25 us -> 6.97 us  [the longest x1 6.36 us: shards(): side = moved(jnp.concatenate([near3, near2, rims], axis=1), COL, 1)]
    ppermute x10, waiting for transfers between devices: 17 us -> 11.2 us  [moved(): lax.ppermute(x, axis, [(i, i + by) for i in range(peers) if 0 <= i + by <...]
    slice x16 -> x12, local copies, waits for them, and re-layouts: 4.99 us -> 8.1 us  [the longest x1 1.38 us: shards(): left3[:, 1:]]
    ppermute x10, starting transfers between devices: 35 us -> 37.6 us  [moved(): lax.ppermute(x, axis, [(i, i + by) for i in range(peers) if 0 <= i + by <...]
    unnamed x33 -> x27, local copies, waits for them, and re-layouts: 4.26 us -> 6.66 us
  transfers between devices with their start and end apart: 15 -> 15, of which waited for: 4 -> 5; matrix products, arithmetic and copies ran while one was open for 6% -> 6% of each run, Pallas kernels for 12% -> 12%
where the time goes in v5:
time: 259 us; the launch traced here: 258 us
  blocking collectives  115 us (44%)
  Pallas kernels  43.1 us (17%)
  starting transfers between devices  42.4 us (16%)
  local copies, waits for them, and re-layouts  24.3 us (9%)
  other arithmetic  14.2 us (5%)
  waiting for transfers between devices  13 us (5%)
  between operations  5.89 us (2%)
    all_to_all x1, blocking collectives, shards(): got = lax.all_to_all(blocks, CHIPS, split_axis=0, concat_axis=0)  65.1 us
    all_to_all x1, blocking collectives, shards(): lax.all_to_all(spread, CHIPS, split_axis=0, concat_axis=0)  49.6 us
    ppermute x10, starting transfers between devices, moved(): lax.ppermute(x, axis, [(i, i + by) for i in range(peers) if 0 <= i + by <...  37.6 us
    pallas_call x3, Pallas kernels, layer_gradient(): pl.pallas_call(third_kernel if hidden else layer_kernel, grid_spec=pltpu....  16.8 us
    pallas_call x1, Pallas kernels, forward(): pl.pallas_call(forward_kernel, grid=(layers + 1,), in_specs=[pl.BlockSpec...  12.1 us
    ppermute x10, waiting for transfers between devices, moved(): lax.ppermute(x, axis, [(i, i + by) for i in range(peers) if 0 <= i + by <...  11.2 us
    pallas_call x2, Pallas kernels, final(): pl.pallas_call(final_kernel, grid_spec=pltpu.PrefetchScalarGridSpec(num_s...  10.3 us
    unnamed x27, local copies, waits for them, and re-layouts  6.66 us
  transfers between devices with their start and end apart: 15, of which 5 were waited for; matrix products, arithmetic and copies ran while one was open for 6% of the time, Pallas kernels for 12%

profile of v5, /device:TPU:1, one launch (start us, length us, event | category | flops | bytes accessed | tf_op | source)
XLA Modules:
  0.0 257.5 jit_solution(5440175953701676474)
XLA Ops:
  0.6 0.8 convert_element_type.16
  1.5 2.6 %bitcast_multiply_fusion.1 = (bf16[32,32,256]{2,1,0:T(8,128)(2,1)S(1)}, bf16[32,32,256]{2,1,0:T(8,128)(2,1)S(1)}, bf16[32,32,256]{2,1,0:T(8,128)(2,1)S(1)}, bf16[32,32,256]{2,1,0:T(8,128)(2,1)}) fusion(bf16[4,32,32,256]{3,2,1,0:T(8,128)(2,1)} %param.8, bf16[32,32]{1,0:T(8,128)(2,1)S(1)} %get-tuple-element.51, bf16[32,32]{1,0:T(8,128)(2,1)S(1)} %get-tuple-element.53, ...), kind=kLoop, calls=%fused_computation.32 | loop fusion | flops 1048576 | bytes 4202496 | tf_op jit(solution)/shard_map/mul | solution.py:285
  4.1 0.8 slice_dynamic-update-slice_fusion.1
  4.9 0.8 slice_dynamic-update-slice_fusion
  5.7 0.6 slice_dynamic-update-slice_fusion.2
  6.3 0.6 constant_dynamic-update-slice_fusion.1
  6.9 0.6 constant_dynamic-update-slice_fusion
  7.6 6.0 %collective-permute-start = (bf16[67,32,256]{2,1,0:T(8,128)(2,1)}, bf16[67,32,256]{2,1,0:T(8,128)(2,1)}, u32[]{:S(2)}, u32[]{:S(2)}) collective-permute-start(bf16[67,32,256]{2,1,0:T(8,128)(2,1)} %get-tuple-element.43), channel_id=1, source_target_pairs={{0,32},{32,64},{64,96},{1,33},{33,65},{65,97},{2,34},{34,66},{66,9... | collective-permute-start | bytes 3293192 | tf_op jit(solution)/shard_map/ppermute | solution.py:30
  13.6 4.0 %collective-permute-start.3 = (bf16[32,32,256]{2,1,0:T(8,128)(2,1)}, bf16[32,32,256]{2,1,0:T(8,128)(2,1)}, u32[]{:S(2)}, u32[]{:S(2)}) collective-permute-start(bf16[32,32,256]{2,1,0:T(8,128)(2,1)} %get-tuple-element.30), channel_id=1, source_target_pairs={{0,1},{1,2},{2,3},{3,4},{4,5},{5,6},{6,7},{7,8},{8,9},{9,10},{10,1... | collective-permute-start | bytes 1572872 | tf_op jit(solution)/shard_map/ppermute | solution.py:30
  17.6 1.9 collective-permute-start.1
  19.6 0.6 fusion.23
  21.6 2.8 %collective-permute-done.1 = bf16[2,32,256]{2,1,0:T(8,128)(2,1)S(1)} collective-permute-done((bf16[2,32,256]{2,1,0:T(8,128)(2,1)S(1)}, bf16[2,32,256]{2,1,0:T(8,128)(2,1)S(1)}, u32[]{:S(2)}, u32[]{:S(2)}) %collective-permute-start.1) | collective-permute-done | bytes 32800 | tf_op jit(solution)/shard_map/ppermute | solution.py:30
  24.4 1.8 collective-permute-done
  26.2 1.3 fusion.19
  27.4 0.2 fusion.9
  27.7 0.9 pad_maximum_fusion
  28.5 0.8 slice.237
  29.4 0.7 fusion.20
  30.1 0.1 pad_maximum_fusion.8
  30.2 6.4 %concatenate.81 = bf16[34,69,256]{2,1,0:T(8,128)(2,1)} concatenate(bf16[34,32,256]{2,1,0:T(8,128)(2,1)} %pad_maximum_fusion, bf16[34,32,256]{2,1,0:T(8,128)(2,1)S(1)} %fusion.9, bf16[34,3,256]{2,1,0:T(4,128)(2,1)S(1)} %pad_maximum_fusion.2, bf16[34,1,256]{2,1,0:T(2,128)(2,1)S(1)} %get-tuple-element.64, bf16[34,1,256]{2,1,0:T(2,128)(2,1)S(1)} %get-tuple-element.63), dimensions={1} | concatenate | bytes 2402304 | tf_op jit(solution)/shard_map/concatenate | solution.py:321
  36.6 4.3 %collective-permute-start.2 = (bf16[34,69,256]{2,1,0:T(8,128)(2,1)}, bf16[34,69,256]{2,1,0:T(8,128)(2,1)}, u32[]{:S(2)}, u32[]{:S(2)}) collective-permute-start(bf16[34,69,256]{2,1,0:T(8,128)(2,1)} %concatenate.81), channel_id=1, source_target_pairs={{0,1},{1,2},{2,3},{3,4},{4,5},{5,6},{6,7},{7,8},{8,9},{9,10},{10,1... | collective-permute-start | bytes 3603464 | tf_op jit(solution)/shard_map/ppermute | solution.py:30
  40.9 1.3 collective-permute-start.4
  45.8 0.1 pad.36.clone
  45.9 1.6 fusion.8
  47.5 0.1 copy.13
  47.7 7.0 %collective-permute-start.5 = (bf16[31,34,256]{2,0,1:T(8,128)(2,1)S(1)}, bf16[31,34,256]{2,0,1:T(8,128)(2,1)S(1)}, u32[]{:S(2)}, u32[]{:S(2)}) collective-permute-start(bf16[31,34,256]{2,0,1:T(8,128)(2,1)S(1)} %copy.13), channel_id=1, source_target_pairs={{0,32},{32,64},{64,96},{1,33},{33,65},{65,97},{2,34},{34,66},{66,9... | collective-permute-start | bytes 1618952 | tf_op jit(solution)/shard_map/ppermute | solution.py:30
  54.8 6.3 %collective-permute-done.5 = bf16[31,34,256]{2,0,1:T(8,128)(2,1)S(1)} collective-permute-done((bf16[31,34,256]{2,0,1:T(8,128)(2,1)S(1)}, bf16[31,34,256]{2,0,1:T(8,128)(2,1)S(1)}, u32[]{:S(2)}, u32[]{:S(2)}) %collective-permute-start.5) | collective-permute-done | bytes 539680 | tf_op jit(solution)/shard_map/ppermute | solution.py:30
  61.1 0.3 copy.14
  61.4 0.3 collective-permute-done.2
  61.7 1.1 fusion.17
  62.7 0.4 fusion.6
  63.1 0.6 fusion.7
  63.7 0.9 slice.246
  64.6 1.1 slice.248
  65.7 1.4 slice.249
  67.1 1.8 maximum_multiply_fusion
  69.1 0.1 collective-permute-start.6
  69.2 1.9 copy-done
  71.1 12.1 %forward.1 = (bf16[1024,256]{1,0:T(8,128)(2,1)}, bf16[1024,256]{1,0:T(8,128)(2,1)}) custom-call(bf16[6,34,40,256]{3,2,1,0:T(8,128)(2,1)} %copy-done, bf16[9,1280,256]{2,1,0:T(8,128)(2,1)} %bitcast.65, bf16[9,256,256]{2,1,0:T(8,128)(2,1)} %bitcast.66), custom_call_target="tpu_custom_call" | custom-call | flops 7247757312 | bytes 25000000 | tf_op jit(solution)/shard_map/forward/pallas_call | solution.py:102
  83.2 0.7 slice_bitcast_fusion
  84.0 2.4 collective-permute-start.9
  86.4 5.3 %collective-permute-start.8 = (bf16[1,32,256]{2,1,0:T(8,128)(2,1)S(1)}, bf16[1,32,256]{2,1,0:T(8,128)(2,1)S(1)}, u32[]{:S(2)}, u32[]{:S(2)}) collective-permute-start(bf16[1,32,256]{2,1,0:T(8,128)(2,1)S(1)} %get-tuple-element.42), channel_id=1, source_target_pairs={{0,32},{32,64},{64,96},{1,33},{33,65},{65,97},{2,34},{34,66},{66,9... | collective-permute-start | bytes 49160 | tf_op jit(solution)/shard_map/ppermute | solution.py:30
  91.8 0.8 copy-done.4
  92.6 5.4 %layer_gradient.3.refs_0_ = bf16[3,2,2304,128]{3,2,1,0:T(8,128)(2,1)} custom-call(s32[1]{0:T(128)} %bitcast.core_ref, bf16[6,34,40,256]{3,2,1,0:T(8,128)(2,1)} %copy-done, bf16[6,34,40,256]{3,2,1,0:T(8,128)(2,1)} %collective-permute-done.6.other_ref, bf16[1024,256]{1,0:T(8,128)(2,1)} %get-tuple-element.17.own_right.own_back, bf16[1024,256]{1,0:T(8,128)(2,1)} %copy-done.4), custom_call_target="tpu_custom_call" | custom-call | flops 2415919104 | bytes 5000000 | tf_op jit(solution)/shard_map/layer_gradient/pallas_call | solution.py:190
  98.0 0.1 collective-permute-start.12
  98.2 1.3 collective-permute-start.11
  99.5 4.1 %collective-permute-start.10 = (bf16[34,1,256]{2,1,0:T(2,128)(2,1)S(1)}, bf16[34,1,256]{2,1,0:T(2,128)(2,1)S(1)}, u32[]{:S(2)}, u32[]{:S(2)}) collective-permute-start(bf16[34,1,256]{2,1,0:T(2,128)(2,1)S(1)} %get-tuple-element.40), channel_id=1, source_target_pairs={{0,1},{1,2},{2,3},{3,4},{4,5},{5,6},{6,7},{7,8},{8,9},{9,10},{10,1... | collective-permute-start | bytes 52232 | tf_op jit(solution)/shard_map/ppermute | solution.py:30
  103.6 5.3 %layer_gradient.4.into_ref = bf16[3,2,2304,128]{3,2,1,0:T(8,128)(2,1)} custom-call(s32[1]{0:T(128)} %bitcast.core_ref, bf16[6,34,40,256]{3,2,1,0:T(8,128)(2,1)} %copy-done, bf16[6,34,40,256]{3,2,1,0:T(8,128)(2,1)} %collective-permute-done.6.other_ref, bf16[1024,256]{1,0:T(8,128)(2,1)} %get-tuple-element.17.own_right.own_back, ...), custom_call_target="tpu_custom_call", output_to_operand_aliasing={{}: (5, {})} | custom-call | flops 2415919104 | bytes 5000000 | tf_op jit(solution)/shard_map/layer_gradient/pallas_call | solution.py:190
  108.9 0.6 maximum_maximum_fusion.hidden_ref.own_hidden
  109.5 1.0 collective-permute-start.13
  110.5 1.8 collective-permute-done.13.other_hidden
  112.3 0.9 copy-done.7
  113.2 6.1 %layer_gradient.5 = bf16[3,2,2304,128]{3,2,1,0:T(8,128)(2,1)} custom-call(s32[1]{0:T(128)} %bitcast.core_ref, bf16[6,34,40,256]{3,2,1,0:T(8,128)(2,1)} %copy-done, bf16[6,34,40,256]{3,2,1,0:T(8,128)(2,1)} %collective-permute-done.6.other_ref, bf16[34,40,256]{2,1,0:T(8,128)(2,1)} %copy-done.5, ...), custom_call_target="tpu_custom_call", output_to_operand_aliasing={{}: (9, {})} | custom-call | flops 2415919104 | bytes 5000000 | tf_op jit(solution)/shard_map/layer_gradient/pallas_call | solution.py:190
  119.3 65.1 %all_to_all.10 = bf16[64,216,128]{2,1,0:T(8,128)(2,1)S(1)} all-to-all(bf16[64,216,128]{2,1,0:T(8,128)(2,1)} %bitcast.54), channel_id=1, replica_groups=mesh['xh'=2,'core'=2,'xl'=2,'z'=4,'y'=4] {'xh','xl','z','y'}, dimensions={0} | all-to-all | bytes 7077888 | tf_op jit(solution)/shard_map/all_to_all | solution.py:379
  184.4 1.1 reduce_sum.12
  185.5 1.3 broadcast_in_dim.5
  186.8 49.6 %all_to_all.11 = bf16[64,216,128]{2,1,0:T(8,128)(2,1)S(1)} all-to-all(bf16[64,216,128]{2,1,0:T(8,128)(2,1)S(1)} %broadcast_in_dim.5), channel_id=1, replica_groups=mesh['xh'=2,'core'=2,'xl'=2,'z'=4,'y'=4] {'xh','xl','z','y'}, dimensions={0} | all-to-all | bytes 7077888 | tf_op jit(solution)/shard_map/all_to_all | solution.py:382
  236.4 3.6 %collective-permute-start.14 = (bf16[3,2,2304,128]{3,2,1,0:T(8,128)(2,1)S(1)}, bf16[3,2,2304,128]{3,2,1,0:T(8,128)(2,1)}, u32[]{:S(2)}, u32[]{:S(2)}) collective-permute-start(bf16[3,2,2304,128]{3,2,1,0:T(8,128)(2,1)S(1)} %bitcast.56), channel_id=1, source_target_pairs={{0,32},{32,0},{1,33},{33,1},{2,34},{34,2},{3,35},{35,3},{4,36},{36... | collective-permute-start | bytes 10616840 | tf_op jit(solution)/shard_map/ppermute | solution.py:349
  240.0 3.8 %merged_step.1 = bf16[32,32,256]{2,1,0:T(8,128)(2,1)} custom-call(bf16[34,40,256]{2,1,0:T(8,128)(2,1)} %copy-done.5, bf16[32,32,256]{2,1,0:T(8,128)(2,1)} %current_ref.1, bf16[9,256,256]{2,1,0:T(8,128)(2,1)} %bitcast.67), custom_call_target="tpu_custom_call" | custom-call | flops 1207959552 | bytes 4000000 | tf_op jit(solution)/shard_map/merged_step/pallas_call | solution.py:230
  243.8 5.0 %final.2.refs_0_ = f32[9,1280,256]{2,1,0:T(8,128)} custom-call(s32[1]{0:T(128)S(6)} %mul.102.base_ref, bf16[3,2,2304,128]{3,2,1,0:T(8,128)(2,1)} %bitcast.57), custom_call_target="tpu_custom_call" | custom-call | bytes 12000000 | tf_op jit(solution)/shard_map/final/pallas_call | solution.py:260
  248.9 1.8 slice_select_fusion
  250.6 0.1 fusion.18
  250.7 1.6 maximum_convert_fusion
  252.3 5.2 %final.3 = f32[9,1280,256]{2,1,0:T(8,128)} custom-call(s32[1]{0:T(128)S(6)} %mul.101.base_ref, bf16[3,2,2304,128]{3,2,1,0:T(8,128)(2,1)} %collective-permute-done.14.sums_ref, f32[9,1280,256]{2,1,0:T(8,128)} %final.2.refs_0_), custom_call_target="tpu_custom_call", output_to_operand_aliasing={{}: (2, {})} | custom-call | bytes 12000000 | tf_op jit(solution)/shard_map/final/pallas_call | solution.py:260
  (46 shorter events, 0.7 us)
Async XLA Ops:
  4.1 2.3 copy-start.3
  4.1 2.9 %copy-start.2 = (bf16[32,32,256]{2,1,0:T(8,128)(2,1)S(1)}, bf16[32,32,256]{2,1,0:T(8,128)(2,1)}, u32[]{:S(2)}) copy-start(bf16[32,32,256]{2,1,0:T(8,128)(2,1)} %param.13) | copy-start | bytes 1572868
  4.1 15.5 %copy-start.9 = (s32[4,2]{0,1:T(2,128)S(1)}, s32[4,2]{0,1:T(2,128)}, u32[]{:S(2)}) copy-start(s32[4,2]{0,1:T(2,128)} %param.10) | copy-start | bytes 100
  7.6 18.6 %collective-permute-start = (bf16[67,32,256]{2,1,0:T(8,128)(2,1)}, bf16[67,32,256]{2,1,0:T(8,128)(2,1)}, u32[]{:S(2)}, u32[]{:S(2)}) collective-permute-start(bf16[67,32,256]{2,1,0:T(8,128)(2,1)} %get-tuple-element.43), channel_id=1, source_target_pairs={{0,32},{32,64},{64,96},{1,33},{33,65},{65,97},{2,34},{34,66},{66,9... | collective-permute-start | bytes 3293192 | tf_op jit(solution)/shard_map/ppermute | solution.py:30
  13.6 32.3 %collective-permute-start.3 = (bf16[32,32,256]{2,1,0:T(8,128)(2,1)}, bf16[32,32,256]{2,1,0:T(8,128)(2,1)}, u32[]{:S(2)}, u32[]{:S(2)}) collective-permute-start(bf16[32,32,256]{2,1,0:T(8,128)(2,1)} %get-tuple-element.30), channel_id=1, source_target_pairs={{0,1},{1,2},{2,3},{3,4},{4,5},{5,6},{6,7},{7,8},{8,9},{9,10},{10,1... | collective-permute-start | bytes 1572872 | tf_op jit(solution)/shard_map/ppermute | solution.py:30
  17.6 6.7 %collective-permute-start.1 = (bf16[2,32,256]{2,1,0:T(8,128)(2,1)S(1)}, bf16[2,32,256]{2,1,0:T(8,128)(2,1)S(1)}, u32[]{:S(2)}, u32[]{:S(2)}) collective-permute-start(bf16[2,32,256]{2,1,0:T(8,128)(2,1)S(1)} %pad_maximum_fusion.10), channel_id=1, source_target_pairs={{32,0},{64,32},{96,64},{33,1},{65,33},{97,65},{34,2},{66,34},{98,6... | collective-permute-start | bytes 98312 | tf_op jit(solution)/shard_map/ppermute | solution.py:30
  36.6 25.1 %collective-permute-start.2 = (bf16[34,69,256]{2,1,0:T(8,128)(2,1)}, bf16[34,69,256]{2,1,0:T(8,128)(2,1)}, u32[]{:S(2)}, u32[]{:S(2)}) collective-permute-start(bf16[34,69,256]{2,1,0:T(8,128)(2,1)} %concatenate.81), channel_id=1, source_target_pairs={{0,1},{1,2},{2,3},{3,4},{4,5},{5,6},{6,7},{7,8},{8,9},{9,10},{10,1... | collective-permute-start | bytes 3603464 | tf_op jit(solution)/shard_map/ppermute | solution.py:30
  40.9 5.0 %collective-permute-start.4 = (bf16[34,2,256]{2,1,0:T(2,128)(2,1)S(1)}, bf16[34,2,256]{2,1,0:T(2,128)(2,1)S(1)}, u32[]{:S(2)}, u32[]{:S(2)}) collective-permute-start(bf16[34,2,256]{2,1,0:T(2,128)(2,1)S(1)} %fusion.16), channel_id=1, source_target_pairs={{1,0},{2,1},{3,2},{4,3},{5,4},{6,5},{7,6},{8,7},{9,8},{10,9},{11,1... | collective-permute-start | bytes 104456 | tf_op jit(solution)/shard_map/ppermute | solution.py:30
  47.7 13.4 %collective-permute-start.5 = (bf16[31,34,256]{2,0,1:T(8,128)(2,1)S(1)}, bf16[31,34,256]{2,0,1:T(8,128)(2,1)S(1)}, u32[]{:S(2)}, u32[]{:S(2)}) collective-permute-start(bf16[31,34,256]{2,0,1:T(8,128)(2,1)S(1)} %copy.13), channel_id=1, source_target_pairs={{0,32},{32,64},{64,96},{1,33},{33,65},{65,97},{2,34},{34,66},{66,9... | collective-permute-start | bytes 1618952 | tf_op jit(solution)/shard_map/ppermute | solution.py:30
  69.1 2.0 copy-start
  69.1 22.7 %collective-permute-start.6 = (bf16[6,34,40,256]{3,2,1,0:T(8,128)(2,1)S(1)}, bf16[6,34,40,256]{3,2,1,0:T(8,128)(2,1)}, u32[]{:S(2)}, u32[]{:S(2)}) collective-permute-start(bf16[6,34,40,256]{3,2,1,0:T(8,128)(2,1)S(1)} %bitcast_dynamic-update-slice_fusion.joined_ref.own_ref), channel_id=1, source_target_pairs={{0,32},{32,0},{1,33},{33,1},{2,34},{34,2},{3,35},{35,3},{4,36},{36... | collective-permute-start | bytes 12533768 | tf_op jit(solution)/shard_map/ppermute | solution.py:349
  83.2 8.5 %collective-permute-start.7 = (bf16[1024,256]{1,0:T(8,128)(2,1)}, bf16[1024,256]{1,0:T(8,128)(2,1)S(1)}, u32[]{:S(2)}, u32[]{:S(2)}) collective-permute-start(bf16[1024,256]{1,0:T(8,128)(2,1)} %get-tuple-element.17.own_right.own_back), channel_id=1, source_target_pairs={{0,32},{32,0},{1,33},{33,1},{2,34},{34,2},{3,35},{35,3},{4,36},{36... | collective-permute-start | bytes 1572872 | tf_op jit(solution)/shard_map/ppermute | solution.py:349
  84.0 14.0 %collective-permute-start.9 = (bf16[1,32,256]{2,1,0:T(8,128)(2,1)S(1)}, bf16[1,32,256]{2,1,0:T(8,128)(2,1)S(1)}, u32[]{:S(2)}, u32[]{:S(2)}) collective-permute-start(bf16[1,32,256]{2,1,0:T(8,128)(2,1)S(1)} %get-tuple-element.41), channel_id=1, source_target_pairs={{32,0},{64,32},{96,64},{33,1},{65,33},{97,65},{34,2},{66,34},{98,6... | collective-permute-start | bytes 49160 | tf_op jit(solution)/shard_map/ppermute | solution.py:30
  86.4 11.6 %collective-permute-start.8 = (bf16[1,32,256]{2,1,0:T(8,128)(2,1)S(1)}, bf16[1,32,256]{2,1,0:T(8,128)(2,1)S(1)}, u32[]{:S(2)}, u32[]{:S(2)}) collective-permute-start(bf16[1,32,256]{2,1,0:T(8,128)(2,1)S(1)} %get-tuple-element.42), channel_id=1, source_target_pairs={{0,32},{32,64},{64,96},{1,33},{33,65},{65,97},{2,34},{34,66},{66,9... | collective-permute-start | bytes 49160 | tf_op jit(solution)/shard_map/ppermute | solution.py:30
  91.8 0.8 copy-start.4
  92.6 5.5 %copy-start.6 = (bf16[1024,256]{1,0:T(8,128)(2,1)S(1)}, bf16[1024,256]{1,0:T(8,128)(2,1)}, u32[]{:S(2)}) copy-start(bf16[1024,256]{1,0:T(8,128)(2,1)} %get-tuple-element.18) | copy-start | bytes 1572868
  98.0 10.9 %collective-permute-start.12 = (bf16[1024,256]{1,0:T(8,128)(2,1)S(1)}, bf16[1024,256]{1,0:T(8,128)(2,1)S(1)}, u32[]{:S(2)}, u32[]{:S(2)}) collective-permute-start(bf16[1024,256]{1,0:T(8,128)(2,1)S(1)} %bitcast.60), channel_id=1, source_target_pairs={{0,32},{32,0},{1,33},{33,1},{2,34},{34,2},{3,35},{35,3},{4,36},{36... | collective-permute-start | bytes 1572872 | tf_op jit(solution)/shard_map/ppermute | solution.py:349
  98.2 10.8 %collective-permute-start.11 = (bf16[34,1,256]{2,1,0:T(2,128)(2,1)S(1)}, bf16[34,1,256]{2,1,0:T(2,128)(2,1)S(1)}, u32[]{:S(2)}, u32[]{:S(2)}) collective-permute-start(bf16[34,1,256]{2,1,0:T(2,128)(2,1)S(1)} %get-tuple-element.39), channel_id=1, source_target_pairs={{1,0},{2,1},{3,2},{4,3},{5,4},{6,5},{7,6},{8,7},{9,8},{10,9},{11,1... | collective-permute-start | bytes 52232 | tf_op jit(solution)/shard_map/ppermute | solution.py:30
  99.5 9.5 %collective-permute-start.10 = (bf16[34,1,256]{2,1,0:T(2,128)(2,1)S(1)}, bf16[34,1,256]{2,1,0:T(2,128)(2,1)S(1)}, u32[]{:S(2)}, u32[]{:S(2)}) collective-permute-start(bf16[34,1,256]{2,1,0:T(2,128)(2,1)S(1)} %get-tuple-element.40), channel_id=1, source_target_pairs={{0,1},{1,2},{2,3},{3,4},{4,5},{5,6},{6,7},{7,8},{8,9},{9,10},{10,1... | collective-permute-start | bytes 52232 | tf_op jit(solution)/shard_map/ppermute | solution.py:30
  108.9 3.4 %copy-start.8 = (bf16[1024,256]{1,0:T(8,128)(2,1)}, bf16[1024,256]{1,0:T(8,128)(2,1)S(1)}, u32[]{:S(2)}) copy-start(bf16[1024,256]{1,0:T(8,128)(2,1)S(1)} %collective-permute-done.12.other_cot) | copy-start | bytes 1572868
  109.5 2.8 %copy-start.5 = (bf16[34,40,256]{2,1,0:T(8,128)(2,1)}, bf16[34,40,256]{2,1,0:T(8,128)(2,1)S(1)}, u32[]{:S(2)}) copy-start(bf16[34,40,256]{2,1,0:T(8,128)(2,1)S(1)} %maximum_maximum_fusion.hidden_ref.own_hidden) | copy-start | bytes 2088964
  109.5 2.8 %collective-permute-start.13 = (bf16[34,40,256]{2,1,0:T(8,128)(2,1)S(1)}, bf16[34,40,256]{2,1,0:T(8,128)(2,1)S(1)}, u32[]{:S(2)}, u32[]{:S(2)}) collective-permute-start(bf16[34,40,256]{2,1,0:T(8,128)(2,1)S(1)} %maximum_maximum_fusion.hidden_ref.own_hidden), channel_id=1, source_target_pairs={{0,32},{32,0},{1,33},{33,1},{2,34},{34,2},{3,35},{35,3},{4,36},{36... | collective-permute-start | bytes 2088968 | tf_op jit(solution)/shard_map/ppermute | solution.py:349
  112.3 0.9 copy-start.7
  236.4 7.4 %copy-start.1 = (bf16[64,216,128]{2,1,0:T(8,128)(2,1)}, bf16[64,216,128]{2,1,0:T(8,128)(2,1)S(1)}, u32[]{:S(2)}) copy-start(bf16[64,216,128]{2,1,0:T(8,128)(2,1)S(1)} %all_to_all.11) | copy-start | bytes 10616836
  236.4 12.4 %collective-permute-start.14 = (bf16[3,2,2304,128]{3,2,1,0:T(8,128)(2,1)S(1)}, bf16[3,2,2304,128]{3,2,1,0:T(8,128)(2,1)}, u32[]{:S(2)}, u32[]{:S(2)}) collective-permute-start(bf16[3,2,2304,128]{3,2,1,0:T(8,128)(2,1)S(1)} %bitcast.56), channel_id=1, source_target_pairs={{0,32},{32,0},{1,33},{33,1},{2,34},{34,2},{3,35},{35,3},{4,36},{36... | collective-permute-start | bytes 10616840 | tf_op jit(solution)/shard_map/ppermute | solution.py:349

commit v6 on v4

--- a/solution.py
+++ b/solution.py
@@ -375,6 +375,7 @@
     half = width // 2
     blocks = sums.reshape(chips, -1, half)
     got = lax.all_to_all(blocks, CHIPS, split_axis=0, concat_axis=0)
+    got, merged = lax.optimization_barrier((got, merged))
     share = jnp.sum(got.astype(F32), axis=0).astype(BF16)
     spread = jnp.broadcast_to(share[None], blocks.shape)
     own = lax.all_to_all(spread, CHIPS, split_axis=0, concat_axis=0).reshape(sums.shape)

time: 256 us -> 262 us (1.023)
  blocking collectives: 117 us -> 58.4 us
  waiting for transfers between devices: 18.7 us -> 60.1 us
  starting transfers between devices: 40 us -> 63.3 us
    all_to_all x1 -> x0, blocking collectives: 67.1 us -> none  [shards(): got = lax.all_to_all(blocks, CHIPS, split_axis=0, concat_axis=0)]
    all_to_all x0 -> x1, waiting for transfers between devices: none -> 40.5 us  [shards(): got = lax.all_to_all(blocks, CHIPS, split_axis=0, concat_axis=0)]
    all_to_all x0 -> x1, starting transfers between devices: none -> 23.8 us  [shards(): got = lax.all_to_all(blocks, CHIPS, split_axis=0, concat_axis=0)]
    all_to_all x1, blocking collectives: 49.6 us -> 58.4 us  [shards(): lax.all_to_all(spread, CHIPS, split_axis=0, concat_axis=0)]
  transfers between devices with their start and end apart: 15 -> 16, of which waited for: 4 -> 6; matrix products, arithmetic and copies ran while one was open for 6% -> 6% of each run, Pallas kernels for 12% -> 12%
where the time goes in v6:
time: 262 us; the launch traced here: 260 us
  starting transfers between devices  63.3 us (24%)
  waiting for transfers between devices  60.1 us (23%)
  blocking collectives  58.4 us (22%)
  Pallas kernels  43.1 us (16%)
  local copies, waits for them, and re-layouts  14.9 us (6%)
  other arithmetic  14.7 us (6%)
  between operations  6 us (2%)
    all_to_all x1, blocking collectives, shards(): lax.all_to_all(spread, CHIPS, split_axis=0, concat_axis=0)  58.4 us
    all_to_all x1, waiting for transfers between devices, shards(): got = lax.all_to_all(blocks, CHIPS, split_axis=0, concat_axis=0)  40.5 us
    ppermute x10, starting transfers between devices, moved(): lax.ppermute(x, axis, [(i, i + by) for i in range(peers) if 0 <= i + by <...  35 us
    all_to_all x1, starting transfers between devices, shards(): got = lax.all_to_all(blocks, CHIPS, split_axis=0, concat_axis=0)  23.8 us
    ppermute x10, waiting for transfers between devices, moved(): lax.ppermute(x, axis, [(i, i + by) for i in range(peers) if 0 <= i + by <...  16.9 us
    pallas_call x3, Pallas kernels, layer_gradient(): pl.pallas_call(third_kernel if hidden else layer_kernel, grid_spec=pltpu....  16.9 us
    pallas_call x1, Pallas kernels, forward(): pl.pallas_call(forward_kernel, grid=(layers + 1,), in_specs=[pl.BlockSpec...  12.1 us
    pallas_call x2, Pallas kernels, final(): pl.pallas_call(final_kernel, grid_spec=pltpu.PrefetchScalarGridSpec(num_s...  10.3 us
  transfers between devices with their start and end apart: 16, of which 6 were waited for; matrix products, arithmetic and copies ran while one was open for 6% of the time, Pallas kernels for 12%

profile of v6, /device:TPU:1, one launch (start us, length us, event | category | flops | bytes accessed | tf_op | source)
XLA Modules:
  0.0 260.5 jit_solution(12754242872546867351)
XLA Ops:
  0.6 0.9 fusion.40
  1.6 3.3 %collective-permute-start.1 = (bf16[2,32,256]{2,1,0:T(8,128)(2,1)S(1)}, bf16[2,32,256]{2,1,0:T(8,128)(2,1)S(1)}, u32[]{:S(2)}, u32[]{:S(2)}) collective-permute-start(bf16[2,32,256]{2,1,0:T(8,128)(2,1)S(1)} %pad_maximum_fusion.9), channel_id=1, source_target_pairs={{32,0},{64,32},{96,64},{33,1},{65,33},{97,65},{34,2},{66,34},{98,6... | collective-permute-start | bytes 98312 | tf_op jit(solution)/shard_map/ppermute | solution.py:30
  4.9 0.8 convert_bitcast_fusion
  5.8 0.8 convert_element_type.16
  6.6 1.6 slice_multiply_fusion
  8.2 0.3 bitcast_multiply_fusion.1
  8.6 0.9 pad_maximum_fusion.3
  9.5 4.8 %collective-permute-start = (bf16[36,32,256]{2,1,0:T(8,128)(2,1)}, bf16[36,32,256]{2,1,0:T(8,128)(2,1)}, u32[]{:S(2)}, u32[]{:S(2)}) collective-permute-start(bf16[36,32,256]{2,1,0:T(8,128)(2,1)} %pad_maximum_fusion.3), channel_id=1, source_target_pairs={{0,32},{32,64},{64,96},{1,33},{33,65},{65,97},{2,34},{34,66},{66,9... | collective-permute-start | bytes 1769480 | tf_op jit(solution)/shard_map/ppermute | solution.py:30
  14.3 4.2 %collective-permute-start.3 = (bf16[2,32,32,256]{3,2,1,0:T(8,128)(2,1)S(1)}, bf16[2,32,32,256]{3,2,1,0:T(8,128)(2,1)}, u32[]{:S(2)}, u32[]{:S(2)}) collective-permute-start(bf16[2,32,32,256]{3,2,1,0:T(8,128)(2,1)S(1)} %slice_multiply_fusion), channel_id=1, source_target_pairs={{0,1},{1,2},{2,3},{3,4},{4,5},{5,6},{6,7},{7,8},{8,9},{9,10},{10,1... | collective-permute-start | bytes 3145736 | tf_op jit(solution)/shard_map/ppermute | solution.py:30
  18.5 1.1 slice_bitcast_fusion.2
  19.6 0.6 fusion.44
  25.1 0.8 slice.227
  26.1 0.7 fusion.39
  26.9 1.3 collective-permute-start.4
  28.2 0.8 slice.228
  29.0 1.1 slice.226
  30.1 0.2 fusion.13
  30.3 4.2 %collective-permute-start.2 = (bf16[34,37,256]{2,1,0:T(8,128)(2,1)S(1)}, bf16[34,37,256]{2,1,0:T(8,128)(2,1)S(1)}, u32[]{:S(2)}, u32[]{:S(2)}) collective-permute-start(bf16[34,37,256]{2,1,0:T(8,128)(2,1)S(1)} %fusion.13), channel_id=1, source_target_pairs={{0,1},{1,2},{2,3},{3,4},{4,5},{5,6},{6,7},{7,8},{8,9},{9,10},{10,1... | collective-permute-start | bytes 1932296 | tf_op jit(solution)/shard_map/ppermute | solution.py:30
  34.5 5.9 %collective-permute-done.3 = bf16[2,32,32,256]{3,2,1,0:T(8,128)(2,1)} collective-permute-done((bf16[2,32,32,256]{3,2,1,0:T(8,128)(2,1)S(1)}, bf16[2,32,32,256]{3,2,1,0:T(8,128)(2,1)}, u32[]{:S(2)}, u32[]{:S(2)}) %collective-permute-start.3) | collective-permute-done | bytes 1048608 | tf_op jit(solution)/shard_map/ppermute | solution.py:30
  40.5 1.3 slice_bitcast_fusion.3
  41.7 0.5 fusion.29
  42.2 0.5 fusion.28
  42.8 0.1 pad_maximum_fusion
  43.0 0.3 copy.13
  43.2 3.3 %collective-permute-start.5 = (bf16[62,34,256]{2,0,1:T(8,128)(2,1)S(1)}, bf16[62,34,256]{2,0,1:T(8,128)(2,1)S(1)}, u32[]{:S(2)}, u32[]{:S(2)}) collective-permute-start(bf16[62,34,256]{2,0,1:T(8,128)(2,1)S(1)} %copy.13), channel_id=1, source_target_pairs={{0,32},{32,64},{64,96},{1,33},{33,65},{65,97},{2,34},{34,66},{66,9... | collective-permute-start | bytes 3237896 | tf_op jit(solution)/shard_map/ppermute | solution.py:30
  46.7 7.8 %collective-permute-done.2 = bf16[34,37,256]{2,1,0:T(8,128)(2,1)S(1)} collective-permute-done((bf16[34,37,256]{2,1,0:T(8,128)(2,1)S(1)}, bf16[34,37,256]{2,1,0:T(8,128)(2,1)S(1)}, u32[]{:S(2)}, u32[]{:S(2)}) %collective-permute-start.2) | collective-permute-done | bytes 644128 | tf_op jit(solution)/shard_map/ppermute | solution.py:30
  54.6 0.3 slice.241
  54.9 0.4 fusion.26
  55.3 0.6 fusion.27
  55.9 3.1 %collective-permute-done.5 = bf16[62,34,256]{2,0,1:T(8,128)(2,1)S(1)} collective-permute-done((bf16[62,34,256]{2,0,1:T(8,128)(2,1)S(1)}, bf16[62,34,256]{2,0,1:T(8,128)(2,1)S(1)}, u32[]{:S(2)}, u32[]{:S(2)}) %collective-permute-start.5) | collective-permute-done | bytes 1079328 | tf_op jit(solution)/shard_map/ppermute | solution.py:30
  59.0 0.3 fusion.37
  59.3 0.3 copy.17
  59.6 0.3 copy.16
  59.9 2.6 %fusion.23 = (bf16[34,34,256]{2,1,0:T(8,128)(2,1)S(1)}, bf16[34,34,256]{2,1,0:T(8,128)(2,1)S(1)}, bf16[34,34,256]{2,1,0:T(8,128)(2,1)S(1)}, bf16[34,34,256]{2,1,0:T(8,128)(2,1)S(1)}) fusion(bf16[3,32,256]{2,1,0:T(8,128)(2,1)S(1)} %slice.227, bf16[31,32,256]{2,1,0:T(8,128)(2,1)S(1)} %slice.226, bf16[34,31,256]{2,1,0:T(8,128)(2,1)S(1)} %slice.241, ...), kind=kLoop, calls=%fused_computation.41 | loop fusion | flops 7398400 | bytes 6269200 | tf_op jit(solution)/shard_map/mul | solution.py:338
  62.8 0.3 collective-permute-start.6
  63.1 1.7 copy-done
  64.8 12.1 %forward.1 = (bf16[1024,256]{1,0:T(8,128)(2,1)}, bf16[1024,256]{1,0:T(8,128)(2,1)}) custom-call(bf16[6,34,40,256]{3,2,1,0:T(8,128)(2,1)} %copy-done, bf16[9,1280,256]{2,1,0:T(8,128)(2,1)} %bitcast.67, bf16[9,256,256]{2,1,0:T(8,128)(2,1)} %bitcast.68), custom_call_target="tpu_custom_call" | custom-call | flops 7247757312 | bytes 25000000 | tf_op jit(solution)/shard_map/forward/pallas_call | solution.py:102
  77.0 0.7 slice_bitcast_fusion.4
  77.7 2.4 collective-permute-start.9
  80.1 5.4 %collective-permute-start.8 = (bf16[1,32,256]{2,1,0:T(8,128)(2,1)S(1)}, bf16[1,32,256]{2,1,0:T(8,128)(2,1)S(1)}, u32[]{:S(2)}, u32[]{:S(2)}) collective-permute-start(bf16[1,32,256]{2,1,0:T(8,128)(2,1)S(1)} %get-tuple-element.52), channel_id=1, source_target_pairs={{0,32},{32,64},{64,96},{1,33},{33,65},{65,97},{2,34},{34,66},{66,9... | collective-permute-start | bytes 49160 | tf_op jit(solution)/shard_map/ppermute | solution.py:30
  85.6 0.8 copy-done.4
  86.3 5.4 %layer_gradient.3.refs_0_ = bf16[3,2,2304,128]{3,2,1,0:T(8,128)(2,1)} custom-call(s32[1]{0:T(128)} %bitcast.core_ref, bf16[6,34,40,256]{3,2,1,0:T(8,128)(2,1)} %copy-done, bf16[6,34,40,256]{3,2,1,0:T(8,128)(2,1)} %collective-permute-done.6.other_ref, bf16[1024,256]{1,0:T(8,128)(2,1)} %get-tuple-element.23.own_right.own_back, bf16[1024,256]{1,0:T(8,128)(2,1)} %copy-done.4), custom_call_target="tpu_custom_call" | custom-call | flops 2415919104 | bytes 5000000 | tf_op jit(solution)/shard_map/layer_gradient/pallas_call | solution.py:190
  91.8 0.1 collective-permute-start.12
  91.9 1.3 collective-permute-start.11
  93.2 4.9 %collective-permute-start.10 = (bf16[34,1,256]{2,1,0:T(2,128)(2,1)S(1)}, bf16[34,1,256]{2,1,0:T(2,128)(2,1)S(1)}, u32[]{:S(2)}, u32[]{:S(2)}) collective-permute-start(bf16[34,1,256]{2,1,0:T(2,128)(2,1)S(1)} %get-tuple-element.50), channel_id=1, source_target_pairs={{0,1},{1,2},{2,3},{3,4},{4,5},{5,6},{6,7},{7,8},{8,9},{9,10},{10,1... | collective-permute-start | bytes 52232 | tf_op jit(solution)/shard_map/ppermute | solution.py:30
  98.1 5.4 %layer_gradient.4.into_ref = bf16[3,2,2304,128]{3,2,1,0:T(8,128)(2,1)} custom-call(s32[1]{0:T(128)} %bitcast.core_ref, bf16[6,34,40,256]{3,2,1,0:T(8,128)(2,1)} %copy-done, bf16[6,34,40,256]{3,2,1,0:T(8,128)(2,1)} %collective-permute-done.6.other_ref, bf16[1024,256]{1,0:T(8,128)(2,1)} %get-tuple-element.23.own_right.own_back, ...), custom_call_target="tpu_custom_call", output_to_operand_aliasing={{}: (5, {})} | custom-call | flops 2415919104 | bytes 5000000 | tf_op jit(solution)/shard_map/layer_gradient/pallas_call | solution.py:190
  103.5 0.6 maximum_maximum_fusion.own_hidden.hidden_ref
  104.1 1.1 collective-permute-start.13
  105.2 1.8 collective-permute-done.13.other_hidden
  107.0 0.9 copy-done.11
  107.9 6.1 %layer_gradient.5 = bf16[3,2,2304,128]{3,2,1,0:T(8,128)(2,1)} custom-call(s32[1]{0:T(128)} %bitcast.core_ref, bf16[6,34,40,256]{3,2,1,0:T(8,128)(2,1)} %copy-done, bf16[6,34,40,256]{3,2,1,0:T(8,128)(2,1)} %collective-permute-done.6.other_ref, bf16[34,40,256]{2,1,0:T(8,128)(2,1)} %copy-done.5, ...), custom_call_target="tpu_custom_call", output_to_operand_aliasing={{}: (9, {})} | custom-call | flops 2415919104 | bytes 5000000 | tf_op jit(solution)/shard_map/layer_gradient/pallas_call | solution.py:190
  113.9 23.8 %all-to-all-start = ((bf16[64,216,128]{2,1,0:T(8,128)(2,1)}), bf16[64,216,128]{2,1,0:T(8,128)(2,1)S(1)}, u32[]{:S(2)}, u32[]{:S(2)}) async-start(bf16[64,216,128]{2,1,0:T(8,128)(2,1)} %bitcast.56), calls=%async_computation | async-start | bytes 7077888 | tf_op jit(solution)/shard_map/all_to_all | solution.py:377
  137.7 3.8 %merged_step.1 = bf16[32,32,256]{2,1,0:T(8,128)(2,1)} custom-call(bf16[34,40,256]{2,1,0:T(8,128)(2,1)} %copy-done.5, bf16[32,32,256]{2,1,0:T(8,128)(2,1)} %current_ref.1, bf16[9,256,256]{2,1,0:T(8,128)(2,1)} %bitcast.69), custom_call_target="tpu_custom_call" | custom-call | flops 1207959552 | bytes 4000000 | tf_op jit(solution)/shard_map/merged_step/pallas_call | solution.py:230
  141.5 40.5 %all-to-all-done = bf16[64,216,128]{2,1,0:T(8,128)(2,1)S(1)} async-done(((bf16[64,216,128]{2,1,0:T(8,128)(2,1)}), bf16[64,216,128]{2,1,0:T(8,128)(2,1)S(1)}, u32[]{:S(2)}, u32[]{:S(2)}) %all-to-all-start) | async-done | bytes 3538976 | tf_op jit(solution)/shard_map/all_to_all | solution.py:377
  182.0 1.1 reduce_sum.12
  183.1 1.3 broadcast_in_dim.8
  184.4 58.4 %all_to_all.10 = bf16[64,216,128]{2,1,0:T(8,128)(2,1)S(1)} all-to-all(bf16[64,216,128]{2,1,0:T(8,128)(2,1)S(1)} %broadcast_in_dim.8), channel_id=1, replica_groups=mesh['xh'=2,'core'=2,'xl'=2,'z'=4,'y'=4] {'xh','xl','z','y'}, dimensions={0} | all-to-all | bytes 7077888 | tf_op jit(solution)/shard_map/all_to_all | solution.py:381
  242.8 3.1 %collective-permute-start.14 = (bf16[3,2,2304,128]{3,2,1,0:T(8,128)(2,1)S(1)}, bf16[3,2,2304,128]{3,2,1,0:T(8,128)(2,1)}, u32[]{:S(2)}, u32[]{:S(2)}) collective-permute-start(bf16[3,2,2304,128]{3,2,1,0:T(8,128)(2,1)S(1)} %bitcast.58), channel_id=1, source_target_pairs={{0,32},{32,0},{1,33},{33,1},{2,34},{34,2},{3,35},{35,3},{4,36},{36... | collective-permute-start | bytes 10616840 | tf_op jit(solution)/shard_map/ppermute | solution.py:347
  245.9 5.0 %final.2.refs_0_ = f32[9,1280,256]{2,1,0:T(8,128)} custom-call(s32[1]{0:T(128)S(6)} %mul.86.base_ref, bf16[3,2,2304,128]{3,2,1,0:T(8,128)(2,1)} %bitcast.59), custom_call_target="tpu_custom_call" | custom-call | bytes 12000000 | tf_op jit(solution)/shard_map/final/pallas_call | solution.py:260
  250.9 0.9 collective-permute-done.14.sums_ref
  251.8 1.7 slice_select_fusion
  253.6 0.1 fusion.36
  253.7 1.6 maximum_convert_fusion
  255.2 5.2 %final.3 = f32[9,1280,256]{2,1,0:T(8,128)} custom-call(s32[1]{0:T(128)S(6)} %mul.85.base_ref, bf16[3,2,2304,128]{3,2,1,0:T(8,128)(2,1)} %collective-permute-done.14.sums_ref, f32[9,1280,256]{2,1,0:T(8,128)} %final.2.refs_0_), custom_call_target="tpu_custom_call", output_to_operand_aliasing={{}: (2, {})} | custom-call | bytes 12000000 | tf_op jit(solution)/shard_map/final/pallas_call | solution.py:260
  (58 shorter events, 0.9 us)
Async XLA Ops:
  0.6 7.6 %copy-start.8 = (bf16[4,32,32,256]{3,2,1,0:T(8,128)(2,1)S(1)}, bf16[4,32,32,256]{3,2,1,0:T(8,128)(2,1)}, u32[]{:S(2)}) copy-start(bf16[4,32,32,256]{3,2,1,0:T(8,128)(2,1)} %param.8) | copy-start | bytes 6291460
  1.6 24.5 %collective-permute-start.1 = (bf16[2,32,256]{2,1,0:T(8,128)(2,1)S(1)}, bf16[2,32,256]{2,1,0:T(8,128)(2,1)S(1)}, u32[]{:S(2)}, u32[]{:S(2)}) collective-permute-start(bf16[2,32,256]{2,1,0:T(8,128)(2,1)S(1)} %pad_maximum_fusion.9), channel_id=1, source_target_pairs={{32,0},{64,32},{96,64},{33,1},{65,33},{97,65},{34,2},{66,34},{98,6... | collective-permute-start | bytes 98312 | tf_op jit(solution)/shard_map/ppermute | solution.py:30
  8.5 11.0 %copy-start.7 = (bf16[32,32,256]{2,1,0:T(8,128)(2,1)}, bf16[32,32,256]{2,1,0:T(8,128)(2,1)S(1)}, u32[]{:S(2)}) copy-start(bf16[32,32,256]{2,1,0:T(8,128)(2,1)S(1)} %get-tuple-element.35) | copy-start | bytes 1572868
  8.6 11.0 %copy-start.13 = (s32[4,2]{0,1:T(2,128)S(1)}, s32[4,2]{0,1:T(2,128)}, u32[]{:S(2)}) copy-start(s32[4,2]{0,1:T(2,128)} %param.10) | copy-start | bytes 100
  9.5 17.3 %copy-start.2 = (bf16[32,32,256]{2,1,0:T(8,128)(2,1)S(1)}, bf16[32,32,256]{2,1,0:T(8,128)(2,1)}, u32[]{:S(2)}) copy-start(bf16[32,32,256]{2,1,0:T(8,128)(2,1)} %param.13) | copy-start | bytes 1572868
  9.5 17.3 %copy-start.3 = (bf16[32,32,256]{2,1,0:T(8,128)(2,1)S(1)}, bf16[32,32,256]{2,1,0:T(8,128)(2,1)}, u32[]{:S(2)}) copy-start(bf16[32,32,256]{2,1,0:T(8,128)(2,1)} %current_ref.1) | copy-start | bytes 1572868
  9.5 16.5 %collective-permute-start = (bf16[36,32,256]{2,1,0:T(8,128)(2,1)}, bf16[36,32,256]{2,1,0:T(8,128)(2,1)}, u32[]{:S(2)}, u32[]{:S(2)}) collective-permute-start(bf16[36,32,256]{2,1,0:T(8,128)(2,1)} %pad_maximum_fusion.3), channel_id=1, source_target_pairs={{0,32},{32,64},{64,96},{1,33},{33,65},{65,97},{2,34},{34,66},{66,9... | collective-permute-start | bytes 1769480 | tf_op jit(solution)/shard_map/ppermute | solution.py:30
  14.3 26.1 %collective-permute-start.3 = (bf16[2,32,32,256]{3,2,1,0:T(8,128)(2,1)S(1)}, bf16[2,32,32,256]{3,2,1,0:T(8,128)(2,1)}, u32[]{:S(2)}, u32[]{:S(2)}) collective-permute-start(bf16[2,32,32,256]{3,2,1,0:T(8,128)(2,1)S(1)} %slice_multiply_fusion), channel_id=1, source_target_pairs={{0,1},{1,2},{2,3},{3,4},{4,5},{5,6},{6,7},{7,8},{8,9},{9,10},{10,1... | collective-permute-start | bytes 3145736 | tf_op jit(solution)/shard_map/ppermute | solution.py:30
  26.9 7.6 %collective-permute-start.4 = (bf16[34,2,256]{2,1,0:T(2,128)(2,1)S(1)}, bf16[34,2,256]{2,1,0:T(2,128)(2,1)S(1)}, u32[]{:S(2)}, u32[]{:S(2)}) collective-permute-start(bf16[34,2,256]{2,1,0:T(2,128)(2,1)S(1)} %fusion.35), channel_id=1, source_target_pairs={{1,0},{2,1},{3,2},{4,3},{5,4},{6,5},{7,6},{8,7},{9,8},{10,9},{11,1... | collective-permute-start | bytes 104456 | tf_op jit(solution)/shard_map/ppermute | solution.py:30
  30.3 11.4 %copy-start.10 = (bf16[32,32,256]{2,1,0:T(8,128)(2,1)S(1)}, bf16[32,32,256]{2,1,0:T(8,128)(2,1)}, u32[]{:S(2)}) copy-start(bf16[32,32,256]{2,1,0:T(8,128)(2,1)} %get-tuple-element.41) | copy-start | bytes 1572868
  30.3 11.9 %copy-start.9 = (bf16[32,32,256]{2,1,0:T(8,128)(2,1)S(1)}, bf16[32,32,256]{2,1,0:T(8,128)(2,1)}, u32[]{:S(2)}) copy-start(bf16[32,32,256]{2,1,0:T(8,128)(2,1)} %get-tuple-element.42) | copy-start | bytes 1572868
  30.3 24.2 %collective-permute-start.2 = (bf16[34,37,256]{2,1,0:T(8,128)(2,1)S(1)}, bf16[34,37,256]{2,1,0:T(8,128)(2,1)S(1)}, u32[]{:S(2)}, u32[]{:S(2)}) collective-permute-start(bf16[34,37,256]{2,1,0:T(8,128)(2,1)S(1)} %fusion.13), channel_id=1, source_target_pairs={{0,1},{1,2},{2,3},{3,4},{4,5},{5,6},{6,7},{7,8},{8,9},{9,10},{10,1... | collective-permute-start | bytes 1932296 | tf_op jit(solution)/shard_map/ppermute | solution.py:30
  43.2 15.8 %collective-permute-start.5 = (bf16[62,34,256]{2,0,1:T(8,128)(2,1)S(1)}, bf16[62,34,256]{2,0,1:T(8,128)(2,1)S(1)}, u32[]{:S(2)}, u32[]{:S(2)}) collective-permute-start(bf16[62,34,256]{2,0,1:T(8,128)(2,1)S(1)} %copy.13), channel_id=1, source_target_pairs={{0,32},{32,64},{64,96},{1,33},{33,65},{65,97},{2,34},{34,66},{66,9... | collective-permute-start | bytes 3237896 | tf_op jit(solution)/shard_map/ppermute | solution.py:30
  62.8 2.0 copy-start
  62.8 22.7 %collective-permute-start.6 = (bf16[6,34,40,256]{3,2,1,0:T(8,128)(2,1)S(1)}, bf16[6,34,40,256]{3,2,1,0:T(8,128)(2,1)}, u32[]{:S(2)}, u32[]{:S(2)}) collective-permute-start(bf16[6,34,40,256]{3,2,1,0:T(8,128)(2,1)S(1)} %bitcast_dynamic-update-slice_fusion.joined_ref.own_ref), channel_id=1, source_target_pairs={{0,32},{32,0},{1,33},{33,1},{2,34},{34,2},{3,35},{35,3},{4,36},{36... | collective-permute-start | bytes 12533768 | tf_op jit(solution)/shard_map/ppermute | solution.py:347
  77.0 8.6 %collective-permute-start.7 = (bf16[1024,256]{1,0:T(8,128)(2,1)}, bf16[1024,256]{1,0:T(8,128)(2,1)S(1)}, u32[]{:S(2)}, u32[]{:S(2)}) collective-permute-start(bf16[1024,256]{1,0:T(8,128)(2,1)} %get-tuple-element.23.own_right.own_back), channel_id=1, source_target_pairs={{0,32},{32,0},{1,33},{33,1},{2,34},{34,2},{3,35},{35,3},{4,36},{36... | collective-permute-start | bytes 1572872 | tf_op jit(solution)/shard_map/ppermute | solution.py:347
  77.7 14.0 %collective-permute-start.9 = (bf16[1,32,256]{2,1,0:T(8,128)(2,1)S(1)}, bf16[1,32,256]{2,1,0:T(8,128)(2,1)S(1)}, u32[]{:S(2)}, u32[]{:S(2)}) collective-permute-start(bf16[1,32,256]{2,1,0:T(8,128)(2,1)S(1)} %get-tuple-element.51), channel_id=1, source_target_pairs={{32,0},{64,32},{96,64},{33,1},{65,33},{97,65},{34,2},{66,34},{98,6... | collective-permute-start | bytes 49160 | tf_op jit(solution)/shard_map/ppermute | solution.py:30
  80.1 11.6 %collective-permute-start.8 = (bf16[1,32,256]{2,1,0:T(8,128)(2,1)S(1)}, bf16[1,32,256]{2,1,0:T(8,128)(2,1)S(1)}, u32[]{:S(2)}, u32[]{:S(2)}) collective-permute-start(bf16[1,32,256]{2,1,0:T(8,128)(2,1)S(1)} %get-tuple-element.52), channel_id=1, source_target_pairs={{0,32},{32,64},{64,96},{1,33},{33,65},{65,97},{2,34},{34,66},{66,9... | collective-permute-start | bytes 49160 | tf_op jit(solution)/shard_map/ppermute | solution.py:30
  85.5 0.8 copy-start.4
  86.3 5.5 %copy-start.6 = (bf16[1024,256]{1,0:T(8,128)(2,1)S(1)}, bf16[1024,256]{1,0:T(8,128)(2,1)}, u32[]{:S(2)}) copy-start(bf16[1024,256]{1,0:T(8,128)(2,1)} %get-tuple-element.24) | copy-start | bytes 1572868
  91.8 11.7 %collective-permute-start.12 = (bf16[1024,256]{1,0:T(8,128)(2,1)S(1)}, bf16[1024,256]{1,0:T(8,128)(2,1)S(1)}, u32[]{:S(2)}, u32[]{:S(2)}) collective-permute-start(bf16[1024,256]{1,0:T(8,128)(2,1)S(1)} %bitcast.62), channel_id=1, source_target_pairs={{0,32},{32,0},{1,33},{33,1},{2,34},{34,2},{3,35},{35,3},{4,36},{36... | collective-permute-start | bytes 1572872 | tf_op jit(solution)/shard_map/ppermute | solution.py:347
  91.9 11.5 %collective-permute-start.11 = (bf16[34,1,256]{2,1,0:T(2,128)(2,1)S(1)}, bf16[34,1,256]{2,1,0:T(2,128)(2,1)S(1)}, u32[]{:S(2)}, u32[]{:S(2)}) collective-permute-start(bf16[34,1,256]{2,1,0:T(2,128)(2,1)S(1)} %get-tuple-element.49), channel_id=1, source_target_pairs={{1,0},{2,1},{3,2},{4,3},{5,4},{6,5},{7,6},{8,7},{9,8},{10,9},{11,1... | collective-permute-start | bytes 52232 | tf_op jit(solution)/shard_map/ppermute | solution.py:30
  93.2 10.3 %collective-permute-start.10 = (bf16[34,1,256]{2,1,0:T(2,128)(2,1)S(1)}, bf16[34,1,256]{2,1,0:T(2,128)(2,1)S(1)}, u32[]{:S(2)}, u32[]{:S(2)}) collective-permute-start(bf16[34,1,256]{2,1,0:T(2,128)(2,1)S(1)} %get-tuple-element.50), channel_id=1, source_target_pairs={{0,1},{1,2},{2,3},{3,4},{4,5},{5,6},{6,7},{7,8},{8,9},{9,10},{10,1... | collective-permute-start | bytes 52232 | tf_op jit(solution)/shard_map/ppermute | solution.py:30
  103.5 3.5 %copy-start.12 = (bf16[1024,256]{1,0:T(8,128)(2,1)}, bf16[1024,256]{1,0:T(8,128)(2,1)S(1)}, u32[]{:S(2)}) copy-start(bf16[1024,256]{1,0:T(8,128)(2,1)S(1)} %collective-permute-done.12.other_cot) | copy-start | bytes 1572868
  104.1 2.9 %copy-start.5 = (bf16[34,40,256]{2,1,0:T(8,128)(2,1)}, bf16[34,40,256]{2,1,0:T(8,128)(2,1)S(1)}, u32[]{:S(2)}) copy-start(bf16[34,40,256]{2,1,0:T(8,128)(2,1)S(1)} %maximum_maximum_fusion.own_hidden.hidden_ref) | copy-start | bytes 2088964
  104.1 2.8 %collective-permute-start.13 = (bf16[34,40,256]{2,1,0:T(8,128)(2,1)S(1)}, bf16[34,40,256]{2,1,0:T(8,128)(2,1)S(1)}, u32[]{:S(2)}, u32[]{:S(2)}) collective-permute-start(bf16[34,40,256]{2,1,0:T(8,128)(2,1)S(1)} %maximum_maximum_fusion.own_hidden.hidden_ref), channel_id=1, source_target_pairs={{0,32},{32,0},{1,33},{33,1},{2,34},{34,2},{3,35},{35,3},{4,36},{36... | collective-permute-start | bytes 2088968 | tf_op jit(solution)/shard_map/ppermute | solution.py:347
  106.9 0.9 copy-start.11
  113.9 68.1 %all-to-all-start = ((bf16[64,216,128]{2,1,0:T(8,128)(2,1)}), bf16[64,216,128]{2,1,0:T(8,128)(2,1)S(1)}, u32[]{:S(2)}, u32[]{:S(2)}) async-start(bf16[64,216,128]{2,1,0:T(8,128)(2,1)} %bitcast.56), calls=%async_computation | async-start | bytes 7077888 | tf_op jit(solution)/shard_map/all_to_all | solution.py:377
  242.8 3.1 %copy-start.1 = (bf16[64,216,128]{2,1,0:T(8,128)(2,1)}, bf16[64,216,128]{2,1,0:T(8,128)(2,1)S(1)}, u32[]{:S(2)}) copy-start(bf16[64,216,128]{2,1,0:T(8,128)(2,1)S(1)} %all_to_all.10) | copy-start | bytes 10616836
  242.8 9.1 %collective-permute-start.14 = (bf16[3,2,2304,128]{3,2,1,0:T(8,128)(2,1)S(1)}, bf16[3,2,2304,128]{3,2,1,0:T(8,128)(2,1)}, u32[]{:S(2)}, u32[]{:S(2)}) collective-permute-start(bf16[3,2,2304,128]{3,2,1,0:T(8,128)(2,1)S(1)} %bitcast.58), channel_id=1, source_target_pairs={{0,32},{32,0},{1,33},{33,1},{2,34},{34,2},{3,35},{35,3},{4,36},{36... | collective-permute-start | bytes 10616840 | tf_op jit(solution)/shard_map/ppermute | solution.py:347
